TPU v7x, 256 devices: a whole 4x4x8 slice. The times are simulated.
256 devices in a mesh: gx: 16 (over z, core), gy: 16 (over x, y).
Axes of the slice: x: 4, y: 4, z: 8, core: 2. Of those that a mesh axis runs over, the one named last changes fastest.
Arguments:
- fields: float32 [256, 6, 8100], P(('gx', 'gy')), may hold values from -6 to 6
- wet_mask: int32 [256, 8100], P(('gx', 'gy')), may hold values 0 or 1
- tile_of_slot: int32 [256], replicated, may hold values from -1 to 255, as said below
- neighbor: int32 [256, 4], replicated, may hold values from -1 to 255, as said below
- rotation: int32 [256, 4], replicated, may hold values from 0 to 3
Outputs:
- updated: float32 [256, 6, 8100], P(('gx', 'gy'))
Inputs may be any that keep to these rules, and one draw needn't show every extreme that they name: `tile_of_slot`: slot s lies on device s, devices numbered gx-major; each tile is held by at most one slot, and every tile named in neighbor is held. Rows of tiles held by no slot are -1. The relation is mutual: side (k + 2 + rotation[t][k]) mod 4 of neighbor[t][k] leads back to t with rotation (4 - rotation[t][k]) mod 4. A tile's neighbour is held on the tile's device, on a device next to it along gx or along gy (gx wrapping at its ends), or, across a pole, on the device 16 / 2 away along gx at the same gy index, for devices at the first or last gy index. For two different devices at most 1 pairs (tile of the first, side) lead to tiles of the second; in every draw some device has exactly 1 such pairs leading to it from each of the four devices next to it.
All inputs are finite; a program needn't handle non-finite values. No bound on the sum of `wet_mask` on one device may be relied on, other than what follows from the above.
Results may differ from a plain program's by a relative error of at most 0.00002.
Values sent between devices are 32-bit elements; how exact they have to be, the bound alone decides.
No kernel may reach another device: no remote copies, remote signals or barrier semaphores. Data moves between devices by JAX's collectives and lax.ppermute only.
A program may use at most 64 MiB of HBM per device.

v0:
```python
import jax
import jax.numpy as jnp
from jax import lax
from jax.sharding import PartitionSpec as P

BLOCK = 1
TILE = 90
SLOTS_DEV = 1


ADVECT = 0.25
DIFFUSE = 0.15
VISCOUS = 0.15
STEP_SIZE = 0.5
CORIOLIS = 0.3
GRAVITY = 0.8


def quarter(first_part, second_part, quarter_turns):
    if quarter_turns == 0:
        return (first_part, second_part)
    if quarter_turns == 1:
        return (second_part, -first_part)
    if quarter_turns == 2:
        return (-first_part, -second_part)
    return (-second_part, first_part)


def edge_strips(values, vector):
    segments = [values[..., 0, :], values[..., :, -1], values[..., -1, ::-1], values[..., ::-1, 0]]
    if vector:
        for facing in range(4):
            segment = segments[facing]
            first_part, second_part = quarter(segment[:, 0:2], segment[:, 2:4], facing)
            segments[facing] = jnp.concatenate([first_part, second_part, segment[:, 4:]], axis=1)
    return jnp.stack(segments, axis=1)


def place_strips(strips, vector):
    placed = []
    for facing in range(4):
        segment = strips[:, facing]
        if facing < 2:
            segment = segment[..., ::-1]
        if vector:
            first_part, second_part = quarter(segment[:, 0:2], segment[:, 2:4], (2 - facing) % 4)
            segment = jnp.concatenate([first_part, second_part, segment[:, 4:]], axis=1)
        placed.append(segment)
    return placed


def shifted(values, rims):
    south_rim, east_rim, north_rim, west_rim = rims
    upward = jnp.concatenate([values[..., 1:, :], north_rim[..., None, :]], axis=-2)
    downward = jnp.concatenate([south_rim[..., None, :], values[..., :-1, :]], axis=-2)
    rightward = jnp.concatenate([values[..., :, 1:], east_rim[..., :, None]], axis=-1)
    leftward = jnp.concatenate([west_rim[..., :, None], values[..., :, :-1]], axis=-1)
    return (rightward, leftward, upward, downward)


def tracer_step(masked, shifts, wet_real):
    rightward, leftward, upward, downward = shifts
    tracer = masked[:, 4:6]
    tracer_dx = 0.5 * (rightward[:, 4:6] - leftward[:, 4:6])
    tracer_dy = 0.5 * (upward[:, 4:6] - downward[:, 4:6])
    laplacian = (
        rightward[:, 4:6] + leftward[:, 4:6] + upward[:, 4:6] + downward[:, 4:6] - 4.0 * tracer
    )
    advection = masked[:, 0:2] * tracer_dx + masked[:, 2:4] * tracer_dy
    return wet_real[:, None] * (tracer - ADVECT * advection + DIFFUSE * laplacian)


def momentum_step(masked, shifts, pressure_shifts, wet_real):
    rightward, leftward, upward, downward = shifts
    press_right, press_left, press_up, press_down = pressure_shifts
    velocity_first = masked[:, 0:2]
    velocity_second = masked[:, 2:4]

    def advance(current, start_ch, stop_ch, turning, gradient):
        along_first = 0.5 * (rightward[:, start_ch:stop_ch] - leftward[:, start_ch:stop_ch])
        along_second = 0.5 * (upward[:, start_ch:stop_ch] - downward[:, start_ch:stop_ch])
        laplacian = (
            rightward[:, start_ch:stop_ch]
            + leftward[:, start_ch:stop_ch]
            + upward[:, start_ch:stop_ch]
            + downward[:, start_ch:stop_ch]
            - 4.0 * current
        )
        change = (
            STEP_SIZE * (turning - gradient)
            - ADVECT * (velocity_first * along_first + velocity_second * along_second)
            + VISCOUS * laplacian
        )
        return wet_real[:, None] * (current + change)

    first_new = advance(
        velocity_first, 0, 2, CORIOLIS * velocity_second, 0.5 * (press_right - press_left)
    )
    second_new = advance(
        velocity_second, 2, 4, -CORIOLIS * velocity_first, 0.5 * (press_up - press_down)
    )
    return (first_new, second_new)


def sources(tile_of_slot, neighbor, rotation):
    slot_count = tile_of_slot.shape[0]
    tile_count = neighbor.shape[0]
    target = jnp.where(tile_of_slot >= 0, tile_of_slot, tile_count)
    slot_of_tile = (
        jnp.full((tile_count,), -1, jnp.int32)
        .at[target]
        .set(jnp.arange(slot_count, dtype=jnp.int32), mode="drop")
    )
    held_tile = jnp.clip(tile_of_slot, 0, tile_count - 1)
    near_tile = jnp.where(tile_of_slot[:, None] >= 0, neighbor[held_tile], -1)
    facing_side = (jnp.arange(4, dtype=jnp.int32)[None, :] + 2 + rotation[held_tile]) % 4
    near_slot = jnp.where(near_tile >= 0, slot_of_tile[jnp.clip(near_tile, 0, tile_count - 1)], -1)
    return jnp.where(near_slot >= 0, near_slot * 4 + facing_side, -1)


def deliver(outgoing, out_index, in_index, first_pass, count_x, count_y):
    payload = outgoing.shape[-1]
    buckets = (
        jnp.zeros((count_x * count_y * BLOCK, payload), jnp.float32)
        .at[out_index]
        .set(outgoing, mode="drop")
    )
    buckets = buckets.reshape(count_x, count_y, BLOCK, payload)
    if first_pass:
        arrived = lax.all_to_all(
            lax.all_to_all(buckets, "gx", split_axis=0, concat_axis=0, tiled=True),
            "gy",
            split_axis=1,
            concat_axis=1,
            tiled=True,
        )
    else:
        arrived = lax.all_to_all(
            lax.all_to_all(buckets, "gx", split_axis=0, concat_axis=0, tiled=True),
            "gy",
            split_axis=1,
            concat_axis=1,
            tiled=True,
        )
    return arrived.reshape(count_x * count_y * BLOCK, payload)[in_index]


def gather_rims(values, vector, routing, first_pass, count_x, count_y):
    out_index, in_index, local_row, has_local, has_far = routing
    strips = edge_strips(values, vector)
    strip_shape = strips.shape
    flat = strips.reshape(4 * SLOTS_DEV, strip_shape[2] * strip_shape[3])
    arrived = deliver(flat, out_index, in_index, first_pass, count_x, count_y)
    own_lines = flat[local_row]
    picked = jnp.where(has_far[:, None], arrived, jnp.where(has_local[:, None], own_lines, 0.0))
    return place_strips(picked.reshape(strip_shape), vector)


def on_device(fields, wet_mask, tile_of_slot, neighbor, rotation):
    count_x = lax.axis_size("gx")
    count_y = lax.axis_size("gy")
    device_count = count_x * count_y
    own_x = lax.axis_index("gx")
    own_y = lax.axis_index("gy")
    myself = own_x * count_y + own_y
    per_device = 4 * SLOTS_DEV
    source = sources(tile_of_slot, neighbor, rotation)
    target_dev = jnp.where(source >= 0, source // per_device, -1)
    owner_dev = jnp.arange(device_count, dtype=jnp.int32)[:, None]
    remote = (target_dev >= 0) & (target_dev != owner_dev)
    line_order = jnp.arange(per_device, dtype=jnp.int32)
    earlier = (
        (target_dev[:, :, None] == target_dev[:, None, :])
        & remote[:, None, :]
        & (line_order[None, None, :] < line_order[None, :, None])
    )
    position = jnp.sum(earlier.astype(jnp.int32), axis=2)
    my_target = lax.dynamic_index_in_dim(target_dev, myself, 0, keepdims=False)
    my_remote = lax.dynamic_index_in_dim(remote, myself, 0, keepdims=False)
    my_position = lax.dynamic_index_in_dim(position, myself, 0, keepdims=False)
    my_source = lax.dynamic_slice_in_dim(source, myself * SLOTS_DEV, SLOTS_DEV).reshape(per_device)
    has_link = my_source >= 0
    from_dev = jnp.where(has_link, my_source // per_device, 0)
    from_row = jnp.where(has_link, my_source % per_device, 0)
    from_pos = position[from_dev, from_row]
    has_local = has_link & (from_dev == myself)
    has_far = has_link & (from_dev != myself)
    out_index = jnp.where(my_remote, my_target * BLOCK + my_position, device_count * BLOCK)
    in_index = jnp.where(has_far, from_dev * BLOCK + from_pos, 0)
    local_row = jnp.where(has_local, from_row, 0)
    routing = (out_index, in_index, local_row, has_local, has_far)
    slot_count = fields.shape[0]
    wet_real = wet_mask.astype(jnp.float32).reshape(slot_count, TILE, TILE)
    masked = fields.reshape(slot_count, 6, TILE, TILE) * wet_real[:, None]
    rim_one = gather_rims(masked, True, routing, True, count_x, count_y)
    shifts = shifted(masked, rim_one)
    tracer_new = tracer_step(masked, shifts, wet_real)
    pressure = GRAVITY * jnp.concatenate(
        [tracer_new[:, 0:1], tracer_new[:, 0:1] + tracer_new[:, 1:2]], axis=1
    )
    rim_two = gather_rims(pressure, False, routing, False, count_x, count_y)
    first_new, second_new = momentum_step(masked, shifts, shifted(pressure, rim_two), wet_real)
    live = (lax.dynamic_slice_in_dim(tile_of_slot, myself * SLOTS_DEV, SLOTS_DEV) >= 0).astype(
        jnp.float32
    )
    combined = (
        jnp.concatenate([first_new, second_new, tracer_new], axis=1) * live[:, None, None, None]
    )
    return combined.reshape(slot_count, 6, TILE * TILE)


def solution(mesh):
    in_specs = (P(("gx", "gy"), None, None), P(("gx", "gy"), None), P(), P(), P())
    out_specs = P(("gx", "gy"), None, None)
    return jax.shard_map(
        on_device, mesh=mesh, in_specs=in_specs, out_specs=out_specs, check_vma=False
    )
```

profile of v0, /device:TPU:1, one launch (start us, length us, event | category | flops | bytes accessed | tf_op | source)
XLA Modules:
  0.0 106.5 jit_solution(4920259326607427526)
XLA Ops:
  0.0 0.7 copy-done.3
  0.7 1.4 %reduce.1 = f32[6,8100]{1,0:T(8,128)S(1)} reduce(f32[1,6,8100]{2,0,1:T(1,128)} %param.5, f32[]{:T(128)} %constant.121), dimensions={0}, to_apply=%param.5.reduce_sub_computation | reduce | bytes 388804 | tf_op args[0]
  2.1 0.4 reshape.844
  2.5 0.4 copy-done
  3.1 0.3 slice_reduce_fusion
  3.5 0.7 copy-done.1
  4.3 0.7 copy-done.2
  5.1 0.7 gather_fusion.2
  5.8 0.7 gather_fusion
  6.8 1.4 %scatter_custom_fusion = s32[256]{0:T(256)S(1)} fusion(s32[256]{0:T(256)S(1)} %get-tuple-element.58, s32[256]{0:T(256)S(1)} %iota.32, s32[]{:T(128)} %constant.89.clone.1), kind=kCustom, calls=%fused_computation.160 | custom fusion | bytes 1028 | tf_op jit(solution)/shard_map/scatter | solution.py:112
  8.2 6.8 %gather_fusion.1 = s32[1024]{0:T(1024)S(1)} fusion(s32[256]{0:T(256)S(1)} %scatter_custom_fusion, s32[1024]{0:T(1024)S(1)} %broadcast_clamp_fusion), kind=kCustom, calls=%fused_computation.1 | custom fusion | bytes 12288 | tf_op jit(solution)/shard_map/gather | solution.py:117
  15.2 0.2 fusion.12
  15.9 0.2 rev.21
  16.2 0.2 reduce.6
  16.9 1.5 %scatter_custom_fusion.1 = f32[256,540]{1,0:T(8,128)} fusion(s32[4]{0:T(128)S(1)} %get-tuple-element.60, f32[]{:T(128)} %constant.97.clone.1, f32[1,540]{1,0:T(1,128)S(1)} %stack.29, f32[1,540]{1,0:T(1,128)S(1)} %stack.28, f32[1,540]{1,0:T(1,128)S(1)} %stack.27, f32[1,540]{1,0:T(1,128)S(1)} %stack.26), kind=kCustom, calls=%fused_computation.16 | custom fusion | flops 6480 | bytes 563204 | tf_op jit(solution)/shard_map/scatter | solution.py:126
  18.4 10.0 %all-to-all-start = ((f32[16,16,1,540]{3,1,2,0:T(8,128)}), f32[16,16,1,540]{3,1,2,0:T(8,128)S(1)}, u32[]{:S(2)}, u32[]{:S(2)}) async-start(f32[16,16,1,540]{3,1,2,0:T(8,128)} %bitcast.5), calls=%async_computation | async-start | bytes 1310720 | tf_op jit(solution)/shard_map/all_to_all | solution.py:131
  28.4 0.6 gather_fusion.3
  29.1 19.3 %all-to-all-done = f32[16,16,1,540]{3,1,2,0:T(8,128)S(1)} async-done(((f32[16,16,1,540]{3,1,2,0:T(8,128)}), f32[16,16,1,540]{3,1,2,0:T(8,128)S(1)}, u32[]{:S(2)}, u32[]{:S(2)}) %all-to-all-start) | async-done | bytes 552992 | tf_op jit(solution)/shard_map/all_to_all | solution.py:131
  48.4 1.0 copy.92
  49.4 6.8 %all-to-all-start.1 = ((f32[16,16,1,540]{3,0,2,1:T(8,128)}), f32[16,16,1,540]{3,0,2,1:T(8,128)S(1)}, u32[]{:S(2)}, u32[]{:S(2)}) async-start(f32[16,16,1,540]{3,0,2,1:T(8,128)} %copy.92), calls=%async_computation.1 | async-start | bytes 1310720 | tf_op jit(solution)/shard_map/all_to_all | solution.py:130
  56.2 0.6 gather_fusion.5
  56.9 0.1 fusion.55
  57.1 11.5 %all-to-all-done.1 = f32[16,16,1,540]{3,0,2,1:T(8,128)S(1)} async-done(((f32[16,16,1,540]{3,0,2,1:T(8,128)}), f32[16,16,1,540]{3,0,2,1:T(8,128)S(1)}, u32[]{:S(2)}, u32[]{:S(2)}) %all-to-all-start.1) | async-done | bytes 552992 | tf_op jit(solution)/shard_map/all_to_all | solution.py:130
  68.6 0.2 copy.93
  68.8 0.6 gather_fusion.4
  70.2 0.2 copy.96
  70.4 0.2 copy.97
  70.6 0.1 add_multiply_fusion
  70.8 0.2 slice_reduce_fusion.1
  71.4 0.5 broadcast.953
  71.9 0.7 reduce.26
  72.8 1.3 %scatter_custom_fusion.2 = f32[256,180]{1,0:T(8,128)} fusion(s32[4]{0:T(128)S(1)} %get-tuple-element.60, f32[]{:T(128)} %constant.97.clone.1, f32[1,180]{1,0:T(1,128)S(1)} %stack.34, f32[1,180]{1,0:T(1,128)S(1)} %stack.33, f32[1,180]{1,0:T(1,128)S(1)} %stack.32, f32[1,180]{1,0:T(1,128)S(1)} %stack.31), kind=kCustom, calls=%fused_computation.47 | custom fusion | flops 2160 | bytes 188420 | tf_op jit(solution)/shard_map/scatter | solution.py:126
  74.1 4.0 %all-to-all-start.2 = ((f32[16,16,1,180]{3,1,2,0:T(8,128)}), f32[16,16,1,180]{3,1,2,0:T(8,128)S(1)}, u32[]{:S(2)}, u32[]{:S(2)}) async-start(f32[16,16,1,180]{3,1,2,0:T(8,128)} %bitcast.20), calls=%async_computation.2 | async-start | bytes 524288 | tf_op jit(solution)/shard_map/all_to_all | solution.py:139
  78.2 0.6 dynamic_slice.21
  79.4 0.2 concatenate.142
  79.6 0.6 gather_fusion.7
  80.3 9.6 %all-to-all-done.2 = f32[16,16,1,180]{3,1,2,0:T(8,128)S(1)} async-done(((f32[16,16,1,180]{3,1,2,0:T(8,128)}), f32[16,16,1,180]{3,1,2,0:T(8,128)S(1)}, u32[]{:S(2)}, u32[]{:S(2)}) %all-to-all-start.2) | async-done | bytes 184352 | tf_op jit(solution)/shard_map/all_to_all | solution.py:139
  89.9 0.8 copy.99
  90.7 3.5 %all-to-all-start.3 = ((f32[16,16,1,180]{3,0,2,1:T(8,128)}), f32[16,16,1,180]{3,0,2,1:T(8,128)S(1)}, u32[]{:S(2)}, u32[]{:S(2)}) async-start(f32[16,16,1,180]{3,0,2,1:T(8,128)} %copy.99), calls=%async_computation.3 | async-start | bytes 524288 | tf_op jit(solution)/shard_map/all_to_all | solution.py:138
  94.4 9.1 %all-to-all-done.3 = f32[16,16,1,180]{3,0,2,1:T(8,128)S(1)} async-done(((f32[16,16,1,180]{3,0,2,1:T(8,128)}), f32[16,16,1,180]{3,0,2,1:T(8,128)S(1)}, u32[]{:S(2)}, u32[]{:S(2)}) %all-to-all-start.3) | async-done | bytes 184352 | tf_op jit(solution)/shard_map/all_to_all | solution.py:138
  103.4 0.2 copy.100
  103.6 0.6 gather_fusion.6
  104.4 0.2 fusion.34
  104.6 0.2 concatenate.141
  105.0 0.1 copy.102
  105.1 0.2 fusion.27
  105.3 0.2 concatenate.136
  105.6 0.9 copy.104
  (87 shorter events, 4.4 us)
Async XLA Ops:
  0.0 0.7 copy-start.3
  2.1 0.8 copy-start
  3.4 0.7 copy-start.1
  4.3 0.7 copy-start.2
  18.4 30.0 %all-to-all-start = ((f32[16,16,1,540]{3,1,2,0:T(8,128)}), f32[16,16,1,540]{3,1,2,0:T(8,128)S(1)}, u32[]{:S(2)}, u32[]{:S(2)}) async-start(f32[16,16,1,540]{3,1,2,0:T(8,128)} %bitcast.5), calls=%async_computation | async-start | bytes 1310720 | tf_op jit(solution)/shard_map/all_to_all | solution.py:131
  49.4 19.2 %all-to-all-start.1 = ((f32[16,16,1,540]{3,0,2,1:T(8,128)}), f32[16,16,1,540]{3,0,2,1:T(8,128)S(1)}, u32[]{:S(2)}, u32[]{:S(2)}) async-start(f32[16,16,1,540]{3,0,2,1:T(8,128)} %copy.92), calls=%async_computation.1 | async-start | bytes 1310720 | tf_op jit(solution)/shard_map/all_to_all | solution.py:130
  74.1 15.8 %all-to-all-start.2 = ((f32[16,16,1,180]{3,1,2,0:T(8,128)}), f32[16,16,1,180]{3,1,2,0:T(8,128)S(1)}, u32[]{:S(2)}, u32[]{:S(2)}) async-start(f32[16,16,1,180]{3,1,2,0:T(8,128)} %bitcast.20), calls=%async_computation.2 | async-start | bytes 524288 | tf_op jit(solution)/shard_map/all_to_all | solution.py:139
  90.7 12.7 %all-to-all-start.3 = ((f32[16,16,1,180]{3,0,2,1:T(8,128)}), f32[16,16,1,180]{3,0,2,1:T(8,128)S(1)}, u32[]{:S(2)}, u32[]{:S(2)}) async-start(f32[16,16,1,180]{3,0,2,1:T(8,128)} %copy.99), calls=%async_computation.3 | async-start | bytes 524288 | tf_op jit(solution)/shard_map/all_to_all | solution.py:138
where the time goes:
time: 107 us; the launch traced here: 106 us
  waiting for transfers between devices  49.6 us (46%)
  local copies, waits for them, and re-layouts  24.8 us (23%)
  starting transfers between devices  24.3 us (23%)
  other arithmetic  6.69 us (6%)
  between operations  1.09 us (1%)
    all_to_all x2, waiting for transfers between devices, deliver(): lax.all_to_all(buckets, 'gx', split_axis=0, concat_axis=0, tiled=True)  28.9 us
    all_to_all x2, waiting for transfers between devices, deliver(): lax.all_to_all(lax.all_to_all(buckets, 'gx', split_axis=0, concat_axis=0,...  20.6 us
    all_to_all x2, starting transfers between devices, deliver(): lax.all_to_all(buckets, 'gx', split_axis=0, concat_axis=0, tiled=True)  14 us
    all_to_all x2, starting transfers between devices, deliver(): lax.all_to_all(lax.all_to_all(buckets, 'gx', split_axis=0, concat_axis=0,...  10.3 us
    gather x2, local copies, waits for them, and re-layouts, sources(): slot_of_tile[jnp.clip(near_tile, 0, tile_count - 1)]  6.96 us
    scatter x2, other arithmetic, deliver(): buckets = jnp.zeros((count_x * count_y * BLOCK, payload), jnp.float32).at...  2.74 us
    unnamed x11, local copies, waits for them, and re-layouts  2.72 us
  transfers between devices with their start and end apart: 4, of which 4 were waited for; matrix products, arithmetic and copies ran while one was open for 3% of the time, Pallas kernels for 0%

commit v1 on v0

v1 whole, which is shorter than its diff:
```python
import jax
import jax.numpy as jnp
from jax import lax
from jax.experimental import pallas as pl
from jax.experimental.pallas import tpu as pltpu
from jax.sharding import PartitionSpec as P

TILE = 90
CELLS = TILE * TILE
LANES = 128
CHUNKS = 64
WIDE = LANES * CHUNKS
HALF = 45
LAST = CELLS - TILE - (CHUNKS - 2) * LANES

ADVECT = 0.25
DIFFUSE = 0.15
STEP_SIZE = 0.5
CORIOLIS = 0.3
GRAVITY = 0.8

AXES = ("gx", "gy")
VMEM = pl.BlockSpec(memory_space=pltpu.VMEM)
SMEM = pl.BlockSpec(memory_space=pltpu.SMEM)
ANY = pl.BlockSpec(memory_space=pl.ANY)


def link_x_even(x, y, nx, ny):
    return x ^ 1, y


def link_x_odd(x, y, nx, ny):
    return (((x + nx - 1) % nx ^ 1) + 1) % nx, y


def link_y_even(x, y, nx, ny):
    return x, y ^ 1


def link_y_odd(x, y, nx, ny):
    if y == 0 or y == ny - 1:
        return (x + nx // 2) % nx, y
    return x, ((y - 1) ^ 1) + 1


LINKS = (link_y_odd, link_x_even, link_y_even, link_x_odd)


def pairs_of(link, nx, ny):
    out = []
    for x in range(nx):
        for y in range(ny):
            to_x, to_y = link(x, y, nx, ny)
            out.append((x * ny + y, to_x * ny + to_y))
    return out


def partner(me, which, nx, ny):
    x, y = me // ny, me % ny
    if which == 0:
        pole = (y == 0) | (y == ny - 1)
        step = jnp.where(y % 2 == 1, 1, -1)
        return jnp.where(pole, (x + nx // 2) % nx * ny + y, me + step)
    if which == 1:
        return me + jnp.where(x % 2 == 0, ny, -ny)
    if which == 2:
        return me + jnp.where(y % 2 == 0, 1, -1)
    return (x + jnp.where(x % 2 == 1, 1, nx - 1)) % nx * ny + y


def lanes():
    return lax.broadcasted_iota(jnp.int32, (8, LANES), 1)


def rows():
    return lax.broadcasted_iota(jnp.int32, (8, LANES), 0)


def pick(values, index):
    return jnp.take_along_axis(values, index, axis=1)


def tiled(values, count):
    return jnp.concatenate([values] * count, axis=1)


def column_of():
    cell = lax.broadcasted_iota(jnp.int32, (8, WIDE), 1)
    line = jnp.floor((cell.astype(jnp.float32) + 0.5) * (1.0 / TILE)).astype(jnp.int32)
    return cell, cell - TILE * line


def edge_lines(state, column):
    lane = lanes()
    edge = (column == 0) | (column == TILE - 1)
    parts = []
    for low, high in ((0, HALF), (HALF, CHUNKS)):
        found = jnp.zeros((8, LANES), jnp.float32)
        for c in range(low, high):
            cut = slice(c * LANES, (c + 1) * LANES)
            found = jnp.where(edge[:, cut], state[:, cut], found)
        parts.append(found)
    east_at = (TILE * lane + TILE - 1) & (LANES - 1)
    west_at = (TILE * lane) & (LANES - 1)
    east = jnp.where(lane < 64, pick(parts[0], east_at), pick(parts[1], east_at))
    west = jnp.where(lane < 64, pick(parts[0], west_at), pick(parts[1], west_at))
    south = state[:, :LANES]
    before = pltpu.roll(state[:, (CHUNKS - 2) * LANES:(CHUNKS - 1) * LANES], LANES - LAST, 1)
    after = pltpu.roll(state[:, (CHUNKS - 1) * LANES:], LANES - LAST, 1)
    north = jnp.where(lane < LANES - LAST, before, after)
    return [south, east, north, west]


def spread(lines, cell, column):
    south, east, north, west = lines
    lane = lanes()
    odd = (lane & 1) == 1
    line_at = (37 * ((lane + jnp.where(odd, 39, 0)) >> 1)) & 63
    early = jnp.where(odd, pick(east, line_at), pick(west, line_at))
    late = jnp.where(odd, pick(east, line_at + 64), pick(west, line_at + 64))
    sides = jnp.concatenate([early] * HALF + [late] * (CHUNKS - HALF), axis=1)
    edge = (column == 0) | (column == TILE - 1)
    out = jnp.where(edge, sides, 0.0)
    first = jnp.where(lane < TILE, south, 0.0) + out[:, :LANES]
    moved = pltpu.roll(north, LAST, 1)
    before = out[:, (CHUNKS - 2) * LANES:(CHUNKS - 1) * LANES] + jnp.where(lane >= LAST, moved, 0.0)
    after = out[:, (CHUNKS - 1) * LANES:] + jnp.where(lane < LAST + TILE - LANES, moved, 0.0)
    return jnp.concatenate([first, out[:, LANES:(CHUNKS - 2) * LANES], before, after], axis=1)


def neighbours(state):
    cell, column = column_of()
    right = jnp.where(column == TILE - 1, 0.0, pltpu.roll(state, WIDE - 1, 1))
    left = jnp.where(column == 0, 0.0, pltpu.roll(state, 1, 1))
    up = jnp.where(cell >= CELLS - TILE, 0.0, pltpu.roll(state, WIDE - TILE, 1))
    down = jnp.where(cell < TILE, 0.0, pltpu.roll(state, TILE, 1))
    return right, left, up, down, cell, column


def row_of(values):
    return lax.broadcasted_iota(jnp.int32, values.shape, 0)


def repeated(values, first):
    row = row_of(values)
    if first == 0:
        pair = jnp.where(row < 2, values, pltpu.roll(values, 2, 0))
    else:
        pair = jnp.where(row < 4, values, pltpu.roll(values, 2, 0))
        pair = jnp.where(row < 2, pltpu.roll(values, 6, 0), pair)
        return pair
    return jnp.where(row < 4, pair, pltpu.roll(values, 4, 0))


def wet_rows(values):
    return jnp.broadcast_to(values[6:7], values.shape)


def turned(line, turns):
    row = row_of(line)
    swapped = jnp.where(row < 2, pltpu.roll(line, 6, 0), pltpu.roll(line, 2, 0))
    velocity = row < 4
    second = jnp.where(row < 2, swapped, -swapped)
    odd = jnp.where(turns % 2 == 1, 1, 0)
    out = jnp.where(jnp.logical_and(velocity, odd == 1), second, line)
    back = jnp.where(turns >= 2, 1, 0)
    return jnp.where(jnp.logical_and(velocity, back == 1), -out, out)


def flipped(line):
    return pick(line, jnp.maximum(TILE - 1 - lanes(), 0))


ROUTE = 48


def outgoing(lines, route, pay_refs, own_ref, vector):
    sent = []
    for side in range(4):
        line = jnp.where(route[32 + side] == 1, flipped(lines[side]), lines[side])
        if vector:
            line = turned(line, route[36 + side])
        sent.append(line)
    for link in range(4):
        total = jnp.zeros((8, LANES), jnp.float32)
        for side in range(4):
            total = jnp.where(route[4 * link + side] == 1, sent[side], total)
        pay_refs[link][...] = total
    for target in range(4):
        total = jnp.zeros((8, LANES), jnp.float32)
        for side in range(4):
            total = jnp.where(route[16 + 4 * side + target] == 1, sent[side], total)
        own_ref[8 * target:8 * target + 8, :] = total


def rims_of(route, own_ref, came_refs):
    out = []
    for side in range(4):
        rim = own_ref[8 * side:8 * side + 8, :]
        for link in range(4):
            rim = jnp.where(route[4 * link + side] == 1, came_refs[link][...], rim)
        out.append(rim)
    return out


def load_kernel(shape, me_ref, tiles_ref, near_ref, turn_ref, fields_ref, wet_ref,
                state_ref, lines_ref, own_ref, pay0, pay1, pay2, pay3, route, raw, wet_raw, sems):
    nx, ny = shape
    copies = [pltpu.make_async_copy(fields_ref.at[c, 0], raw.at[c], sems.at[c])
              for c in range(6)]
    copies.append(pltpu.make_async_copy(wet_ref.at[0], wet_raw.at[0], sems.at[6]))
    for copy in copies:
        copy.start()
    me = me_ref[0]
    tile = tiles_ref[me]
    live = tile >= 0
    held = jnp.maximum(tile, 0)
    near = [jnp.where(live, near_ref[side, held], -1) for side in range(4)]
    turn = [turn_ref[side, held] for side in range(4)]
    for link in range(4):
        other = tiles_ref[partner(me, link, nx, ny)]
        for side in range(4):
            route[4 * link + side] = jnp.where((near[side] >= 0) & (near[side] == other), 1, 0)
    for side in range(4):
        target = (side + 2 + turn[side]) % 4
        for k in range(4):
            route[16 + 4 * side + k] = jnp.where((near[side] >= 0) & (near[side] == tile) & (target == k), 1, 0)
        route[32 + side] = jnp.where((target < 2) != (side >= 2), 1, 0)
        route[36 + side] = (4 - turn[side]) % 4
    route[40] = jnp.where(live, 1, 0)
    for copy in copies:
        copy.wait()
    state_ref[:, (CHUNKS - 1) * LANES:] = jnp.zeros((8, LANES), jnp.float32)
    for low, high in ((0, (CHUNKS - 1) * LANES), ((CHUNKS - 1) * LANES, CELLS)):
        size = (8, high - low)
        row = lax.broadcasted_iota(jnp.int32, size, 0)
        wet = jnp.broadcast_to(wet_raw[0:1, low:high].astype(jnp.float32), size)
        state_ref[:, low:high] = jnp.where(row < 6, raw[:, low:high] * wet, jnp.where(row == 6, wet, 0.0))
    state = state_ref[...]
    cell, column = column_of()
    lines = edge_lines(state, column)
    for side in range(4):
        lines_ref[8 * side:8 * side + 8, :] = lines[side]
    outgoing(lines, route, (pay0, pay1, pay2, pay3), own_ref, True)


def inner_kernel(state_ref, base_ref, base_lines_ref):
    state = state_ref[...]
    right, left, up, down, cell, column = neighbours(state)
    first, second, wet = repeated(state, 0), repeated(state, 2), wet_rows(state)
    along = first * (right - left) + second * (up - down)
    round_sum = right + left + up + down - 4.0 * state
    base = wet * (state - (0.5 * ADVECT) * along + DIFFUSE * round_sum)
    base_ref[...] = base
    lines = edge_lines(base, column)
    for side in range(4):
        base_lines_ref[8 * side:8 * side + 8, :] = lines[side]


def at_ends(line, lane_from, lane_to):
    value = jnp.broadcast_to(line[:, lane_from:lane_from + 1], (8, LANES))
    return jnp.where(lanes() == lane_to, value, 0.0)


def edge_kernel(route, lines_ref, own_ref, base_lines_ref, came0, came1, came2, came3,
                patch_ref, own_two_ref, pay0, pay1, pay2, pay3):
    rims = rims_of(route, own_ref, (came0, came1, came2, came3))
    patch = []
    for side in range(4):
        line = lines_ref[8 * side:8 * side + 8, :]
        drift = repeated(line, 0 if side % 2 == 1 else 2)
        sign = 1.0 if side in (1, 2) else -1.0
        patch.append(wet_rows(line) * (DIFFUSE - (sign * 0.5 * ADVECT) * drift) * rims[side])
    south, east, north, west = patch
    for side in range(4):
        patch_ref[8 * side:8 * side + 8, :] = patch[side]
    end = TILE - 1
    whole = [
        south + at_ends(west, 0, 0) + at_ends(east, 0, end),
        east + at_ends(south, end, 0) + at_ends(north, end, end),
        north + at_ends(west, end, 0) + at_ends(east, end, end),
        west + at_ends(south, 0, 0) + at_ends(north, 0, end),
    ]
    press = []
    for side in range(4):
        tracer = base_lines_ref[8 * side:8 * side + 8, :] + whole[side]
        row = row_of(tracer)
        press.append(GRAVITY * jnp.where(row == 5, tracer + pltpu.roll(tracer, 1, 0), tracer))
    outgoing(press, route, (pay0, pay1, pay2, pay3), own_two_ref, False)


def middle_kernel(route, state_ref, base_ref, patch_ref, out_ref):
    state = state_ref[...]
    cell, column = column_of()
    patch = [patch_ref[8 * side:8 * side + 8, :] for side in range(4)]
    base = base_ref[...] + spread(patch, cell, column)
    row = lax.broadcasted_iota(jnp.int32, (8, WIDE), 0)
    pressure = GRAVITY * jnp.where(row == 5, base + pltpu.roll(base, 1, 0), base)
    right, left, up, down, cell, column = neighbours(pressure)
    slope = jnp.where(row < 2, pltpu.roll(right - left, 4, 0), pltpu.roll(up - down, 6, 0))
    swapped = jnp.where(row < 2, pltpu.roll(state, 6, 0), -pltpu.roll(state, 2, 0))
    force = STEP_SIZE * (CORIOLIS * swapped - 0.5 * slope)
    live = jnp.where(route[40] == 1, 1.0, 0.0)
    out_ref[...] = (base + jnp.where(row < 4, wet_rows(state) * force, 0.0)) * live


def last_kernel(route, lines_ref, own_ref, almost_ref, came0, came1, came2, came3, out_ref, full, sems):
    rims = rims_of(route, own_ref, (came0, came1, came2, came3))
    patch = []
    for side in range(4):
        wet = wet_rows(lines_ref[8 * side:8 * side + 8, :])
        row = row_of(wet)
        shift = 4 if side % 2 == 1 else 6
        rim = pltpu.roll(rims[side], shift, 0)
        mine = row < 2 if side % 2 == 1 else (row >= 2) & (row < 4)
        sign = -1.0 if side in (1, 2) else 1.0
        patch.append(jnp.where(mine, (sign * 0.5 * STEP_SIZE) * wet * rim, 0.0))
    cell, column = column_of()
    full[...] = (almost_ref[...] + spread(patch, cell, column))[:, :CELLS]
    copies = [pltpu.make_async_copy(full.at[c], out_ref.at[c, 0], sems.at[c])
              for c in range(6)]
    for copy in copies:
        copy.start()
    for copy in copies:
        copy.wait()


def sds(*shape, dtype=jnp.float32):
    return jax.ShapeDtypeStruct(shape, dtype)


PARAMS = pltpu.CompilerParams(vmem_limit_bytes=16 * 1024 * 1024)


def on_device(nx, ny, fields, wet_mask, tile_of_slot, neighbor, rotation):
    me = (lax.axis_index("gx") * ny + lax.axis_index("gy")).astype(jnp.int32).reshape(1)
    line = sds(8, LANES)
    wide = sds(8, WIDE)
    four = sds(32, LANES)
    state, lines, own, *pays, route = pl.pallas_call(
        lambda *refs: load_kernel((nx, ny), *refs),
        out_shape=[wide, four, four, line, line, line, line, sds(ROUTE, dtype=jnp.int32)],
        in_specs=[SMEM, SMEM, SMEM, SMEM, ANY, ANY],
        out_specs=[VMEM] * 7 + [SMEM],
        scratch_shapes=[pltpu.VMEM((8, CELLS), jnp.float32), pltpu.VMEM((8, CELLS), jnp.int32),
                        pltpu.SemaphoreType.DMA((7,))],
        compiler_params=PARAMS, name="load",
    )(me, tile_of_slot, neighbor.T, rotation.T, fields.reshape(6, 1, CELLS), wet_mask)
    pairs = [pairs_of(link, nx, ny) for link in LINKS]
    came = [lax.ppermute(pay, AXES, pair) for pay, pair in zip(pays, pairs)]
    base, base_lines = pl.pallas_call(
        inner_kernel, out_shape=[wide, four], in_specs=[VMEM], out_specs=[VMEM] * 2,
        compiler_params=PARAMS, name="inner",
        cost_estimate=pl.CostEstimate(flops=2000000, bytes_accessed=600000, transcendentals=0),
    )(state)
    patch, own_two, *pays = pl.pallas_call(
        edge_kernel, out_shape=[four, four, line, line, line, line],
        in_specs=[SMEM] + [VMEM] * 7, out_specs=[VMEM] * 6,
        compiler_params=PARAMS, name="edge",
    )(route, lines, own, base_lines, *came)
    came = [lax.ppermute(pay, AXES, pair) for pay, pair in zip(pays, pairs)]
    almost = pl.pallas_call(
        middle_kernel, out_shape=wide, in_specs=[SMEM] + [VMEM] * 3, out_specs=VMEM,
        compiler_params=PARAMS, name="middle",
        cost_estimate=pl.CostEstimate(flops=2000000, bytes_accessed=800000, transcendentals=0),
    )(route, state, base, patch)
    out = pl.pallas_call(
        last_kernel, out_shape=sds(6, 1, CELLS), in_specs=[SMEM] + [VMEM] * 7, out_specs=ANY,
        scratch_shapes=[pltpu.VMEM((8, CELLS), jnp.float32), pltpu.SemaphoreType.DMA((6,))],
        compiler_params=PARAMS, name="last",
    )(route, lines, own_two, almost, *came)
    return out.reshape(1, 6, CELLS)


def solution(mesh):
    nx, ny = mesh.shape["gx"], mesh.shape["gy"]
    in_specs = (P(AXES, None, None), P(AXES, None), P(), P(), P())
    return jax.shard_map(lambda *args: on_device(nx, ny, *args), mesh=mesh, in_specs=in_specs,
                         out_specs=P(AXES, None, None), check_vma=False)
```

time: 107 us -> 26.9 us (0.25)
  the two profiles are of different devices: /device:TPU:1 before, /device:TPU:22 now
where the time goes in v1:
time: 26.9 us; the launch traced here: 26.8 us
  starting transfers between devices  12.8 us (48%)
  waiting for transfers between devices  5.96 us (22%)
  Pallas kernels  5.53 us (21%)
  local copies, waits for them, and re-layouts  2.39 us (9%)
    ppermute x8, starting transfers between devices, on_device(): came = [lax.ppermute(pay, AXES, pair) for pay, pair in zip(pays, pairs)]  12.8 us
    ppermute x8, waiting for transfers between devices, on_device(): came = [lax.ppermute(pay, AXES, pair) for pay, pair in zip(pays, pairs)]  5.96 us
    unnamed x10, local copies, waits for them, and re-layouts  2.39 us
    pallas_call x1, Pallas kernels, on_device(): pl.pallas_call(lambda *refs: load_kernel((nx, ny), *refs), out_shape=[wid...  1.8 us
    pallas_call x1, Pallas kernels, on_device(): pl.pallas_call(last_kernel, out_shape=sds(6, 1, CELLS), in_specs=[SMEM] +...  1.41 us
    pallas_call x1, Pallas kernels, on_device(): pl.pallas_call(middle_kernel, out_shape=wide, in_specs=[SMEM] + [VMEM] *...  1.07 us
    pallas_call x1, Pallas kernels, on_device(): pl.pallas_call(edge_kernel, out_shape=[four, four, line, line, line, line...  0.71 us
  transfers between devices with their start and end apart: 8, of which 3 were waited for; matrix products, arithmetic and copies ran while one was open for 0% of the time, Pallas kernels for 6%

profile of v1, /device:TPU:22, one launch (start us, length us, event | category | flops | bytes accessed | tf_op | source)
XLA Modules:
  0.0 26.8 jit_solution(13773749986983714688)
XLA Ops:
  0.0 0.0 copy-start.3
  0.0 0.0 copy-start.2
  0.0 0.0 copy-start.4
  0.0 0.7 %copy-done.3 = s32[256,4]{0,1:T(4,128)S(1)} copy-done((s32[256,4]{0,1:T(4,128)S(1)}, s32[256,4]{0,1:T(4,128)}, u32[]{:S(2)}) %copy-start.3) | copy-done | bytes 4120
  0.7 0.0 copy-done.2
  0.7 0.0 copy-done.4
  0.7 0.0 copy-start
  0.7 0.9 %copy-done = f32[1,6,8100]{2,0,1:T(1,128)S(1)} copy-done((f32[1,6,8100]{2,0,1:T(1,128)S(1)}, f32[1,6,8100]{2,0,1:T(1,128)}, u32[]{:S(2)}) %copy-start) | copy-done | bytes 194424
  1.6 0.0 copy-start.1
  1.6 0.8 %copy-done.1 = s32[1,8100]{1,0:T(1,128)S(1)} copy-done((s32[1,8100]{1,0:T(1,128)S(1)}, s32[1,8100]{1,0:T(1,128)}, u32[]{:S(2)}) %copy-start.1) | copy-done | bytes 32424
  2.4 1.8 %load.1 = (f32[8,8192]{1,0:T(8,128)S(1)}, f32[32,128]{1,0:T(8,128)S(1)}, f32[32,128]{1,0:T(8,128)S(1)}, f32[8,128]{1,0:T(8,128)S(1)}, f32[8,128]{1,0:T(8,128)S(1...) custom-call(s32[1]{0:T(128)} %bitcast.refs_0_, s32[256]{0:T(256)S(1)} %copy-done.4, ...), custom_call_target="tpu_custom_call" | custom-call | tf_op jit(solution)/shard_map/load/pallas_call | solution.py:340
  4.2 0.5 %collective-permute-start = (f32[8,128]{1,0:T(8,128)S(1)}, f32[8,128]{1,0:T(8,128)S(1)}, u32[]{:S(2)}, u32[]{:S(2)}) collective-permute-start(f32[8,128]{1,0:T(8,128)S(1)} %get-tuple-element.26), channel_id=1, source_target_pairs={{0,128},{1,2},{2,1},{3,4},{4,3},{5,6},{6,5},{7,8},{8,7},{9,10},{10... | collective-permute-start | bytes 12296 | tf_op jit(solution)/shard_map/ppermute | solution.py:350
  4.7 0.0 collective-permute-start.1
  4.7 8.0 %collective-permute-start.2 = (f32[8,128]{1,0:T(8,128)S(1)}, f32[8,128]{1,0:T(8,128)S(1)}, u32[]{:S(2)}, u32[]{:S(2)}) collective-permute-start(f32[8,128]{1,0:T(8,128)S(1)} %get-tuple-element.28), channel_id=1, source_target_pairs={{0,1},{1,0},{2,3},{3,2},{4,5},{5,4},{6,7},{7,6},{8,9},{9,8},{10,11... | collective-permute-start | bytes 12296 | tf_op jit(solution)/shard_map/ppermute | solution.py:350
  12.8 0.0 collective-permute-start.3
  12.8 0.5 %inner.1 = (f32[8,8192]{1,0:T(8,128)S(1)}, f32[32,128]{1,0:T(8,128)S(1)}) custom-call(f32[8,8192]{1,0:T(8,128)S(1)} %get-tuple-element.24.state_ref), custom_call_target="tpu_custom_call" | custom-call | flops 2000000 | bytes 600000 | tf_op jit(solution)/shard_map/inner/pallas_call | solution.py:351
  13.3 0.0 collective-permute-done.came0
  13.3 0.0 collective-permute-done.1.came1
  13.3 1.0 %collective-permute-done.2.came2 = f32[8,128]{1,0:T(8,128)S(1)} collective-permute-done((f32[8,128]{1,0:T(8,128)S(1)}, f32[8,128]{1,0:T(8,128)S(1)}, u32[]{:S(2)}, u32[]{:S(2)}) %collective-permute-start.2) | collective-permute-done | bytes 4128 | tf_op jit(solution)/shard_map/ppermute | solution.py:350
  14.4 2.7 %collective-permute-done.3.came3 = f32[8,128]{1,0:T(8,128)S(1)} collective-permute-done((f32[8,128]{1,0:T(8,128)S(1)}, f32[8,128]{1,0:T(8,128)S(1)}, u32[]{:S(2)}, u32[]{:S(2)}) %collective-permute-start.3) | collective-permute-done | bytes 4128 | tf_op jit(solution)/shard_map/ppermute | solution.py:350
  17.0 0.7 %edge.1 = (f32[32,128]{1,0:T(8,128)S(1)}, f32[32,128]{1,0:T(8,128)S(1)}, f32[8,128]{1,0:T(8,128)S(1)}, f32[8,128]{1,0:T(8,128)S(1)}, f32[8,128]{1,0:T(8,128)S(1)}, /*index=5*/f32[8,128]{1,0:T(8,128)S(1)}) custom-call(s32[48]{0:T(128)S(1)} %get-tuple-element.21.route, f32[32,128]{1,0:T(8,128)S(1)} %get-tuple-element.22.lines_ref, ...), custom_call_target="tpu_custom_call" | custom-call | tf_op jit(solution)/shard_map/edge/pallas_call | solution.py:356
  17.7 0.1 collective-permute-start.4
  17.8 0.1 collective-permute-start.5
  17.9 3.2 %collective-permute-start.6 = (f32[8,128]{1,0:T(8,128)S(1)}, f32[8,128]{1,0:T(8,128)S(1)}, u32[]{:S(2)}, u32[]{:S(2)}) collective-permute-start(f32[8,128]{1,0:T(8,128)S(1)} %get-tuple-element.35), channel_id=1, source_target_pairs={{0,1},{1,0},{2,3},{3,2},{4,5},{5,4},{6,7},{7,6},{8,9},{9,8},{10,11... | collective-permute-start | bytes 12296 | tf_op jit(solution)/shard_map/ppermute | solution.py:361
  21.1 0.9 %collective-permute-start.7 = (f32[8,128]{1,0:T(8,128)S(1)}, f32[8,128]{1,0:T(8,128)S(1)}, u32[]{:S(2)}, u32[]{:S(2)}) collective-permute-start(f32[8,128]{1,0:T(8,128)S(1)} %get-tuple-element.36), channel_id=1, source_target_pairs={{0,240},{1,241},{2,242},{3,243},{4,244},{5,245},{6,246},{7,247},{8... | collective-permute-start | bytes 12296 | tf_op jit(solution)/shard_map/ppermute | solution.py:361
  22.0 1.1 %middle.1.almost_ref = f32[8,8192]{1,0:T(8,128)S(1)} custom-call(s32[48]{0:T(128)S(1)} %get-tuple-element.21.route, f32[8,8192]{1,0:T(8,128)S(1)} %get-tuple-element.24.state_ref, f32[8,8192]{1,0:T(8,128)S(1)} %get-tuple-element.31.base_ref, f32[32,128]{1,0:T(8,128)S(1)} %get-tuple-element.32.patch_ref), custom_call_target="tpu_custom_call" | custom-call | flops 2000000 | bytes 800000 | tf_op jit(solution)/shard_map/middle/pallas_call | solution.py:362
  23.0 0.0 collective-permute-done.4.came0
  23.1 0.0 collective-permute-done.5.came1
  23.1 0.0 collective-permute-done.6.came2
  23.1 2.3 %collective-permute-done.7.came3 = f32[8,128]{1,0:T(8,128)S(1)} collective-permute-done((f32[8,128]{1,0:T(8,128)S(1)}, f32[8,128]{1,0:T(8,128)S(1)}, u32[]{:S(2)}, u32[]{:S(2)}) %collective-permute-start.7) | collective-permute-done | bytes 4128 | tf_op jit(solution)/shard_map/ppermute | solution.py:361
  25.3 1.4 %last.1 = f32[6,1,8100]{2,1,0:T(1,128)} custom-call(s32[48]{0:T(128)S(1)} %get-tuple-element.21.route, f32[32,128]{1,0:T(8,128)S(1)} %get-tuple-element.22.lines_ref, f32[32,128]{1,0:T(8,128)S(1)} %get-tuple-element.30.own_ref, f32[8,8192]{1,0:T(8,128)S(1)} %middle.1.almost_ref, f32[8,128]{1,0:T(8,128)S(1)} %collective-permute-done.4.came0, ...), custom_call_target="tpu_custom_call" | custom-call | tf_op jit(solution)/shard_map/last/pallas_call | solution.py:367
Async XLA Ops:
  0.0 0.7 %copy-start.3 = (s32[256,4]{0,1:T(4,128)S(1)}, s32[256,4]{0,1:T(4,128)}, u32[]{:S(2)}) copy-start(s32[256,4]{0,1:T(4,128)} %param.9) | copy-start | bytes 12292
  0.0 0.7 %copy-start.2 = (s32[256,4]{0,1:T(4,128)S(1)}, s32[256,4]{0,1:T(4,128)}, u32[]{:S(2)}) copy-start(s32[256,4]{0,1:T(4,128)} %param.8) | copy-start | bytes 12292
  0.0 0.7 %copy-start.4 = (s32[256]{0:T(256)S(1)}, s32[256]{0:T(256)}, u32[]{:S(2)}) copy-start(s32[256]{0:T(256)} %refs_1_.1) | copy-start | bytes 3076
  0.7 0.9 %copy-start = (f32[1,6,8100]{2,0,1:T(1,128)S(1)}, f32[1,6,8100]{2,0,1:T(1,128)}, u32[]{:S(2)}) copy-start(f32[1,6,8100]{2,0,1:T(1,128)} %param.5) | copy-start | bytes 583204
  1.6 0.8 %copy-start.1 = (s32[1,8100]{1,0:T(1,128)S(1)}, s32[1,8100]{1,0:T(1,128)}, u32[]{:S(2)}) copy-start(s32[1,8100]{1,0:T(1,128)} %refs_5_.1) | copy-start | bytes 97204
  4.2 9.1 %collective-permute-start = (f32[8,128]{1,0:T(8,128)S(1)}, f32[8,128]{1,0:T(8,128)S(1)}, u32[]{:S(2)}, u32[]{:S(2)}) collective-permute-start(f32[8,128]{1,0:T(8,128)S(1)} %get-tuple-element.26), channel_id=1, source_target_pairs={{0,128},{1,2},{2,1},{3,4},{4,3},{5,6},{6,5},{7,8},{8,7},{9,10},{10... | collective-permute-start | bytes 12296 | tf_op jit(solution)/shard_map/ppermute | solution.py:350
  4.7 8.6 %collective-permute-start.1 = (f32[8,128]{1,0:T(8,128)S(1)}, f32[8,128]{1,0:T(8,128)S(1)}, u32[]{:S(2)}, u32[]{:S(2)}) collective-permute-start(f32[8,128]{1,0:T(8,128)S(1)} %get-tuple-element.27), channel_id=1, source_target_pairs={{0,16},{1,17},{2,18},{3,19},{4,20},{5,21},{6,22},{7,23},{8,24},{9,... | collective-permute-start | bytes 12296 | tf_op jit(solution)/shard_map/ppermute | solution.py:350
  4.7 9.6 %collective-permute-start.2 = (f32[8,128]{1,0:T(8,128)S(1)}, f32[8,128]{1,0:T(8,128)S(1)}, u32[]{:S(2)}, u32[]{:S(2)}) collective-permute-start(f32[8,128]{1,0:T(8,128)S(1)} %get-tuple-element.28), channel_id=1, source_target_pairs={{0,1},{1,0},{2,3},{3,2},{4,5},{5,4},{6,7},{7,6},{8,9},{9,8},{10,11... | collective-permute-start | bytes 12296 | tf_op jit(solution)/shard_map/ppermute | solution.py:350
  12.8 4.2 %collective-permute-start.3 = (f32[8,128]{1,0:T(8,128)S(1)}, f32[8,128]{1,0:T(8,128)S(1)}, u32[]{:S(2)}, u32[]{:S(2)}) collective-permute-start(f32[8,128]{1,0:T(8,128)S(1)} %get-tuple-element.29), channel_id=1, source_target_pairs={{0,240},{1,241},{2,242},{3,243},{4,244},{5,245},{6,246},{7,247},{8... | collective-permute-start | bytes 12296 | tf_op jit(solution)/shard_map/ppermute | solution.py:350
  17.7 5.3 %collective-permute-start.4 = (f32[8,128]{1,0:T(8,128)S(1)}, f32[8,128]{1,0:T(8,128)S(1)}, u32[]{:S(2)}, u32[]{:S(2)}) collective-permute-start(f32[8,128]{1,0:T(8,128)S(1)} %get-tuple-element.33), channel_id=1, source_target_pairs={{0,128},{1,2},{2,1},{3,4},{4,3},{5,6},{6,5},{7,8},{8,7},{9,10},{10... | collective-permute-start | bytes 12296 | tf_op jit(solution)/shard_map/ppermute | solution.py:361
  17.8 5.2 %collective-permute-start.5 = (f32[8,128]{1,0:T(8,128)S(1)}, f32[8,128]{1,0:T(8,128)S(1)}, u32[]{:S(2)}, u32[]{:S(2)}) collective-permute-start(f32[8,128]{1,0:T(8,128)S(1)} %get-tuple-element.34), channel_id=1, source_target_pairs={{0,16},{1,17},{2,18},{3,19},{4,20},{5,21},{6,22},{7,23},{8,24},{9,... | collective-permute-start | bytes 12296 | tf_op jit(solution)/shard_map/ppermute | solution.py:361
  17.9 5.1 %collective-permute-start.6 = (f32[8,128]{1,0:T(8,128)S(1)}, f32[8,128]{1,0:T(8,128)S(1)}, u32[]{:S(2)}, u32[]{:S(2)}) collective-permute-start(f32[8,128]{1,0:T(8,128)S(1)} %get-tuple-element.35), channel_id=1, source_target_pairs={{0,1},{1,0},{2,3},{3,2},{4,5},{5,4},{6,7},{7,6},{8,9},{9,8},{10,11... | collective-permute-start | bytes 12296 | tf_op jit(solution)/shard_map/ppermute | solution.py:361
  21.1 4.2 %collective-permute-start.7 = (f32[8,128]{1,0:T(8,128)S(1)}, f32[8,128]{1,0:T(8,128)S(1)}, u32[]{:S(2)}, u32[]{:S(2)}) collective-permute-start(f32[8,128]{1,0:T(8,128)S(1)} %get-tuple-element.36), channel_id=1, source_target_pairs={{0,240},{1,241},{2,242},{3,243},{4,244},{5,245},{6,246},{7,247},{8... | collective-permute-start | bytes 12296 | tf_op jit(solution)/shard_map/ppermute | solution.py:361

commit v2 on v1

--- a/solution.py
+++ b/solution.py
@@ -23,6 +23,7 @@
 VMEM = pl.BlockSpec(memory_space=pltpu.VMEM)
 SMEM = pl.BlockSpec(memory_space=pltpu.SMEM)
 ANY = pl.BlockSpec(memory_space=pl.ANY)
+HBM = pl.BlockSpec(memory_space=pltpu.HBM)
 
 
 def link_x_even(x, y, nx, ny):
@@ -53,6 +54,18 @@
             to_x, to_y = link(x, y, nx, ny)
             out.append((x * ny + y, to_x * ny + to_y))
     return out
+
+
+FIRST_ORDER = (0, 3, 2, 1)
+SECOND_ORDER = (2, 0, 3, 1)
+
+
+def exchanged(pays, order, nx, ny):
+    return [lax.ppermute(pay, AXES, pairs_of(LINKS[link], nx, ny)) for pay, link in zip(pays, order)]
+
+
+def by_link(refs, order):
+    return [refs[order.index(link)] for link in range(len(LINKS))]
 
 
 def partner(me, which, nx, ny):
@@ -203,14 +216,41 @@
     return out
 
 
-def load_kernel(shape, me_ref, tiles_ref, near_ref, turn_ref, fields_ref, wet_ref,
-                state_ref, lines_ref, own_ref, pay0, pay1, pay2, pay3, route, raw, wet_raw, sems):
+def raw_lines(chunk_of, low_row):
+    lane = lanes()
+    odd = lane & 1
+    line_at = (37 * ((lane + 39 * odd) >> 1)) & 63
+    home = (TILE * line_at + (TILE - 1) * odd) >> 7
+    parts = []
+    for low, high in ((0, HALF), (HALF, CHUNKS)):
+        found = chunk_of(low)
+        for c in range(low + 1, high):
+            found = jnp.where(home == c - low, chunk_of(c), found)
+        parts.append(found)
+    early = lane < 64
+    east_at = (TILE * lane + TILE - 1) & (LANES - 1)
+    west_at = (TILE * lane) & (LANES - 1)
+    east = jnp.where(early, pick(parts[0], east_at), pick(parts[1], east_at))
+    west = jnp.where(early, pick(parts[0], west_at), pick(parts[1], west_at))
+    before = pltpu.roll(chunk_of(CHUNKS - 2), LANES - LAST, 1)
+    after = pltpu.roll(chunk_of(CHUNKS - 1), LANES - LAST, 1)
+    north = jnp.where(lane < LANES - LAST, before, after)
+    return [chunk_of(0), east, north, west]
+
+
+def load_kernel(shape, me_ref, tiles_hbm, near_hbm, turn_hbm, fields_ref, wet_ref,
+                raw, wet_raw, lines_ref, own_ref, pay0, pay1, pay2, pay3, route,
+                tiles_ref, near_ref, turn_ref, sems):
     nx, ny = shape
-    copies = [pltpu.make_async_copy(fields_ref.at[c, 0], raw.at[c], sems.at[c])
-              for c in range(6)]
+    tables = [pltpu.make_async_copy(tiles_hbm, tiles_ref, sems.at[7]),
+              pltpu.make_async_copy(near_hbm, near_ref, sems.at[8]),
+              pltpu.make_async_copy(turn_hbm, turn_ref, sems.at[9])]
+    copies = [pltpu.make_async_copy(fields_ref.at[c, 0], raw.at[c], sems.at[c]) for c in range(6)]
     copies.append(pltpu.make_async_copy(wet_ref.at[0], wet_raw.at[0], sems.at[6]))
-    for copy in copies:
+    for copy in tables + copies:
         copy.start()
+    for copy in tables:
+        copy.wait()
     me = me_ref[0]
     tile = tiles_ref[me]
     live = tile >= 0
@@ -230,21 +270,33 @@
     route[40] = jnp.where(live, 1, 0)
     for copy in copies:
         copy.wait()
+
+    def chunk(ref, c):
+        if c < CHUNKS - 1:
+            return ref[:, c * LANES:(c + 1) * LANES]
+        rest = CELLS - c * LANES
+        part = ref[:, c * LANES:CELLS]
+        return jnp.concatenate([part, jnp.zeros((8, LANES - rest), part.dtype)], axis=1)
+
+    values = raw_lines(lambda c: chunk(raw, c), 0)
+    wets = raw_lines(lambda c: chunk(wet_raw, c), 0)
+    row = rows()
+    lines = []
+    for value, wet in zip(values, wets):
+        wet = jnp.broadcast_to(wet[0:1], (8, LANES)).astype(jnp.float32)
+        lines.append(jnp.where(row < 6, value * wet, jnp.where(row == 6, wet, 0.0)))
+    for side in range(4):
+        lines_ref[8 * side:8 * side + 8, :] = lines[side]
+    outgoing(lines, route, by_link((pay0, pay1, pay2, pay3), FIRST_ORDER), own_ref, True)
+
+
+def inner_kernel(raw, wet_raw, state_ref, base_ref, base_lines_ref):
     state_ref[:, (CHUNKS - 1) * LANES:] = jnp.zeros((8, LANES), jnp.float32)
     for low, high in ((0, (CHUNKS - 1) * LANES), ((CHUNKS - 1) * LANES, CELLS)):
         size = (8, high - low)
         row = lax.broadcasted_iota(jnp.int32, size, 0)
         wet = jnp.broadcast_to(wet_raw[0:1, low:high].astype(jnp.float32), size)
         state_ref[:, low:high] = jnp.where(row < 6, raw[:, low:high] * wet, jnp.where(row == 6, wet, 0.0))
-    state = state_ref[...]
-    cell, column = column_of()
-    lines = edge_lines(state, column)
-    for side in range(4):
-        lines_ref[8 * side:8 * side + 8, :] = lines[side]
-    outgoing(lines, route, (pay0, pay1, pay2, pay3), own_ref, True)
-
-
-def inner_kernel(state_ref, base_ref, base_lines_ref):
     state = state_ref[...]
     right, left, up, down, cell, column = neighbours(state)
     first, second, wet = repeated(state, 0), repeated(state, 2), wet_rows(state)
@@ -264,7 +316,7 @@
 
 def edge_kernel(route, lines_ref, own_ref, base_lines_ref, came0, came1, came2, came3,
                 patch_ref, own_two_ref, pay0, pay1, pay2, pay3):
-    rims = rims_of(route, own_ref, (came0, came1, came2, came3))
+    rims = rims_of(route, own_ref, by_link((came0, came1, came2, came3), FIRST_ORDER))
     patch = []
     for side in range(4):
         line = lines_ref[8 * side:8 * side + 8, :]
@@ -286,7 +338,7 @@
         tracer = base_lines_ref[8 * side:8 * side + 8, :] + whole[side]
         row = row_of(tracer)
         press.append(GRAVITY * jnp.where(row == 5, tracer + pltpu.roll(tracer, 1, 0), tracer))
-    outgoing(press, route, (pay0, pay1, pay2, pay3), own_two_ref, False)
+    outgoing(press, route, by_link((pay0, pay1, pay2, pay3), SECOND_ORDER), own_two_ref, False)
 
 
 def middle_kernel(route, state_ref, base_ref, patch_ref, out_ref):
@@ -305,7 +357,7 @@
 
 
 def last_kernel(route, lines_ref, own_ref, almost_ref, came0, came1, came2, came3, out_ref, full, sems):
-    rims = rims_of(route, own_ref, (came0, came1, came2, came3))
+    rims = rims_of(route, own_ref, by_link((came0, came1, came2, came3), SECOND_ORDER))
     patch = []
     for side in range(4):
         wet = wet_rows(lines_ref[8 * side:8 * side + 8, :])
@@ -337,28 +389,28 @@
     line = sds(8, LANES)
     wide = sds(8, WIDE)
     four = sds(32, LANES)
-    state, lines, own, *pays, route = pl.pallas_call(
+    raw, wet_raw, lines, own, *pays, route = pl.pallas_call(
         lambda *refs: load_kernel((nx, ny), *refs),
-        out_shape=[wide, four, four, line, line, line, line, sds(ROUTE, dtype=jnp.int32)],
-        in_specs=[SMEM, SMEM, SMEM, SMEM, ANY, ANY],
-        out_specs=[VMEM] * 7 + [SMEM],
-        scratch_shapes=[pltpu.VMEM((8, CELLS), jnp.float32), pltpu.VMEM((8, CELLS), jnp.int32),
-                        pltpu.SemaphoreType.DMA((7,))],
+        out_shape=[sds(8, CELLS), sds(8, CELLS, dtype=jnp.int32), four, four, line, line, line, line,
+                   sds(ROUTE, dtype=jnp.int32)],
+        in_specs=[SMEM] + [HBM] * 5,
+        out_specs=[VMEM] * 8 + [SMEM],
+        scratch_shapes=[pltpu.SMEM((nx * ny,), jnp.int32), pltpu.SMEM((4, nx * ny), jnp.int32),
+                        pltpu.SMEM((4, nx * ny), jnp.int32), pltpu.SemaphoreType.DMA((10,))],
         compiler_params=PARAMS, name="load",
-    )(me, tile_of_slot, neighbor.T, rotation.T, fields.reshape(6, 1, CELLS), wet_mask)
-    pairs = [pairs_of(link, nx, ny) for link in LINKS]
-    came = [lax.ppermute(pay, AXES, pair) for pay, pair in zip(pays, pairs)]
-    base, base_lines = pl.pallas_call(
-        inner_kernel, out_shape=[wide, four], in_specs=[VMEM], out_specs=[VMEM] * 2,
+    )(me, *(pltpu.with_memory_space_constraint(v, pltpu.HBM) for v in (tile_of_slot, neighbor.T, rotation.T, fields.reshape(6, 1, CELLS), wet_mask)))
+    came = exchanged(pays, FIRST_ORDER, nx, ny)
+    state, base, base_lines = pl.pallas_call(
+        inner_kernel, out_shape=[wide, wide, four], in_specs=[VMEM] * 2, out_specs=[VMEM] * 3,
         compiler_params=PARAMS, name="inner",
         cost_estimate=pl.CostEstimate(flops=2000000, bytes_accessed=600000, transcendentals=0),
-    )(state)
+    )(raw, wet_raw)
     patch, own_two, *pays = pl.pallas_call(
         edge_kernel, out_shape=[four, four, line, line, line, line],
         in_specs=[SMEM] + [VMEM] * 7, out_specs=[VMEM] * 6,
         compiler_params=PARAMS, name="edge",
     )(route, lines, own, base_lines, *came)
-    came = [lax.ppermute(pay, AXES, pair) for pay, pair in zip(pays, pairs)]
+    came = exchanged(pays, SECOND_ORDER, nx, ny)
     almost = pl.pallas_call(
         middle_kernel, out_shape=wide, in_specs=[SMEM] + [VMEM] * 3, out_specs=VMEM,
         compiler_params=PARAMS, name="middle",

time: 26.9 us -> 23.2 us (0.86)
  the two profiles are of different devices: /device:TPU:22 before, /device:TPU:30 now
where the time goes in v2:
time: 23.2 us; the launch traced here: 23 us
  starting transfers between devices  13 us (56%)
  Pallas kernels  5.3 us (23%)
  waiting for transfers between devices  4.68 us (20%)
    ppermute x8, starting transfers between devices, exchanged(): lax.ppermute(pay, AXES, pairs_of(LINKS[link], nx, ny))  13 us
    ppermute x8, waiting for transfers between devices, exchanged(): lax.ppermute(pay, AXES, pairs_of(LINKS[link], nx, ny))  4.68 us
    pallas_call x1, Pallas kernels, on_device(): pl.pallas_call(lambda *refs: load_kernel((nx, ny), *refs), out_shape=[sds...  1.62 us
    pallas_call x1, Pallas kernels, on_device(): pl.pallas_call(last_kernel, out_shape=sds(6, 1, CELLS), in_specs=[SMEM] +...  1.41 us
    pallas_call x1, Pallas kernels, on_device(): pl.pallas_call(middle_kernel, out_shape=wide, in_specs=[SMEM] + [VMEM] *...  1.06 us
    pallas_call x1, Pallas kernels, on_device(): pl.pallas_call(edge_kernel, out_shape=[four, four, line, line, line, line...  0.71 us
    pallas_call x1, Pallas kernels, on_device(): pl.pallas_call(inner_kernel, out_shape=[wide, wide, four], in_specs=[VMEM...  0.5 us
  transfers between devices with their start and end apart: 8, of which 2 were waited for; matrix products, arithmetic and copies ran while one was open for 0% of the time, Pallas kernels for 7%

profile of v2, /device:TPU:30, one launch (start us, length us, event | category | flops | bytes accessed | tf_op | source)
XLA Modules:
  0.0 23.0 jit_solution(14591822365672971988)
XLA Ops:
  0.0 1.6 %load.1 = (f32[8,8100]{1,0:T(8,128)S(1)}, s32[8,8100]{1,0:T(8,128)S(1)}, f32[32,128]{1,0:T(8,128)S(1)}, f32[32,128]{1,0:T(8,128)S(1)}, f32[8,128]{1,0:T(8,128)S(...) custom-call(s32[1]{0:T(128)} %bitcast.refs_0_, s32[256]{0:T(256)} %refs_1_.1, ...), custom_call_target="tpu_custom_call" | custom-call | tf_op jit(solution)/shard_map/load/pallas_call | solution.py:392
  1.6 7.3 %collective-permute-start = (f32[8,128]{1,0:T(8,128)S(1)}, f32[8,128]{1,0:T(8,128)S(1)}, u32[]{:S(2)}, u32[]{:S(2)}) collective-permute-start(f32[8,128]{1,0:T(8,128)S(1)} %get-tuple-element.29), channel_id=1, source_target_pairs={{0,128},{1,2},{2,1},{3,4},{4,3},{5,6},{6,5},{7,8},{8,7},{9,10},{10... | collective-permute-start | bytes 12296 | tf_op jit(solution)/shard_map/ppermute | solution.py:64
  8.9 0.0 collective-permute-start.1
  8.9 0.0 collective-permute-start.2
  8.9 1.1 %collective-permute-start.3 = (f32[8,128]{1,0:T(8,128)S(1)}, f32[8,128]{1,0:T(8,128)S(1)}, u32[]{:S(2)}, u32[]{:S(2)}) collective-permute-start(f32[8,128]{1,0:T(8,128)S(1)} %get-tuple-element.32), channel_id=1, source_target_pairs={{0,16},{1,17},{2,18},{3,19},{4,20},{5,21},{6,22},{7,23},{8,24},{9,... | collective-permute-start | bytes 12296 | tf_op jit(solution)/shard_map/ppermute | solution.py:64
  10.0 0.5 %inner.1 = (f32[8,8192]{1,0:T(8,128)S(1)}, f32[8,8192]{1,0:T(8,128)S(1)}, f32[32,128]{1,0:T(8,128)S(1)}) custom-call(f32[8,8100]{1,0:T(8,128)S(1)} %get-tuple-element.26.raw, s32[8,8100]{1,0:T(8,128)S(1)} %get-tuple-element.27.wet_raw), custom_call_target="tpu_custom_call" | custom-call | flops 2000000 | bytes 600000 | tf_op jit(solution)/shard_map/inner/pallas_call | solution.py:403
  10.5 0.0 collective-permute-done.came0
  10.5 2.6 %collective-permute-done.1.came1 = f32[8,128]{1,0:T(8,128)S(1)} collective-permute-done((f32[8,128]{1,0:T(8,128)S(1)}, f32[8,128]{1,0:T(8,128)S(1)}, u32[]{:S(2)}, u32[]{:S(2)}) %collective-permute-start.1) | collective-permute-done | bytes 4128 | tf_op jit(solution)/shard_map/ppermute | solution.py:64
  13.2 0.0 collective-permute-done.2.came2
  13.2 0.0 collective-permute-done.3.came3
  13.2 0.7 %edge.1 = (f32[32,128]{1,0:T(8,128)S(1)}, f32[32,128]{1,0:T(8,128)S(1)}, f32[8,128]{1,0:T(8,128)S(1)}, f32[8,128]{1,0:T(8,128)S(1)}, f32[8,128]{1,0:T(8,128)S(1)}, /*index=5*/f32[8,128]{1,0:T(8,128)S(1)}) custom-call(s32[48]{0:T(128)S(1)} %get-tuple-element.23.route, f32[32,128]{1,0:T(8,128)S(1)} %get-tuple-element.24.lines_ref, ...), custom_call_target="tpu_custom_call" | custom-call | tf_op jit(solution)/shard_map/edge/pallas_call | solution.py:408
  13.9 0.1 collective-permute-start.4
  14.0 3.4 %collective-permute-start.5 = (f32[8,128]{1,0:T(8,128)S(1)}, f32[8,128]{1,0:T(8,128)S(1)}, u32[]{:S(2)}, u32[]{:S(2)}) collective-permute-start(f32[8,128]{1,0:T(8,128)S(1)} %get-tuple-element.38), channel_id=1, source_target_pairs={{0,128},{1,2},{2,1},{3,4},{4,3},{5,6},{6,5},{7,8},{8,7},{9,10},{10... | collective-permute-start | bytes 12296 | tf_op jit(solution)/shard_map/ppermute | solution.py:64
  17.3 0.2 collective-permute-start.6
  17.5 0.9 %collective-permute-start.7 = (f32[8,128]{1,0:T(8,128)S(1)}, f32[8,128]{1,0:T(8,128)S(1)}, u32[]{:S(2)}, u32[]{:S(2)}) collective-permute-start(f32[8,128]{1,0:T(8,128)S(1)} %get-tuple-element.40), channel_id=1, source_target_pairs={{0,16},{1,17},{2,18},{3,19},{4,20},{5,21},{6,22},{7,23},{8,24},{9,... | collective-permute-start | bytes 12296 | tf_op jit(solution)/shard_map/ppermute | solution.py:64
  18.5 1.1 %middle.1.almost_ref = f32[8,8192]{1,0:T(8,128)S(1)} custom-call(s32[48]{0:T(128)S(1)} %get-tuple-element.23.route, f32[8,8192]{1,0:T(8,128)S(1)} %get-tuple-element.34.state_ref, f32[8,8192]{1,0:T(8,128)S(1)} %get-tuple-element.35.base_ref, f32[32,128]{1,0:T(8,128)S(1)} %get-tuple-element.36.patch_ref), custom_call_target="tpu_custom_call" | custom-call | flops 2000000 | bytes 800000 | tf_op jit(solution)/shard_map/middle/pallas_call | solution.py:414
  19.5 0.0 collective-permute-done.4.came0
  19.5 2.1 %collective-permute-done.5.came1 = f32[8,128]{1,0:T(8,128)S(1)} collective-permute-done((f32[8,128]{1,0:T(8,128)S(1)}, f32[8,128]{1,0:T(8,128)S(1)}, u32[]{:S(2)}, u32[]{:S(2)}) %collective-permute-start.5) | collective-permute-done | bytes 4128 | tf_op jit(solution)/shard_map/ppermute | solution.py:64
  21.6 0.0 collective-permute-done.6.came2
  21.6 0.0 collective-permute-done.7.came3
  21.6 1.4 %last.1 = f32[6,1,8100]{2,1,0:T(1,128)} custom-call(s32[48]{0:T(128)S(1)} %get-tuple-element.23.route, f32[32,128]{1,0:T(8,128)S(1)} %get-tuple-element.24.lines_ref, f32[32,128]{1,0:T(8,128)S(1)} %get-tuple-element.33.own_ref, f32[8,8192]{1,0:T(8,128)S(1)} %middle.1.almost_ref, f32[8,128]{1,0:T(8,128)S(1)} %collective-permute-done.4.came0, ...), custom_call_target="tpu_custom_call" | custom-call | tf_op jit(solution)/shard_map/last/pallas_call | solution.py:419
Async XLA Ops:
  1.6 8.9 %collective-permute-start = (f32[8,128]{1,0:T(8,128)S(1)}, f32[8,128]{1,0:T(8,128)S(1)}, u32[]{:S(2)}, u32[]{:S(2)}) collective-permute-start(f32[8,128]{1,0:T(8,128)S(1)} %get-tuple-element.29), channel_id=1, source_target_pairs={{0,128},{1,2},{2,1},{3,4},{4,3},{5,6},{6,5},{7,8},{8,7},{9,10},{10... | collective-permute-start | bytes 12296 | tf_op jit(solution)/shard_map/ppermute | solution.py:64
  8.9 4.2 %collective-permute-start.1 = (f32[8,128]{1,0:T(8,128)S(1)}, f32[8,128]{1,0:T(8,128)S(1)}, u32[]{:S(2)}, u32[]{:S(2)}) collective-permute-start(f32[8,128]{1,0:T(8,128)S(1)} %get-tuple-element.30), channel_id=1, source_target_pairs={{0,240},{1,241},{2,242},{3,243},{4,244},{5,245},{6,246},{7,247},{8... | collective-permute-start | bytes 12296 | tf_op jit(solution)/shard_map/ppermute | solution.py:64
  8.9 4.2 %collective-permute-start.2 = (f32[8,128]{1,0:T(8,128)S(1)}, f32[8,128]{1,0:T(8,128)S(1)}, u32[]{:S(2)}, u32[]{:S(2)}) collective-permute-start(f32[8,128]{1,0:T(8,128)S(1)} %get-tuple-element.31), channel_id=1, source_target_pairs={{0,1},{1,0},{2,3},{3,2},{4,5},{5,4},{6,7},{7,6},{8,9},{9,8},{10,11... | collective-permute-start | bytes 12296 | tf_op jit(solution)/shard_map/ppermute | solution.py:64
  8.9 4.2 %collective-permute-start.3 = (f32[8,128]{1,0:T(8,128)S(1)}, f32[8,128]{1,0:T(8,128)S(1)}, u32[]{:S(2)}, u32[]{:S(2)}) collective-permute-start(f32[8,128]{1,0:T(8,128)S(1)} %get-tuple-element.32), channel_id=1, source_target_pairs={{0,16},{1,17},{2,18},{3,19},{4,20},{5,21},{6,22},{7,23},{8,24},{9,... | collective-permute-start | bytes 12296 | tf_op jit(solution)/shard_map/ppermute | solution.py:64
  13.9 5.7 %collective-permute-start.4 = (f32[8,128]{1,0:T(8,128)S(1)}, f32[8,128]{1,0:T(8,128)S(1)}, u32[]{:S(2)}, u32[]{:S(2)}) collective-permute-start(f32[8,128]{1,0:T(8,128)S(1)} %get-tuple-element.37), channel_id=1, source_target_pairs={{0,1},{1,0},{2,3},{3,2},{4,5},{5,4},{6,7},{7,6},{8,9},{9,8},{10,11... | collective-permute-start | bytes 12296 | tf_op jit(solution)/shard_map/ppermute | solution.py:64
  14.0 7.6 %collective-permute-start.5 = (f32[8,128]{1,0:T(8,128)S(1)}, f32[8,128]{1,0:T(8,128)S(1)}, u32[]{:S(2)}, u32[]{:S(2)}) collective-permute-start(f32[8,128]{1,0:T(8,128)S(1)} %get-tuple-element.38), channel_id=1, source_target_pairs={{0,128},{1,2},{2,1},{3,4},{4,3},{5,6},{6,5},{7,8},{8,7},{9,10},{10... | collective-permute-start | bytes 12296 | tf_op jit(solution)/shard_map/ppermute | solution.py:64
  17.3 4.3 %collective-permute-start.6 = (f32[8,128]{1,0:T(8,128)S(1)}, f32[8,128]{1,0:T(8,128)S(1)}, u32[]{:S(2)}, u32[]{:S(2)}) collective-permute-start(f32[8,128]{1,0:T(8,128)S(1)} %get-tuple-element.39), channel_id=1, source_target_pairs={{0,240},{1,241},{2,242},{3,243},{4,244},{5,245},{6,246},{7,247},{8... | collective-permute-start | bytes 12296 | tf_op jit(solution)/shard_map/ppermute | solution.py:64
  17.5 4.1 %collective-permute-start.7 = (f32[8,128]{1,0:T(8,128)S(1)}, f32[8,128]{1,0:T(8,128)S(1)}, u32[]{:S(2)}, u32[]{:S(2)}) collective-permute-start(f32[8,128]{1,0:T(8,128)S(1)} %get-tuple-element.40), channel_id=1, source_target_pairs={{0,16},{1,17},{2,18},{3,19},{4,20},{5,21},{6,22},{7,23},{8,24},{9,... | collective-permute-start | bytes 12296 | tf_op jit(solution)/shard_map/ppermute | solution.py:64

commit v3 on v2

v3 whole, which is shorter than its diff:
```python
import jax
import jax.numpy as jnp
from jax import lax
from jax.experimental import pallas as pl
from jax.experimental.pallas import tpu as pltpu
from jax.sharding import PartitionSpec as P

TILE = 90
CELLS = TILE * TILE
LANES = 128
CHUNKS = 64
WIDE = LANES * CHUNKS
HALF = 45
LAST = CELLS - TILE - (CHUNKS - 2) * LANES

ADVECT = 0.25
DIFFUSE = 0.15
STEP_SIZE = 0.5
CORIOLIS = 0.3
GRAVITY = 0.8

AXES = ("gx", "gy")
VMEM = pl.BlockSpec(memory_space=pltpu.VMEM)
SMEM = pl.BlockSpec(memory_space=pltpu.SMEM)
ANY = pl.BlockSpec(memory_space=pl.ANY)
HBM = pl.BlockSpec(memory_space=pltpu.HBM)


def link_x_even(x, y, nx, ny):
    return x ^ 1, y


def link_x_odd(x, y, nx, ny):
    return (((x + nx - 1) % nx ^ 1) + 1) % nx, y


def link_y_even(x, y, nx, ny):
    return x, y ^ 1


def link_y_odd(x, y, nx, ny):
    if y == 0 or y == ny - 1:
        return (x + nx // 2) % nx, y
    return x, ((y - 1) ^ 1) + 1


LINKS = (link_y_odd, link_x_even, link_y_even, link_x_odd)


def pairs_of(link, nx, ny):
    out = []
    for x in range(nx):
        for y in range(ny):
            to_x, to_y = link(x, y, nx, ny)
            out.append((x * ny + y, to_x * ny + to_y))
    return out


X_ORDER = (3, 1)
U_ORDER = (0, 2)
BOTH = X_ORDER + U_ORDER
SECOND_ORDER = (2, 0, 3, 1)


def exchanged(pays, order, nx, ny):
    return [lax.ppermute(pay, AXES, pairs_of(LINKS[link], nx, ny)) for pay, link in zip(pays, order)]


def by_link(refs, order, links=(0, 1, 2, 3)):
    return [refs[order.index(link)] for link in links]


def partner(me, which, nx, ny):
    x, y = me // ny, me % ny
    if which == 0:
        pole = (y == 0) | (y == ny - 1)
        step = jnp.where(y % 2 == 1, 1, -1)
        return jnp.where(pole, (x + nx // 2) % nx * ny + y, me + step)
    if which == 1:
        return me + jnp.where(x % 2 == 0, ny, -ny)
    if which == 2:
        return me + jnp.where(y % 2 == 0, 1, -1)
    return (x + jnp.where(x % 2 == 1, 1, nx - 1)) % nx * ny + y


def lanes():
    return lax.broadcasted_iota(jnp.int32, (8, LANES), 1)


def rows():
    return lax.broadcasted_iota(jnp.int32, (8, LANES), 0)


def pick(values, index):
    return jnp.take_along_axis(values, index, axis=1)


def tiled(values, count):
    return jnp.concatenate([values] * count, axis=1)


def column_of():
    cell = lax.broadcasted_iota(jnp.int32, (8, WIDE), 1)
    line = jnp.floor((cell.astype(jnp.float32) + 0.5) * (1.0 / TILE)).astype(jnp.int32)
    return cell, cell - TILE * line


def edge_lines(state, column):
    lane = lanes()
    edge = (column == 0) | (column == TILE - 1)
    parts = []
    for low, high in ((0, HALF), (HALF, CHUNKS)):
        found = jnp.zeros((8, LANES), jnp.float32)
        for c in range(low, high):
            cut = slice(c * LANES, (c + 1) * LANES)
            found = jnp.where(edge[:, cut], state[:, cut], found)
        parts.append(found)
    east_at = (TILE * lane + TILE - 1) & (LANES - 1)
    west_at = (TILE * lane) & (LANES - 1)
    east = jnp.where(lane < 64, pick(parts[0], east_at), pick(parts[1], east_at))
    west = jnp.where(lane < 64, pick(parts[0], west_at), pick(parts[1], west_at))
    south = state[:, :LANES]
    before = pltpu.roll(state[:, (CHUNKS - 2) * LANES:(CHUNKS - 1) * LANES], LANES - LAST, 1)
    after = pltpu.roll(state[:, (CHUNKS - 1) * LANES:], LANES - LAST, 1)
    north = jnp.where(lane < LANES - LAST, before, after)
    return [south, east, north, west]


def spread(lines, cell, column):
    south, east, north, west = lines
    lane = lanes()
    odd = (lane & 1) == 1
    line_at = (37 * ((lane + jnp.where(odd, 39, 0)) >> 1)) & 63
    early = jnp.where(odd, pick(east, line_at), pick(west, line_at))
    late = jnp.where(odd, pick(east, line_at + 64), pick(west, line_at + 64))
    sides = jnp.concatenate([early] * HALF + [late] * (CHUNKS - HALF), axis=1)
    edge = (column == 0) | (column == TILE - 1)
    out = jnp.where(edge, sides, 0.0)
    first = jnp.where(lane < TILE, south, 0.0) + out[:, :LANES]
    moved = pltpu.roll(north, LAST, 1)
    before = out[:, (CHUNKS - 2) * LANES:(CHUNKS - 1) * LANES] + jnp.where(lane >= LAST, moved, 0.0)
    after = out[:, (CHUNKS - 1) * LANES:] + jnp.where(lane < LAST + TILE - LANES, moved, 0.0)
    return jnp.concatenate([first, out[:, LANES:(CHUNKS - 2) * LANES], before, after], axis=1)


def neighbours(state):
    cell, column = column_of()
    right = jnp.where(column == TILE - 1, 0.0, pltpu.roll(state, WIDE - 1, 1))
    left = jnp.where(column == 0, 0.0, pltpu.roll(state, 1, 1))
    up = jnp.where(cell >= CELLS - TILE, 0.0, pltpu.roll(state, WIDE - TILE, 1))
    down = jnp.where(cell < TILE, 0.0, pltpu.roll(state, TILE, 1))
    return right, left, up, down, cell, column


def row_of(values):
    return lax.broadcasted_iota(jnp.int32, values.shape, 0)


def repeated(values, first):
    row = row_of(values)
    if first == 0:
        pair = jnp.where(row < 2, values, pltpu.roll(values, 2, 0))
    else:
        pair = jnp.where(row < 4, values, pltpu.roll(values, 2, 0))
        pair = jnp.where(row < 2, pltpu.roll(values, 6, 0), pair)
        return pair
    return jnp.where(row < 4, pair, pltpu.roll(values, 4, 0))


def wet_rows(values):
    return jnp.broadcast_to(values[6:7], values.shape)


def turned(line, turns):
    row = row_of(line)
    swapped = jnp.where(row < 2, pltpu.roll(line, 6, 0), pltpu.roll(line, 2, 0))
    velocity = row < 4
    second = jnp.where(row < 2, swapped, -swapped)
    odd = jnp.where(turns % 2 == 1, 1, 0)
    out = jnp.where(jnp.logical_and(velocity, odd == 1), second, line)
    back = jnp.where(turns >= 2, 1, 0)
    return jnp.where(jnp.logical_and(velocity, back == 1), -out, out)


def flipped(line):
    return pick(line, jnp.maximum(TILE - 1 - lanes(), 0))


ROUTE = 48
OWN_AT, RELAY_AT = TILE, {1: TILE + 4, 3: TILE + 8}


class Rows:
    def __init__(self, ref):
        self.ref = ref

    def __getitem__(self, i):
        return jnp.broadcast_to(self.ref[i:i + 1, :], (8, LANES))


def my_index(ny):
    return lax.axis_index("gx") * ny + lax.axis_index("gy")


def sent_line(line, side, route, vector):
    line = jnp.where(route[32 + side] == 1, flipped(line), line)
    return turned(line, route[36 + side]) if vector else line


def chosen(lines, route, link):
    total = jnp.zeros((8, LANES), jnp.float32)
    for side in range(4):
        total = jnp.where(route[4 * link + side] == 1, lines[side], total)
    return total


def own_rims(sent, route):
    out = []
    for target in range(4):
        total = jnp.zeros((8, LANES), jnp.float32)
        for side in range(4):
            total = jnp.where(route[16 + 4 * side + target] == 1, sent[side], total)
        out.append(total)
    return out


def rims_of(route, base, came):
    out = []
    for side in range(4):
        rim = base[side] if base is not None else jnp.zeros((8, LANES), jnp.float32)
        for link in range(4):
            rim = jnp.where(route[4 * link + side] == 1, came[link], rim)
        out.append(rim)
    return out


def four_of(ref):
    return [ref[8 * side:8 * side + 8, :] for side in range(4)]


def columns_at(step):
    lane = lanes()
    odd = lane & 1
    shift = jnp.where(odd == 1, 39 + step, -step) if step % 2 == 0 else jnp.where(odd == 1, -step, 39 + step)
    column = jnp.where(odd == 1, TILE - 1 - step, step) if step % 2 == 0 else jnp.where(odd == 1, step, TILE - 1 - step)
    line_at = (37 * ((lane + shift) >> 1)) & 63
    return line_at, (TILE * line_at + column) >> 7


def raw_lines(chunk_of, step):
    lane = lanes()
    _, home = columns_at(step)
    parts = []
    for low, high in ((0, HALF), (HALF, CHUNKS)):
        found = chunk_of(low)
        for c in range(low + 1, high):
            found = jnp.where(home == c - low, chunk_of(c), found)
        parts.append(found)
    early = lane < 64
    out = [None] * 4
    for side, column in ((1, TILE - 1 - step), (3, step)):
        at = (TILE * lane + column) & (LANES - 1)
        out[side] = jnp.where(early, pick(parts[0], at), pick(parts[1], at))
    for side, first in ((0, TILE * step), (2, CELLS - TILE - TILE * step)):
        low, start = first // LANES, first % LANES
        if start == 0:
            out[side] = chunk_of(low)
        else:
            before = pltpu.roll(chunk_of(low), LANES - start, 1)
            after = pltpu.roll(chunk_of(low + 1), LANES - start, 1)
            out[side] = jnp.where(lane < LANES - start, before, after)
    return out


def spread_chunks(lines, step):
    lane = lanes()
    line_at, home = columns_at(step)
    odd = (lane & 1) == 1
    first_odd, first_even = (lines[1], lines[3]) if step % 2 == 0 else (lines[3], lines[1])
    early = jnp.where(odd, pick(first_odd, line_at), pick(first_even, line_at))
    late = jnp.where(odd, pick(first_odd, line_at + 64), pick(first_even, line_at + 64))
    out = []
    for c in range(CHUNKS):
        out.append(jnp.where(home == (c if c < HALF else c - HALF), early if c < HALF else late, 0.0))
    for side, first in ((0, TILE * step), (2, CELLS - TILE - TILE * step)):
        low, start = first // LANES, first % LANES
        line = jnp.where(lane < TILE, lines[side], 0.0)
        if start == 0:
            out[low] = out[low] + line
        else:
            moved = pltpu.roll(line, start, 1)
            out[low] = out[low] + jnp.where(lane >= start, moved, 0.0)
            if start + TILE > LANES:
                out[low + 1] = out[low + 1] + jnp.where(lane < start + TILE - LANES, moved, 0.0)
    return out


def load_kernel(shape, tiles_hbm, near_hbm, turn_hbm, fields_ref, wet_ref,
                raw, wet_raw, lines_ref, inner_ref, pay0, pay1, pay2, pay3, route_ref,
                tiles_ref, near_ref, turn_ref, sems):
    nx, ny = shape
    tables = [pltpu.make_async_copy(tiles_hbm, tiles_ref, sems.at[7]),
              pltpu.make_async_copy(near_hbm, near_ref, sems.at[8]),
              pltpu.make_async_copy(turn_hbm, turn_ref, sems.at[9])]
    copies = [pltpu.make_async_copy(fields_ref.at[c, 0], raw.at[c], sems.at[c]) for c in range(6)]
    copies.append(pltpu.make_async_copy(wet_ref.at[0], wet_raw.at[0], sems.at[6]))
    for copy in tables + copies:
        copy.start()
    for copy in tables:
        copy.wait()
    me = my_index(ny)
    route = [None] * ROUTE
    tile = tiles_ref[me]
    live = tile >= 0
    held = jnp.maximum(tile, 0)
    near = [jnp.where(live, near_ref[side, held], -1) for side in range(4)]
    turn = [turn_ref[side, held] for side in range(4)]
    for link in range(4):
        other = tiles_ref[partner(me, link, nx, ny)]
        for side in range(4):
            route[4 * link + side] = jnp.where((near[side] >= 0) & (near[side] == other), 1, 0)
    for side in range(4):
        target = (side + 2 + turn[side]) % 4
        for k in range(4):
            route[16 + 4 * side + k] = jnp.where((near[side] >= 0) & (near[side] == tile) & (target == k), 1, 0)
        route[32 + side] = jnp.where((target < 2) != (side >= 2), 1, 0)
        route[36 + side] = (4 - turn[side]) % 4
    route[40] = jnp.where(live, 1, 0)
    for i in range(41):
        route_ref[i:i + 1, :] = jnp.full((1, LANES), route[i], jnp.int32)
    for copy in copies:
        copy.wait()

    def chunk(ref, c):
        if c < CHUNKS - 1:
            return ref[:, c * LANES:(c + 1) * LANES]
        rest = CELLS - c * LANES
        part = ref[:, c * LANES:CELLS]
        return jnp.concatenate([part, jnp.zeros((8, LANES - rest), part.dtype)], axis=1)

    row, lane = rows(), lanes()
    both = []
    for step, ref in ((0, lines_ref), (1, inner_ref)):
        lines = []
        for value, wet in zip(raw_lines(lambda c: chunk(raw, c), step), raw_lines(lambda c: chunk(wet_raw, c), step)):
            wet = jnp.broadcast_to(wet[0:1], (8, LANES)).astype(jnp.float32)
            lines.append(jnp.where(row < 6, value * wet, jnp.where(row == 6, wet, 0.0)))
        for side in range(4):
            ref[8 * side:8 * side + 8, :] = lines[side]
        both.append(lines)
    ends = [jnp.where((lane == OWN_AT + 1) | (lane == OWN_AT + 2), TILE - 1, 0)] * 2
    corners = jnp.where(lane < OWN_AT + 2, pick(both[0][0], ends[0]), pick(both[0][2], ends[1]))
    at_corners = (lane >= OWN_AT) & (lane < OWN_AT + 4)
    sent = [sent_line(both[0][side], side, route, True) for side in range(4)]
    sent_inner = [sent_line(both[1][side], side, route, False) for side in range(4)]
    for link, pay in zip(BOTH, (pay0, pay1, pay2, pay3)):
        pay[0:8, :] = jnp.where(at_corners, corners, chosen(sent, route, link))
        pay[8:16, :] = chosen(sent_inner, route, link)


def pressure_of(tracer, row):
    return GRAVITY * jnp.where(row == 5, tracer + pltpu.roll(tracer, 1, 0), tracer)


def force_of(state, base, row):
    right, left, up, down, cell, column = neighbours(pressure_of(base, row))
    slope = jnp.where(row < 2, pltpu.roll(right - left, 4, 0), pltpu.roll(up - down, 6, 0))
    swapped = jnp.where(row < 2, pltpu.roll(state, 6, 0), -pltpu.roll(state, 2, 0))
    force = STEP_SIZE * (CORIOLIS * swapped - 0.5 * slope)
    return jnp.where(row < 4, wet_rows(state) * force, 0.0)


def masked_state(raw, wet_raw, state_ref):
    state_ref[:, (CHUNKS - 1) * LANES:] = jnp.zeros((8, LANES), jnp.float32)
    for low, high in ((0, (CHUNKS - 1) * LANES), ((CHUNKS - 1) * LANES, CELLS)):
        size = (8, high - low)
        row = lax.broadcasted_iota(jnp.int32, size, 0)
        wet = jnp.broadcast_to(wet_raw[0:1, low:high].astype(jnp.float32), size)
        state_ref[:, low:high] = jnp.where(row < 6, raw[:, low:high] * wet, jnp.where(row == 6, wet, 0.0))
    return state_ref[...]


def without_rims(state):
    right, left, up, down, cell, column = neighbours(state)
    first, second, wet = repeated(state, 0), repeated(state, 2), wet_rows(state)
    along = first * (right - left) + second * (up - down)
    round_sum = right + left + up + down - 4.0 * state
    return wet * (state - (0.5 * ADVECT) * along + DIFFUSE * round_sum), column


def if_live(route_ref, values):
    return jnp.where(tiled(Rows(route_ref)[40], CHUNKS) == 1, values, 0.0)


def base_kernel(raw, wet_raw, state_ref, base_ref, base_lines_ref):
    state = masked_state(raw, wet_raw, state_ref)
    base, column = without_rims(state)
    base_ref[...] = base
    lines = edge_lines(base, column)
    for side in range(4):
        base_lines_ref[8 * side:8 * side + 8, :] = lines[side]


def check_kernel(shape, tiles_hbm, near_hbm, flag, tiles_ref, near_ref, sems):
    nx, ny = shape
    copies = [pltpu.make_async_copy(tiles_hbm, tiles_ref, sems.at[0]),
              pltpu.make_async_copy(near_hbm, near_ref.at[0:4], sems.at[1])]
    for copy in copies:
        copy.start()
    for copy in copies:
        copy.wait()
    row, lane = rows(), lanes()
    tiles = [jnp.broadcast_to(tiles_ref[half:half + 1, :], (8, LANES)) for half in range(2)]
    near = [near_ref[:, half * LANES:(half + 1) * LANES] for half in range(2)]

    def look(table, index):
        return jnp.where(index < LANES, pick(table[0], index & (LANES - 1)), pick(table[1], index & (LANES - 1)))

    worst = jnp.zeros((8, LANES), jnp.int32)
    for half in range(2):
        tile = tiles[half]
        mine = look(near, jnp.maximum(tile, 0))
        linked = (tile >= 0) & (mine >= 0) & (row < 4)
        other = [look(tiles, partner(lane + half * LANES, link, nx, ny)) for link in range(4)]
        over_x = (mine == other[1]) | (mine == other[3])
        kind = jnp.where(linked, jnp.where(mine == tile, 4, jnp.where(over_x, 1, 2)), 0)
        after = jnp.where(row < 3, pltpu.roll(kind, 7, 0), pltpu.roll(kind, 3, 0))
        odd = (kind == 4) | ((kind > 0) & (kind == after) & (row < 4))
        worst = jnp.where(odd, 1, worst)
    flag[0] = jnp.max(worst)


def plan_kernel(shape, tiles_hbm, near_hbm, turn_hbm, raw, wet_raw, route_ref, plan_ref, almost_ref,
                state_ref, tiles_ref, near_ref, turn_ref, sems):
    nx, ny = shape
    copies = [pltpu.make_async_copy(tiles_hbm, tiles_ref, sems.at[0]),
              pltpu.make_async_copy(near_hbm, near_ref, sems.at[1]),
              pltpu.make_async_copy(turn_hbm, turn_ref, sems.at[2])]
    for copy in copies:
        copy.start()
    state = masked_state(raw, wet_raw, state_ref)
    base, _ = without_rims(state)
    row = lax.broadcasted_iota(jnp.int32, (8, WIDE), 0)
    almost_ref[...] = if_live(route_ref, base + force_of(state, base, row))
    for copy in copies:
        copy.wait()
    me = my_index(ny)
    tile = tiles_ref[me]
    held = jnp.maximum(tile, 0)
    across = [partner(me, link, nx, ny) for link in range(4)]
    for link in range(4):
        other = tiles_ref[across[link]]
        side = jnp.int32(-1)
        for k in range(4):
            side = jnp.where((tile >= 0) & (other >= 0) & (near_ref[k, held] == other), k, side)
        linked = side >= 0
        facing = (side + 2 + turn_ref[jnp.maximum(side, 0), held]) % 4
        there = jnp.maximum(other, 0)
        for end in range(2):
            later = (side < 2) == (end == 0)
            lateral = jnp.where(later, facing + 1, facing + 3) % 4
            beyond = jnp.where(linked, near_ref[lateral, there], -1)
            back = (lateral + 2 + turn_ref[lateral, there]) % 4
            corner = jnp.where(later, back + 1, back) % 4
            if link in (1, 3):
                found = [tiles_ref[partner(across[u], link, nx, ny)] for u in (0, 2)]
                which = jnp.where(beyond == found[0], 1, jnp.where(beyond == found[1], 2, 0))
                lane = corner + RELAY_AT[link]
            else:
                found = [tiles_ref[partner(across[link], v, nx, ny)] for v in (1, 3)]
                which = jnp.where((beyond == found[0]) | (beyond == found[1]), 1 + link // 2, 0)
                lane = corner + jnp.where(beyond == found[0], RELAY_AT[1], RELAY_AT[3])
            for i, value in ((0, jnp.where(beyond >= 0, which, 0)), (1, lane)):
                at = 2 * (2 * link + end) + i
                plan_ref[at:at + 1, :] = jnp.full((1, LANES), value, jnp.int32)


def relay_kernel(pay0, pay2, came1, came3, out0, out2):
    lane = lanes()
    for pay, out in ((pay0, out0), (pay2, out2)):
        line = pay[0:8, :]
        for link, came in ((1, came1), (3, came3)):
            moved = pltpu.roll(came[0:8, :], RELAY_AT[link] - OWN_AT, 1)
            line = jnp.where((lane >= RELAY_AT[link]) & (lane < RELAY_AT[link] + 4), moved, line)
        out[0:8, :] = line
        out[8:16, :] = pay[8:16, :]


def edge_patches(lines, rims):
    patch = []
    for side in range(4):
        drift = repeated(lines[side], 0 if side % 2 == 1 else 2)
        sign = 1.0 if side in (1, 2) else -1.0
        patch.append(wet_rows(lines[side]) * (DIFFUSE - (sign * 0.5 * ADVECT) * drift) * rims[side])
    return patch


def with_ends(patch):
    south, east, north, west = patch
    end = TILE - 1
    return [
        south + at_ends(west, 0, 0) + at_ends(east, 0, end),
        east + at_ends(south, end, 0) + at_ends(north, end, end),
        north + at_ends(west, end, 0) + at_ends(east, end, end),
        west + at_ends(south, 0, 0) + at_ends(north, 0, end),
    ]


def final_kernel(route_ref, plan_ref, lines_ref, inner_ref, almost_ref, came1, came3, came0, came2, out_ref, full, sems):
    lane, row = lanes(), rows()
    route, plan = Rows(route_ref), Rows(plan_ref)
    came = [came0, came1, came2, came3]
    outer = []
    for link in range(4):
        line = came[link][0:8, :]
        for end, lane_to in ((0, LANES - 1), (1, TILE)):
            which, lane_from = plan[2 * (2 * link + end)], plan[2 * (2 * link + end) + 1]
            held = came[link][0:8, :]
            if link in (1, 3):
                held = jnp.where(which == 2, came2[0:8, :], came0[0:8, :])
            value = pick(held, lane_from)
            line = jnp.where(lane == lane_to, jnp.where(which > 0, value, 0.0), line)
        outer.append(line)
    rims = rims_of(route, None, outer)
    beyond = rims_of(route, None, [came[link][8:16, :] for link in range(4)])
    lines, inner = four_of(lines_ref), four_of(inner_ref)
    patch = edge_patches(lines, rims)
    whole = with_ends(patch)
    on_edge, inside = [], []
    for side in range(4):
        sign = 1.0 if side in (1, 2) else -1.0
        line, wet, wet_in = rims[side], wet_rows(lines[side]), wet_rows(inner[side])
        after, before = pltpu.roll(line, LANES - 1, 1), pltpu.roll(line, 1, 1)
        first, second = pltpu.roll(line, 4, 0), pltpu.roll(line, 2, 0)
        normal, tangent = (first, second) if side % 2 == 1 else (second, first)
        along = normal * (sign * (beyond[side] - lines[side])) + tangent * (after - before)
        round_sum = after + before + beyond[side] + lines[side] - 4.0 * line
        tracer = wet_rows(line) * (line - (0.5 * ADVECT) * along + DIFFUSE * round_sum)
        far = pressure_of(tracer, row)
        mine = jnp.where(lane < TILE, pressure_of(whole[side], row), 0.0)
        drop = pltpu.roll(mine, LANES - 1, 1) - pltpu.roll(mine, 1, 1)
        to_normal, to_tangent = (4, 6) if side % 2 == 1 else (6, 4)
        own_row = row < 2 if side % 2 == 1 else (row >= 2) & (row < 4)
        cross_row = (row >= 2) & (row < 4) if side % 2 == 1 else row < 2
        push = jnp.where(own_row, sign * pltpu.roll(far, to_normal, 0), 0.0)
        push = jnp.where(cross_row, pltpu.roll(drop, to_tangent, 0), push)
        on_edge.append(patch[side] - (0.5 * STEP_SIZE) * wet * push)
        kept = own_row & (lane > 0) & (lane < TILE - 1)
        inside.append(jnp.where(kept, (-sign * 0.5 * STEP_SIZE) * wet_in * pltpu.roll(mine, to_normal, 0), 0.0))
    edges, seconds = spread_chunks(on_edge, 0), spread_chunks(inside, 1)
    copies = []
    for low, high in ((0, 24), (24, CHUNKS)):
        for c in range(low, high):
            cut = slice(c * LANES, min((c + 1) * LANES, CELLS))
            width = cut.stop - cut.start
            full[:, cut] = (almost_ref[:, c * LANES:(c + 1) * LANES] + (edges[c] + seconds[c]))[:, :width]
        cells = pl.ds(low * LANES, min(high * LANES, CELLS) - low * LANES)
        for c in range(6):
            copies.append(pltpu.make_async_copy(full.at[c, cells], out_ref.at[c, 0, cells], sems.at[len(copies)]))
            copies[-1].start()
    for copy in copies:
        copy.wait()


def write_out(full, out_ref, sems):
    copies = [pltpu.make_async_copy(full.at[c], out_ref.at[c, 0], sems.at[c]) for c in range(6)]
    for copy in copies:
        copy.start()
    for copy in copies:
        copy.wait()


def at_ends(line, lane_from, lane_to):
    value = jnp.broadcast_to(line[:, lane_from:lane_from + 1], (8, LANES))
    return jnp.where(lanes() == lane_to, value, 0.0)


def edge_kernel(route_ref, lines_ref, base_lines_ref, came0, came1, came2, came3,
                patch_ref, own_two_ref, pay0, pay1, pay2, pay3):
    route = Rows(route_ref)
    lines, base = four_of(lines_ref), four_of(base_lines_ref)
    own = own_rims([sent_line(lines[side], side, route, True) for side in range(4)], route)
    rims = rims_of(route, own, [came[0:8, :] for came in by_link((came0, came1, came2, came3), BOTH)])
    patch = edge_patches(lines, rims)
    whole = with_ends(patch)
    press = []
    for side in range(4):
        patch_ref[8 * side:8 * side + 8, :] = patch[side]
        press.append(sent_line(pressure_of(base[side] + whole[side], rows()), side, route, False))
    for link, pay in zip(SECOND_ORDER, (pay0, pay1, pay2, pay3)):
        pay[...] = chosen(press, route, link)
    own = own_rims(press, route)
    for side in range(4):
        own_two_ref[8 * side:8 * side + 8, :] = own[side]


def middle_kernel(route_ref, state_ref, base_ref, patch_ref, out_ref):
    state = state_ref[...]
    cell, column = column_of()
    base = base_ref[...] + spread(four_of(patch_ref), cell, column)
    row = lax.broadcasted_iota(jnp.int32, (8, WIDE), 0)
    out_ref[...] = if_live(route_ref, base + force_of(state, base, row))


def last_kernel(route_ref, lines_ref, own_ref, almost_ref, came0, came1, came2, came3, out_ref, full, sems):
    route = Rows(route_ref)
    rims = rims_of(route, four_of(own_ref), [came[...] for came in by_link((came0, came1, came2, came3), SECOND_ORDER)])
    patch = []
    for side in range(4):
        wet = wet_rows(lines_ref[8 * side:8 * side + 8, :])
        row = rows()
        rim = pltpu.roll(rims[side], 4 if side % 2 == 1 else 6, 0)
        mine = row < 2 if side % 2 == 1 else (row >= 2) & (row < 4)
        sign = -1.0 if side in (1, 2) else 1.0
        patch.append(jnp.where(mine, (sign * 0.5 * STEP_SIZE) * wet * rim, 0.0))
    cell, column = column_of()
    full[...] = (almost_ref[...] + spread(patch, cell, column))[:, :CELLS]
    write_out(full, out_ref, sems)


def sds(*shape, dtype=jnp.float32):
    return jax.ShapeDtypeStruct(shape, dtype)


PARAMS = pltpu.CompilerParams(vmem_limit_bytes=16 * 1024 * 1024)


def on_device(nx, ny, fields, wet_mask, tile_of_slot, neighbor, rotation):
    line, pair, four, wide = sds(8, LANES), sds(16, LANES), sds(32, LANES), sds(8, WIDE)
    table = pltpu.SMEM((4, nx * ny), jnp.int32)
    tables = [pltpu.with_memory_space_constraint(v, pltpu.HBM) for v in (tile_of_slot, neighbor.T, rotation.T)]
    inputs = [pltpu.with_memory_space_constraint(v, pltpu.HBM) for v in (fields.reshape(6, 1, CELLS), wet_mask)]
    raw, wet_raw, lines, inner, *pays, route = pl.pallas_call(
        lambda *refs: load_kernel((nx, ny), *refs),
        out_shape=[sds(8, CELLS), sds(8, CELLS, dtype=jnp.int32), four, four, pair, pair, pair, pair,
                   sds(ROUTE, LANES, dtype=jnp.int32)],
        in_specs=[HBM] * 5,
        out_specs=[VMEM] * 9,
        scratch_shapes=[pltpu.SMEM((nx * ny,), jnp.int32), table, table, pltpu.SemaphoreType.DMA((10,))],
        compiler_params=PARAMS, name="load",
    )(*tables, *inputs)
    came_x = exchanged(pays[:2], X_ORDER, nx, ny)
    halves = pltpu.with_memory_space_constraint(tile_of_slot.reshape(2, LANES), pltpu.HBM)
    flag = pl.pallas_call(
        lambda *refs: check_kernel((nx, ny), *refs),
        out_shape=sds(1, dtype=jnp.int32), in_specs=[HBM] * 2, out_specs=SMEM,
        scratch_shapes=[pltpu.VMEM((2, LANES), jnp.int32), pltpu.VMEM((8, nx * ny), jnp.int32),
                        pltpu.SemaphoreType.DMA((2,))],
        compiler_params=PARAMS, name="check",
        cost_estimate=pl.CostEstimate(flops=1000000, bytes_accessed=600000, transcendentals=0),
    )(halves, tables[1])

    result = pltpu.HBM((6, 1, CELLS), jnp.float32)
    writing = [pltpu.VMEM((8, CELLS), jnp.float32), pltpu.SemaphoreType.DMA((12,))]

    def grid_like():
        sent = pl.pallas_call(
            relay_kernel, out_shape=[pair, pair], in_specs=[VMEM] * 4, out_specs=[VMEM] * 2,
            compiler_params=PARAMS, name="relay",
        )(*by_link(pays[2:], U_ORDER, (0, 2)), *by_link(came_x, X_ORDER, (1, 3)))
        came_u = exchanged([sent[(0, 2).index(link)] for link in U_ORDER], U_ORDER, nx, ny)
        plan, almost = pl.pallas_call(
            lambda *refs: plan_kernel((nx, ny), *refs),
            out_shape=[sds(16, LANES, dtype=jnp.int32), wide], in_specs=[HBM] * 3 + [VMEM] * 3, out_specs=[VMEM] * 2,
            scratch_shapes=[pltpu.VMEM((8, WIDE), jnp.float32), pltpu.SMEM((nx * ny,), jnp.int32), table, table,
                            pltpu.SemaphoreType.DMA((3,))],
            compiler_params=PARAMS, name="plan",
            cost_estimate=pl.CostEstimate(flops=2000000, bytes_accessed=800000, transcendentals=0),
        )(*tables, raw, wet_raw, route)
        return pl.pallas_call(
            final_kernel, out_shape=result, in_specs=[VMEM] * 9, out_specs=HBM,
            scratch_shapes=writing, compiler_params=PARAMS, name="final",
        )(route, plan, lines, inner, almost, *by_link(came_x, X_ORDER, (1, 3)), *by_link(came_u, U_ORDER, (0, 2)))

    def general():
        came = came_x + exchanged(pays[2:], U_ORDER, nx, ny)
        state, base, base_lines = pl.pallas_call(
            base_kernel, out_shape=[wide, wide, four], in_specs=[VMEM] * 2, out_specs=[VMEM] * 3,
            compiler_params=PARAMS, name="base",
            cost_estimate=pl.CostEstimate(flops=2000000, bytes_accessed=800000, transcendentals=0),
        )(raw, wet_raw)
        patch, own_two, *press = pl.pallas_call(
            edge_kernel, out_shape=[four, four, line, line, line, line],
            in_specs=[VMEM] * 7, out_specs=[VMEM] * 6,
            compiler_params=PARAMS, name="edge",
        )(route, lines, base_lines, *came)
        came_two = exchanged(press, SECOND_ORDER, nx, ny)
        nearly = pl.pallas_call(
            middle_kernel, out_shape=wide, in_specs=[VMEM] * 4, out_specs=VMEM,
            compiler_params=PARAMS, name="middle",
            cost_estimate=pl.CostEstimate(flops=2000000, bytes_accessed=800000, transcendentals=0),
        )(route, state, base, patch)
        return pl.pallas_call(
            last_kernel, out_shape=result, in_specs=[VMEM] * 8, out_specs=HBM,
            scratch_shapes=writing, compiler_params=PARAMS, name="last",
        )(route, lines, own_two, nearly, *came_two)

    out = lax.cond(flag[0] == 0, grid_like, general)
    return out.reshape(1, 6, CELLS)


def solution(mesh):
    nx, ny = mesh.shape["gx"], mesh.shape["gy"]
    in_specs = (P(AXES, None, None), P(AXES, None), P(), P(), P())
    return jax.shard_map(lambda *args: on_device(nx, ny, *args), mesh=mesh, in_specs=in_specs,
                         out_specs=P(AXES, None, None), check_vma=False)
```

time: 23.2 us -> 18.2 us (0.78)
  the two profiles are of different devices: /device:TPU:30 before, /device:TPU:1 now
where the time goes in v3:
time: 18.2 us; the launch traced here: 18 us
  starting transfers between devices  9.51 us (52%)
  Pallas kernels  5.57 us (31%)
  waiting for transfers between devices  2.19 us (12%)
  between operations  0.68 us (4%)
    ppermute x4, starting transfers between devices, exchanged(): lax.ppermute(pay, AXES, pairs_of(LINKS[link], nx, ny))  9.51 us
    ppermute x4, waiting for transfers between devices, exchanged(): lax.ppermute(pay, AXES, pairs_of(LINKS[link], nx, ny))  2.19 us
    pallas_call x1, Pallas kernels, grid_like(): pl.pallas_call(lambda *refs: plan_kernel((nx, ny), *refs), out_shape=[sds...  1.63 us
    pallas_call x1, Pallas kernels, on_device(): pl.pallas_call(lambda *refs: check_kernel((nx, ny), *refs), out_shape=sds...  1.54 us
    pallas_call x1, Pallas kernels, on_device(): pl.pallas_call(lambda *refs: load_kernel((nx, ny), *refs), out_shape=[sds...  1.22 us
    pallas_call x1, Pallas kernels, grid_like(): pl.pallas_call(final_kernel, out_shape=result, in_specs=[VMEM] * 9, out_s...  1.1 us
  transfers between devices with their start and end apart: 4, of which 1 were waited for; matrix products, arithmetic and copies ran while one was open for 0% of the time, Pallas kernels for 18%

profile of v3, /device:TPU:1, one launch (start us, length us, event | category | flops | bytes accessed | tf_op | source)
XLA Modules:
  0.0 18.0 jit_solution(13926638088738403236)
XLA Ops:
  0.0 1.2 %load.1 = (f32[8,8100]{1,0:T(8,128)S(1)}, s32[8,8100]{1,0:T(8,128)S(1)}, f32[32,128]{1,0:T(8,128)S(1)}, f32[32,128]{1,0:T(8,128)S(1)}, f32[16,128]{1,0:T(8,128)S...) custom-call(s32[256]{0:T(256)} %refs_0_.1, ...), custom_call_target="tpu_custom_call" | custom-call | tf_op jit(solution)/shard_map/load/pallas_call | solution.py:633
  1.2 3.1 %collective-permute-start.8 = (f32[16,128]{1,0:T(8,128)S(1)}, f32[16,128]{1,0:T(8,128)S(1)}, u32[]{:S(2)}, u32[]{:S(2)}) collective-permute-start(f32[16,128]{1,0:T(8,128)S(1)} %get-tuple-element.97), channel_id=1, source_target_pairs={{0,240},{1,241},{2,242},{3,243},{4,244},{5,245},{6,246},{7,247},{8... | collective-permute-start | bytes 24584 | tf_op jit(solution)/shard_map/ppermute | solution.py:66
  4.3 3.8 %collective-permute-start.9 = (f32[16,128]{1,0:T(8,128)S(1)}, f32[16,128]{1,0:T(8,128)S(1)}, u32[]{:S(2)}, u32[]{:S(2)}) collective-permute-start(f32[16,128]{1,0:T(8,128)S(1)} %get-tuple-element.98), channel_id=1, source_target_pairs={{0,16},{1,17},{2,18},{3,19},{4,20},{5,21},{6,22},{7,23},{8,24},{9,... | collective-permute-start | bytes 24584 | tf_op jit(solution)/shard_map/ppermute | solution.py:66
  8.1 1.5 %check.1 = s32[1]{0:T(128)} custom-call(s32[2,128]{1,0:T(2,128)} %bitcast.15, s32[4,256]{1,0:T(4,128)} %bitcast.11), custom_call_target="tpu_custom_call" | custom-call | flops 1000000 | bytes 600000 | tf_op jit(solution)/shard_map/check/pallas_call | solution.py:644
  10.3 0.0 collective-permute-done.8
  10.3 0.0 collective-permute-done.9
  10.3 7.6 %conditional.1 = (f32[1,6,8100]{2,0,1:T(1,128)}) conditional(s32[]{:T(128)} %bitcast.4, (f32[8,8100]{1,0:T(8,128)S(1)}, s32[8,8100]{1,0:T(8,128)S(1)}, f32[16,128]{1,0:T(8,128)S(1)}, f32[16,128]{1,0:T(8,128)S(1)}, s32[48,128]{1,0:T(8,128)S(1)}, /*index=5*/f32[32,128]{1,0:T(8,128)S(1)}, f32[16,128]{1,0:T(8,128)S(1)}, ...), branch_computations={%region_0.0_spmd, %region_1.0_spmd} | conditional | flops 4000000 | bytes 1731320 | solution.py:698
  10.4 0.1 relay.1
  10.4 2.3 %collective-permute-start.6 = (f32[16,128]{1,0:T(8,128)S(1)}, f32[16,128]{1,0:T(8,128)S(1)}, u32[]{:S(2)}, u32[]{:S(2)}) collective-permute-start(f32[16,128]{1,0:T(8,128)S(1)} %get-tuple-element.80), channel_id=1, source_target_pairs={{0,128},{1,2},{2,1},{3,4},{4,3},{5,6},{6,5},{7,8},{8,7},{9,10},{10... | collective-permute-start | bytes 24584 | tf_op jit(solution)/shard_map/cond/branch_1_fun/ppermute | solution.py:66
  12.7 0.4 %collective-permute-start.7 = (f32[16,128]{1,0:T(8,128)S(1)}, f32[16,128]{1,0:T(8,128)S(1)}, u32[]{:S(2)}, u32[]{:S(2)}) collective-permute-start(f32[16,128]{1,0:T(8,128)S(1)} %get-tuple-element.81), channel_id=1, source_target_pairs={{0,1},{1,0},{2,3},{3,2},{4,5},{5,4},{6,7},{7,6},{8,9},{9,8},{10,11... | collective-permute-start | bytes 24584 | tf_op jit(solution)/shard_map/cond/branch_1_fun/ppermute | solution.py:66
  13.1 1.6 %plan.1 = (s32[16,128]{1,0:T(8,128)S(1)}, f32[8,8192]{1,0:T(8,128)S(1)}) custom-call(s32[256]{0:T(256)} %get-tuple-element.67.refs_0_, s32[4,256]{1,0:T(4,128)} %get-tuple-element.68.refs_1_, s32[4,256]{1,0:T(4,128)} %get-tuple-element.69.refs_2_, f32[8,8100]{1,0:T(8,128)S(1)} %get-tuple-element.70.refs_3_, s32[8,8100]{1,0:T(8,128)S(1)} %get-tuple-element.71.refs_4_, ...), custom_call_target="tpu_custom_call" | custom-call | flops 2000000 | bytes 800000 | tf_op jit(solution)/shard_map/cond/branch_1_fun/plan/pallas_call | solution.py:662
  14.7 2.2 %collective-permute-done.6.came0 = f32[16,128]{1,0:T(8,128)S(1)} collective-permute-done((f32[16,128]{1,0:T(8,128)S(1)}, f32[16,128]{1,0:T(8,128)S(1)}, u32[]{:S(2)}, u32[]{:S(2)}) %collective-permute-start.6) | collective-permute-done | bytes 8224 | tf_op jit(solution)/shard_map/cond/branch_1_fun/ppermute | solution.py:66
  16.9 0.0 collective-permute-done.7.came2
  16.9 1.1 %final.1 = f32[6,1,8100]{2,1,0:T(1,128)} custom-call(s32[48,128]{1,0:T(8,128)S(1)} %get-tuple-element.66.refs_5_.route_ref, s32[16,128]{1,0:T(8,128)S(1)} %get-tuple-element.72.plan_ref, f32[32,128]{1,0:T(8,128)S(1)} %get-tuple-element.73.lines_ref, f32[32,128]{1,0:T(8,128)S(1)} %get-tuple-element.74.inner_ref, f32[8,8192]{1,0:T(8,128)S(1)} %get-tuple-element.75.almost_ref, ...), custom_call_target="tpu_custom_call" | custom-call | tf_op jit(solution)/shard_map/cond/branch_1_fun/final/pallas_call | solution.py:670
Async XLA Ops:
  1.2 9.1 %collective-permute-start.8 = (f32[16,128]{1,0:T(8,128)S(1)}, f32[16,128]{1,0:T(8,128)S(1)}, u32[]{:S(2)}, u32[]{:S(2)}) collective-permute-start(f32[16,128]{1,0:T(8,128)S(1)} %get-tuple-element.97), channel_id=1, source_target_pairs={{0,240},{1,241},{2,242},{3,243},{4,244},{5,245},{6,246},{7,247},{8... | collective-permute-start | bytes 24584 | tf_op jit(solution)/shard_map/ppermute | solution.py:66
  4.3 6.0 %collective-permute-start.9 = (f32[16,128]{1,0:T(8,128)S(1)}, f32[16,128]{1,0:T(8,128)S(1)}, u32[]{:S(2)}, u32[]{:S(2)}) collective-permute-start(f32[16,128]{1,0:T(8,128)S(1)} %get-tuple-element.98), channel_id=1, source_target_pairs={{0,16},{1,17},{2,18},{3,19},{4,20},{5,21},{6,22},{7,23},{8,24},{9,... | collective-permute-start | bytes 24584 | tf_op jit(solution)/shard_map/ppermute | solution.py:66
  10.4 6.4 %collective-permute-start.6 = (f32[16,128]{1,0:T(8,128)S(1)}, f32[16,128]{1,0:T(8,128)S(1)}, u32[]{:S(2)}, u32[]{:S(2)}) collective-permute-start(f32[16,128]{1,0:T(8,128)S(1)} %get-tuple-element.80), channel_id=1, source_target_pairs={{0,128},{1,2},{2,1},{3,4},{4,3},{5,6},{6,5},{7,8},{8,7},{9,10},{10... | collective-permute-start | bytes 24584 | tf_op jit(solution)/shard_map/cond/branch_1_fun/ppermute | solution.py:66
  12.7 4.2 %collective-permute-start.7 = (f32[16,128]{1,0:T(8,128)S(1)}, f32[16,128]{1,0:T(8,128)S(1)}, u32[]{:S(2)}, u32[]{:S(2)}) collective-permute-start(f32[16,128]{1,0:T(8,128)S(1)} %get-tuple-element.81), channel_id=1, source_target_pairs={{0,1},{1,0},{2,3},{3,2},{4,5},{5,4},{6,7},{7,6},{8,9},{9,8},{10,11... | collective-permute-start | bytes 24584 | tf_op jit(solution)/shard_map/cond/branch_1_fun/ppermute | solution.py:66

commit v4 on v3

--- a/solution.py
+++ b/solution.py
@@ -57,7 +57,7 @@
 
 
 X_ORDER = (3, 1)
-U_ORDER = (0, 2)
+U_ORDER = (2, 0)
 BOTH = X_ORDER + U_ORDER
 SECOND_ORDER = (2, 0, 3, 1)
 
@@ -295,8 +295,8 @@
     return out
 
 
-def load_kernel(shape, tiles_hbm, near_hbm, turn_hbm, fields_ref, wet_ref,
-                raw, wet_raw, lines_ref, inner_ref, pay0, pay1, pay2, pay3, route_ref,
+def load_kernel(shape, tiles_hbm, halves_hbm, near_hbm, turn_hbm, fields_ref, wet_ref,
+                raw, wet_raw, lines_ref, inner_ref, pay0, pay1, pay2, pay3, route_ref, halves_ref, table_ref,
                 tiles_ref, near_ref, turn_ref, sems):
     nx, ny = shape
     tables = [pltpu.make_async_copy(tiles_hbm, tiles_ref, sems.at[7]),
@@ -304,6 +304,8 @@
               pltpu.make_async_copy(turn_hbm, turn_ref, sems.at[9])]
     copies = [pltpu.make_async_copy(fields_ref.at[c, 0], raw.at[c], sems.at[c]) for c in range(6)]
     copies.append(pltpu.make_async_copy(wet_ref.at[0], wet_raw.at[0], sems.at[6]))
+    copies.append(pltpu.make_async_copy(halves_hbm, halves_ref, sems.at[10]))
+    copies.append(pltpu.make_async_copy(near_hbm, table_ref.at[0:4], sems.at[11]))
     for copy in tables + copies:
         copy.start()
     for copy in tables:
@@ -401,17 +403,29 @@
         base_lines_ref[8 * side:8 * side + 8, :] = lines[side]
 
 
-def check_kernel(shape, tiles_hbm, near_hbm, flag, tiles_ref, near_ref, sems):
-    nx, ny = shape
+def inner_kernel(shape, tiles_hbm, near_hbm, turn_hbm, raw, wet_raw, route_ref, almost_ref, plan_ref,
+                 state_ref, tiles_ref, near_ref, turn_ref, sems):
     copies = [pltpu.make_async_copy(tiles_hbm, tiles_ref, sems.at[0]),
-              pltpu.make_async_copy(near_hbm, near_ref.at[0:4], sems.at[1])]
+              pltpu.make_async_copy(near_hbm, near_ref, sems.at[1]),
+              pltpu.make_async_copy(turn_hbm, turn_ref, sems.at[2])]
     for copy in copies:
         copy.start()
+    state = masked_state(raw, wet_raw, state_ref)
+    base, _ = without_rims(state)
+    almost_ref[...] = base
     for copy in copies:
         copy.wait()
+    corner_plan(shape, tiles_ref, near_ref, turn_ref, plan_ref)
+    base = almost_ref[...]
+    row = lax.broadcasted_iota(jnp.int32, (8, WIDE), 0)
+    almost_ref[...] = if_live(route_ref, base + force_of(state, base, row))
+
+
+def check_kernel(shape, halves_ref, table_ref, after, flag):
+    nx, ny = shape
     row, lane = rows(), lanes()
-    tiles = [jnp.broadcast_to(tiles_ref[half:half + 1, :], (8, LANES)) for half in range(2)]
-    near = [near_ref[:, half * LANES:(half + 1) * LANES] for half in range(2)]
+    tiles = [jnp.broadcast_to(halves_ref[half:half + 1, :], (8, LANES)) for half in range(2)]
+    near = [table_ref[:, half * LANES:(half + 1) * LANES] for half in range(2)]
 
     def look(table, index):
         return jnp.where(index < LANES, pick(table[0], index & (LANES - 1)), pick(table[1], index & (LANES - 1)))
@@ -430,20 +444,8 @@
     flag[0] = jnp.max(worst)
 
 
-def plan_kernel(shape, tiles_hbm, near_hbm, turn_hbm, raw, wet_raw, route_ref, plan_ref, almost_ref,
-                state_ref, tiles_ref, near_ref, turn_ref, sems):
+def corner_plan(shape, tiles_ref, near_ref, turn_ref, plan_ref):
     nx, ny = shape
-    copies = [pltpu.make_async_copy(tiles_hbm, tiles_ref, sems.at[0]),
-              pltpu.make_async_copy(near_hbm, near_ref, sems.at[1]),
-              pltpu.make_async_copy(turn_hbm, turn_ref, sems.at[2])]
-    for copy in copies:
-        copy.start()
-    state = masked_state(raw, wet_raw, state_ref)
-    base, _ = without_rims(state)
-    row = lax.broadcasted_iota(jnp.int32, (8, WIDE), 0)
-    almost_ref[...] = if_live(route_ref, base + force_of(state, base, row))
-    for copy in copies:
-        copy.wait()
     me = my_index(ny)
     tile = tiles_ref[me]
     held = jnp.maximum(tile, 0)
@@ -475,11 +477,11 @@
                 plan_ref[at:at + 1, :] = jnp.full((1, LANES), value, jnp.int32)
 
 
-def relay_kernel(pay0, pay2, came1, came3, out0, out2):
+def relay_kernel(pay0, pay1, came0, came1, after, out0, out1):
     lane = lanes()
-    for pay, out in ((pay0, out0), (pay2, out2)):
+    for pay, out in ((pay0, out0), (pay1, out1)):
         line = pay[0:8, :]
-        for link, came in ((1, came1), (3, came3)):
+        for link, came in zip(X_ORDER, (came0, came1)):
             moved = pltpu.roll(came[0:8, :], RELAY_AT[link] - OWN_AT, 1)
             line = jnp.where((lane >= RELAY_AT[link]) & (lane < RELAY_AT[link] + 4), moved, line)
         out[0:8, :] = line
@@ -506,10 +508,10 @@
     ]
 
 
-def final_kernel(route_ref, plan_ref, lines_ref, inner_ref, almost_ref, came1, came3, came0, came2, out_ref, full, sems):
+def final_kernel(route_ref, plan_ref, lines_ref, inner_ref, almost_ref, first, second, third, fourth, out_ref, full, sems):
     lane, row = lanes(), rows()
     route, plan = Rows(route_ref), Rows(plan_ref)
-    came = [came0, came1, came2, came3]
+    came = by_link((first, second, third, fourth), BOTH)
     outer = []
     for link in range(4):
         line = came[link][0:8, :]
@@ -517,7 +519,7 @@
             which, lane_from = plan[2 * (2 * link + end)], plan[2 * (2 * link + end) + 1]
             held = came[link][0:8, :]
             if link in (1, 3):
-                held = jnp.where(which == 2, came2[0:8, :], came0[0:8, :])
+                held = jnp.where(which == 2, came[2][0:8, :], came[0][0:8, :])
             value = pick(held, lane_from)
             line = jnp.where(lane == lane_to, jnp.where(which > 0, value, 0.0), line)
         outer.append(line)
@@ -627,53 +629,52 @@
 
 def on_device(nx, ny, fields, wet_mask, tile_of_slot, neighbor, rotation):
     line, pair, four, wide = sds(8, LANES), sds(16, LANES), sds(32, LANES), sds(8, WIDE)
-    table = pltpu.SMEM((4, nx * ny), jnp.int32)
+    scalars = pltpu.SMEM((4, nx * ny), jnp.int32)
     tables = [pltpu.with_memory_space_constraint(v, pltpu.HBM) for v in (tile_of_slot, neighbor.T, rotation.T)]
     inputs = [pltpu.with_memory_space_constraint(v, pltpu.HBM) for v in (fields.reshape(6, 1, CELLS), wet_mask)]
-    raw, wet_raw, lines, inner, *pays, route = pl.pallas_call(
+    halves = pltpu.with_memory_space_constraint(tile_of_slot.reshape(2, LANES), pltpu.HBM)
+    raw, wet_raw, lines, inner, *pays, route, halves, table = pl.pallas_call(
         lambda *refs: load_kernel((nx, ny), *refs),
         out_shape=[sds(8, CELLS), sds(8, CELLS, dtype=jnp.int32), four, four, pair, pair, pair, pair,
-                   sds(ROUTE, LANES, dtype=jnp.int32)],
-        in_specs=[HBM] * 5,
-        out_specs=[VMEM] * 9,
-        scratch_shapes=[pltpu.SMEM((nx * ny,), jnp.int32), table, table, pltpu.SemaphoreType.DMA((10,))],
+                   sds(ROUTE, LANES, dtype=jnp.int32),
+                   sds(2, LANES, dtype=jnp.int32), sds(8, nx * ny, dtype=jnp.int32)],
+        in_specs=[HBM] * 6,
+        out_specs=[VMEM] * 11,
+        scratch_shapes=[pltpu.SMEM((nx * ny,), jnp.int32), scalars, scalars, pltpu.SemaphoreType.DMA((12,))],
         compiler_params=PARAMS, name="load",
-    )(*tables, *inputs)
+    )(tables[0], halves, *tables[1:], *inputs)
     came_x = exchanged(pays[:2], X_ORDER, nx, ny)
-    halves = pltpu.with_memory_space_constraint(tile_of_slot.reshape(2, LANES), pltpu.HBM)
+    almost, plan = pl.pallas_call(
+        lambda *refs: inner_kernel((nx, ny), *refs),
+        out_shape=[wide, sds(16, LANES, dtype=jnp.int32)], in_specs=[HBM] * 3 + [VMEM] * 3, out_specs=[VMEM] * 2,
+        scratch_shapes=[pltpu.VMEM((8, WIDE), jnp.float32), pltpu.SMEM((nx * ny,), jnp.int32), scalars, scalars,
+                        pltpu.SemaphoreType.DMA((3,))],
+        compiler_params=PARAMS, name="inner",
+        cost_estimate=pl.CostEstimate(flops=2000000, bytes_accessed=800000, transcendentals=0),
+    )(*tables, raw, wet_raw, route)
+    sent = pl.pallas_call(
+        relay_kernel, out_shape=[pair, pair], in_specs=[VMEM] * 4 + [ANY], out_specs=[VMEM] * 2,
+        compiler_params=PARAMS, name="relay",
+    )(*pays[2:], *came_x, almost)
+    came_u = exchanged(sent, U_ORDER, nx, ny)
     flag = pl.pallas_call(
         lambda *refs: check_kernel((nx, ny), *refs),
-        out_shape=sds(1, dtype=jnp.int32), in_specs=[HBM] * 2, out_specs=SMEM,
-        scratch_shapes=[pltpu.VMEM((2, LANES), jnp.int32), pltpu.VMEM((8, nx * ny), jnp.int32),
-                        pltpu.SemaphoreType.DMA((2,))],
+        out_shape=sds(1, dtype=jnp.int32), in_specs=[VMEM] * 2 + [ANY], out_specs=SMEM,
         compiler_params=PARAMS, name="check",
-        cost_estimate=pl.CostEstimate(flops=1000000, bytes_accessed=600000, transcendentals=0),
-    )(halves, tables[1])
+        cost_estimate=pl.CostEstimate(flops=2000000, bytes_accessed=800000, transcendentals=0),
+    )(halves, table, sent[0])
 
     result = pltpu.HBM((6, 1, CELLS), jnp.float32)
     writing = [pltpu.VMEM((8, CELLS), jnp.float32), pltpu.SemaphoreType.DMA((12,))]
 
     def grid_like():
-        sent = pl.pallas_call(
-            relay_kernel, out_shape=[pair, pair], in_specs=[VMEM] * 4, out_specs=[VMEM] * 2,
-            compiler_params=PARAMS, name="relay",
-        )(*by_link(pays[2:], U_ORDER, (0, 2)), *by_link(came_x, X_ORDER, (1, 3)))
-        came_u = exchanged([sent[(0, 2).index(link)] for link in U_ORDER], U_ORDER, nx, ny)
-        plan, almost = pl.pallas_call(
-            lambda *refs: plan_kernel((nx, ny), *refs),
-            out_shape=[sds(16, LANES, dtype=jnp.int32), wide], in_specs=[HBM] * 3 + [VMEM] * 3, out_specs=[VMEM] * 2,
-            scratch_shapes=[pltpu.VMEM((8, WIDE), jnp.float32), pltpu.SMEM((nx * ny,), jnp.int32), table, table,
-                            pltpu.SemaphoreType.DMA((3,))],
-            compiler_params=PARAMS, name="plan",
-            cost_estimate=pl.CostEstimate(flops=2000000, bytes_accessed=800000, transcendentals=0),
-        )(*tables, raw, wet_raw, route)
         return pl.pallas_call(
             final_kernel, out_shape=result, in_specs=[VMEM] * 9, out_specs=HBM,
             scratch_shapes=writing, compiler_params=PARAMS, name="final",
-        )(route, plan, lines, inner, almost, *by_link(came_x, X_ORDER, (1, 3)), *by_link(came_u, U_ORDER, (0, 2)))
+        )(route, plan, lines, inner, almost, *came_x, *came_u)
 
     def general():
-        came = came_x + exchanged(pays[2:], U_ORDER, nx, ny)
+        came = came_x + came_u
         state, base, base_lines = pl.pallas_call(
             base_kernel, out_shape=[wide, wide, four], in_specs=[VMEM] * 2, out_specs=[VMEM] * 3,
             compiler_params=PARAMS, name="base",

time: 18.2 us -> 17.9 us (0.984)
  the two profiles are of different devices: /device:TPU:1 before, /device:TPU:30 now
where the time goes in v4:
time: 17.9 us; the launch traced here: 17.7 us
  starting transfers between devices  10.2 us (57%)
  Pallas kernels  4.6 us (26%)
  waiting for transfers between devices  2.18 us (12%)
  between operations  0.69 us (4%)
    ppermute x4, starting transfers between devices, exchanged(): lax.ppermute(pay, AXES, pairs_of(LINKS[link], nx, ny))  10.2 us
    ppermute x4, waiting for transfers between devices, exchanged(): lax.ppermute(pay, AXES, pairs_of(LINKS[link], nx, ny))  2.18 us
    pallas_call x1, Pallas kernels, on_device(): pl.pallas_call(lambda *refs: inner_kernel((nx, ny), *refs), out_shape=[wi...  1.37 us
    pallas_call x1, Pallas kernels, on_device(): pl.pallas_call(lambda *refs: load_kernel((nx, ny), *refs), out_shape=[sds...  1.25 us
    pallas_call x1, Pallas kernels, grid_like(): pl.pallas_call(final_kernel, out_shape=result, in_specs=[VMEM] * 9, out_s...  1.1 us
    pallas_call x1, Pallas kernels, on_device(): pl.pallas_call(lambda *refs: check_kernel((nx, ny), *refs), out_shape=sds...  0.82 us
  transfers between devices with their start and end apart: 4, of which 2 were waited for; matrix products, arithmetic and copies ran while one was open for 0% of the time, Pallas kernels for 12%

profile of v4, /device:TPU:30, one launch (start us, length us, event | category | flops | bytes accessed | tf_op | source)
XLA Modules:
  0.0 17.7 jit_solution(2965237638503596489)
XLA Ops:
  0.0 1.2 %load.1 = (f32[8,8100]{1,0:T(8,128)S(1)}, s32[8,8100]{1,0:T(8,128)S(1)}, f32[32,128]{1,0:T(8,128)S(1)}, f32[32,128]{1,0:T(8,128)S(1)}, f32[16,128]{1,0:T(8,128)S...) custom-call(s32[256]{0:T(256)} %refs_0_.3, ...), custom_call_target="tpu_custom_call" | custom-call | tf_op jit(solution)/shard_map/load/pallas_call | solution.py:636
  1.3 5.4 %collective-permute-start.4 = (f32[16,128]{1,0:T(8,128)S(1)}, f32[16,128]{1,0:T(8,128)S(1)}, u32[]{:S(2)}, u32[]{:S(2)}) collective-permute-start(f32[16,128]{1,0:T(8,128)S(1)} %get-tuple-element.88), channel_id=1, source_target_pairs={{0,240},{1,241},{2,242},{3,243},{4,244},{5,245},{6,246},{7,247},{8... | collective-permute-start | bytes 24584 | tf_op jit(solution)/shard_map/ppermute | solution.py:66
  6.6 0.0 collective-permute-start.5
  6.6 1.4 %inner.1 = (f32[8,8192]{1,0:T(8,128)S(1)}, s32[16,128]{1,0:T(8,128)S(1)}) custom-call(s32[256]{0:T(256)} %refs_0_.3, s32[4,256]{1,0:T(4,128)} %bitcast.11, s32[4,256]{1,0:T(4,128)} %bitcast.13, f32[8,8100]{1,0:T(8,128)S(1)} %get-tuple-element.90.refs_3_, s32[8,8100]{1,0:T(8,128)S(1)} %get-tuple-element.91.refs_4_, s32[48,128]{1,0:T(8,128)S(1)} %get-tuple-element.92.refs_5_), custom_call_target="tpu_custom_call" | custom-call | flops 2000000 | bytes 800000 | tf_op jit(solution)/shard_map/inner/pallas_call | solution.py:647
  8.0 0.0 collective-permute-done.4.came0
  8.0 0.0 collective-permute-done.5.came1
  8.0 0.1 relay.1
  8.1 4.8 %collective-permute-start.7 = (f32[16,128]{1,0:T(8,128)S(1)}, f32[16,128]{1,0:T(8,128)S(1)}, u32[]{:S(2)}, u32[]{:S(2)}) collective-permute-start(f32[16,128]{1,0:T(8,128)S(1)} %get-tuple-element.96), channel_id=1, source_target_pairs={{0,128},{1,2},{2,1},{3,4},{4,3},{5,6},{6,5},{7,8},{8,7},{9,10},{10... | collective-permute-start | bytes 24584 | tf_op jit(solution)/shard_map/ppermute | solution.py:66
  12.9 0.0 collective-permute-start.6
  12.9 0.8 %check.1 = s32[1]{0:T(128)} custom-call(s32[2,128]{1,0:T(2,128)S(1)} %get-tuple-element.84.refs_0_, s32[8,256]{1,0:T(8,128)S(1)} %get-tuple-element.85.refs_1_, f32[16,128]{1,0:T(8,128)S(1)} %get-tuple-element.94.refs_2_), custom_call_target="tpu_custom_call" | custom-call | flops 2000000 | bytes 800000 | tf_op jit(solution)/shard_map/check/pallas_call | solution.py:660
  14.4 1.3 %collective-permute-done.7 = f32[16,128]{1,0:T(8,128)S(1)} collective-permute-done((f32[16,128]{1,0:T(8,128)S(1)}, f32[16,128]{1,0:T(8,128)S(1)}, u32[]{:S(2)}, u32[]{:S(2)}) %collective-permute-start.7) | collective-permute-done | bytes 8224 | tf_op jit(solution)/shard_map/ppermute | solution.py:66
  15.7 0.9 %collective-permute-done.6 = f32[16,128]{1,0:T(8,128)S(1)} collective-permute-done((f32[16,128]{1,0:T(8,128)S(1)}, f32[16,128]{1,0:T(8,128)S(1)}, u32[]{:S(2)}, u32[]{:S(2)}) %collective-permute-start.6) | collective-permute-done | bytes 8224 | tf_op jit(solution)/shard_map/ppermute | solution.py:66
  16.6 1.1 %conditional.1 = (f32[1,6,8100]{2,0,1:T(1,128)}) conditional(s32[]{:T(128)} %bitcast.6, (f32[8,8100]{1,0:T(8,128)S(1)}, s32[8,8100]{1,0:T(8,128)S(1)}, s32[48,128]{1,0:T(8,128)S(1)}, f32[32,128]{1,0:T(8,128)S(1)}, f32[16,128]{1,0:T(8,128)S(1)}, /*index=5*/f32[16,128]{1,0:T(8,128)S(1)}, f32[16,128]{1,0:T(8,128)S(1)}, ...), branch_computations={%region_0.0_spmd, %region_1.0_spmd} | conditional | flops 4000000 | bytes 1665704 | solution.py:699
  16.6 1.1 %final.1 = f32[6,1,8100]{2,1,0:T(1,128)} custom-call(s32[48,128]{1,0:T(8,128)S(1)} %get-tuple-element.60.route_ref, s32[16,128]{1,0:T(8,128)S(1)} %get-tuple-element.61.plan_ref, f32[32,128]{1,0:T(8,128)S(1)} %get-tuple-element.62.lines_ref, f32[32,128]{1,0:T(8,128)S(1)} %get-tuple-element.63.inner_ref, f32[8,8192]{1,0:T(8,128)S(1)} %get-tuple-element.64.almost_ref, ...), custom_call_target="tpu_custom_call" | custom-call | tf_op jit(solution)/shard_map/cond/branch_1_fun/final/pallas_call | solution.py:671
Async XLA Ops:
  1.3 6.8 %collective-permute-start.4 = (f32[16,128]{1,0:T(8,128)S(1)}, f32[16,128]{1,0:T(8,128)S(1)}, u32[]{:S(2)}, u32[]{:S(2)}) collective-permute-start(f32[16,128]{1,0:T(8,128)S(1)} %get-tuple-element.88), channel_id=1, source_target_pairs={{0,240},{1,241},{2,242},{3,243},{4,244},{5,245},{6,246},{7,247},{8... | collective-permute-start | bytes 24584 | tf_op jit(solution)/shard_map/ppermute | solution.py:66
  6.6 1.4 %collective-permute-start.5 = (f32[16,128]{1,0:T(8,128)S(1)}, f32[16,128]{1,0:T(8,128)S(1)}, u32[]{:S(2)}, u32[]{:S(2)}) collective-permute-start(f32[16,128]{1,0:T(8,128)S(1)} %get-tuple-element.89), channel_id=1, source_target_pairs={{0,16},{1,17},{2,18},{3,19},{4,20},{5,21},{6,22},{7,23},{8,24},{9,... | collective-permute-start | bytes 24584 | tf_op jit(solution)/shard_map/ppermute | solution.py:66
  8.1 7.6 %collective-permute-start.7 = (f32[16,128]{1,0:T(8,128)S(1)}, f32[16,128]{1,0:T(8,128)S(1)}, u32[]{:S(2)}, u32[]{:S(2)}) collective-permute-start(f32[16,128]{1,0:T(8,128)S(1)} %get-tuple-element.96), channel_id=1, source_target_pairs={{0,128},{1,2},{2,1},{3,4},{4,3},{5,6},{6,5},{7,8},{8,7},{9,10},{10... | collective-permute-start | bytes 24584 | tf_op jit(solution)/shard_map/ppermute | solution.py:66
  12.9 3.7 %collective-permute-start.6 = (f32[16,128]{1,0:T(8,128)S(1)}, f32[16,128]{1,0:T(8,128)S(1)}, u32[]{:S(2)}, u32[]{:S(2)}) collective-permute-start(f32[16,128]{1,0:T(8,128)S(1)} %get-tuple-element.94.refs_2_), channel_id=1, source_target_pairs={{0,1},{1,0},{2,3},{3,2},{4,5},{5,4},{6,7},{7,6},{8,9},{9,8},{10,11... | collective-permute-start | bytes 24584 | tf_op jit(solution)/shard_map/ppermute | solution.py:66

commit v5 on v4

--- a/solution.py
+++ b/solution.py
@@ -44,7 +44,19 @@
     return x, ((y - 1) ^ 1) + 1
 
 
-LINKS = (link_y_odd, link_x_even, link_y_even, link_x_odd)
+def swapped(x, nx):
+    return (x % (nx // 2) == 0) | (x % (nx // 2) == 2)
+
+
+def link_u_first(x, y, nx, ny):
+    return (link_y_even if swapped(x, nx) else link_y_odd)(x, y, nx, ny)
+
+
+def link_u_second(x, y, nx, ny):
+    return (link_y_odd if swapped(x, nx) else link_y_even)(x, y, nx, ny)
+
+
+LINKS = (link_u_first, link_x_even, link_u_second, link_x_odd)
 
 
 def pairs_of(link, nx, ny):
@@ -56,9 +68,9 @@
     return out
 
 
+U_ORDER = (0, 2)
 X_ORDER = (3, 1)
-U_ORDER = (2, 0)
-BOTH = X_ORDER + U_ORDER
+BOTH = U_ORDER + X_ORDER
 SECOND_ORDER = (2, 0, 3, 1)
 
 
@@ -72,15 +84,14 @@
 
 def partner(me, which, nx, ny):
     x, y = me // ny, me % ny
-    if which == 0:
-        pole = (y == 0) | (y == ny - 1)
-        step = jnp.where(y % 2 == 1, 1, -1)
-        return jnp.where(pole, (x + nx // 2) % nx * ny + y, me + step)
     if which == 1:
         return me + jnp.where(x % 2 == 0, ny, -ny)
-    if which == 2:
-        return me + jnp.where(y % 2 == 0, 1, -1)
-    return (x + jnp.where(x % 2 == 1, 1, nx - 1)) % nx * ny + y
+    if which == 3:
+        return (x + jnp.where(x % 2 == 1, 1, nx - 1)) % nx * ny + y
+    even = me + jnp.where(y % 2 == 0, 1, -1)
+    pole = (y == 0) | (y == ny - 1)
+    odd = jnp.where(pole, (x + nx // 2) % nx * ny + y, me + jnp.where(y % 2 == 1, 1, -1))
+    return jnp.where(swapped(x, nx), even, odd) if which == 0 else jnp.where(swapped(x, nx), odd, even)
 
 
 def lanes():
@@ -187,7 +198,7 @@
 
 
 ROUTE = 48
-OWN_AT, RELAY_AT = TILE, {1: TILE + 4, 3: TILE + 8}
+OWN_AT, RELAY_AT = TILE, {0: TILE + 4, 2: TILE + 8}
 
 
 class Rows:
@@ -403,13 +414,14 @@
         base_lines_ref[8 * side:8 * side + 8, :] = lines[side]
 
 
-def inner_kernel(shape, tiles_hbm, near_hbm, turn_hbm, raw, wet_raw, route_ref, almost_ref, plan_ref,
-                 state_ref, tiles_ref, near_ref, turn_ref, sems):
+def inner_kernel(shape, tiles_hbm, near_hbm, turn_hbm, raw, wet_raw, route_ref, halves_ref, table_ref,
+                 almost_ref, plan_ref, flag, state_ref, tiles_ref, near_ref, turn_ref, sems):
     copies = [pltpu.make_async_copy(tiles_hbm, tiles_ref, sems.at[0]),
               pltpu.make_async_copy(near_hbm, near_ref, sems.at[1]),
               pltpu.make_async_copy(turn_hbm, turn_ref, sems.at[2])]
     for copy in copies:
         copy.start()
+    flag[0] = off_grid(shape, halves_ref, table_ref)
     state = masked_state(raw, wet_raw, state_ref)
     base, _ = without_rims(state)
     almost_ref[...] = base
@@ -418,10 +430,10 @@
     corner_plan(shape, tiles_ref, near_ref, turn_ref, plan_ref)
     base = almost_ref[...]
     row = lax.broadcasted_iota(jnp.int32, (8, WIDE), 0)
-    almost_ref[...] = if_live(route_ref, base + force_of(state, base, row))
-
-
-def check_kernel(shape, halves_ref, table_ref, after, flag):
+    almost_ref[...] = if_live(route_ref, base + force_of(state_ref[...], base, row))
+
+
+def off_grid(shape, halves_ref, table_ref):
     nx, ny = shape
     row, lane = rows(), lanes()
     tiles = [jnp.broadcast_to(halves_ref[half:half + 1, :], (8, LANES)) for half in range(2)]
@@ -441,7 +453,7 @@
         after = jnp.where(row < 3, pltpu.roll(kind, 7, 0), pltpu.roll(kind, 3, 0))
         odd = (kind == 4) | ((kind > 0) & (kind == after) & (row < 4))
         worst = jnp.where(odd, 1, worst)
-    flag[0] = jnp.max(worst)
+    return jnp.max(worst)
 
 
 def corner_plan(shape, tiles_ref, near_ref, turn_ref, plan_ref):
@@ -450,38 +462,35 @@
     tile = tiles_ref[me]
     held = jnp.maximum(tile, 0)
     across = [partner(me, link, nx, ny) for link in range(4)]
+    relayed = [(which, RELAY_AT[u], tiles_ref[partner(across[x], u, nx, ny)])
+               for which, x in ((1, 1), (2, 3)) for u in (0, 2)]
     for link in range(4):
         other = tiles_ref[across[link]]
         side = jnp.int32(-1)
         for k in range(4):
             side = jnp.where((tile >= 0) & (other >= 0) & (near_ref[k, held] == other), k, side)
-        linked = side >= 0
         facing = (side + 2 + turn_ref[jnp.maximum(side, 0), held]) % 4
         there = jnp.maximum(other, 0)
         for end in range(2):
             later = (side < 2) == (end == 0)
             lateral = jnp.where(later, facing + 1, facing + 3) % 4
-            beyond = jnp.where(linked, near_ref[lateral, there], -1)
+            beyond = jnp.where(side >= 0, near_ref[lateral, there], -1)
             back = (lateral + 2 + turn_ref[lateral, there]) % 4
             corner = jnp.where(later, back + 1, back) % 4
-            if link in (1, 3):
-                found = [tiles_ref[partner(across[u], link, nx, ny)] for u in (0, 2)]
-                which = jnp.where(beyond == found[0], 1, jnp.where(beyond == found[1], 2, 0))
-                lane = corner + RELAY_AT[link]
-            else:
-                found = [tiles_ref[partner(across[link], v, nx, ny)] for v in (1, 3)]
-                which = jnp.where((beyond == found[0]) | (beyond == found[1]), 1 + link // 2, 0)
-                lane = corner + jnp.where(beyond == found[0], RELAY_AT[1], RELAY_AT[3])
-            for i, value in ((0, jnp.where(beyond >= 0, which, 0)), (1, lane)):
-                at = 2 * (2 * link + end) + i
-                plan_ref[at:at + 1, :] = jnp.full((1, LANES), value, jnp.int32)
+            buffer, lane = jnp.int32(0), jnp.int32(0)
+            for which, base, name in relayed:
+                here = (beyond >= 0) & (beyond == name)
+                buffer, lane = jnp.where(here, which, buffer), jnp.where(here, base + corner, lane)
+            at = 2 * (2 * link + end)
+            plan_ref[at:at + 1, :] = jnp.full((1, LANES), buffer, jnp.int32)
+            plan_ref[at + 1:at + 2, :] = jnp.full((1, LANES), lane, jnp.int32)
 
 
 def relay_kernel(pay0, pay1, came0, came1, after, out0, out1):
     lane = lanes()
     for pay, out in ((pay0, out0), (pay1, out1)):
         line = pay[0:8, :]
-        for link, came in zip(X_ORDER, (came0, came1)):
+        for link, came in zip(U_ORDER, (came0, came1)):
             moved = pltpu.roll(came[0:8, :], RELAY_AT[link] - OWN_AT, 1)
             line = jnp.where((lane >= RELAY_AT[link]) & (lane < RELAY_AT[link] + 4), moved, line)
         out[0:8, :] = line
@@ -517,9 +526,7 @@
         line = came[link][0:8, :]
         for end, lane_to in ((0, LANES - 1), (1, TILE)):
             which, lane_from = plan[2 * (2 * link + end)], plan[2 * (2 * link + end) + 1]
-            held = came[link][0:8, :]
-            if link in (1, 3):
-                held = jnp.where(which == 2, came[2][0:8, :], came[0][0:8, :])
+            held = jnp.where(which == 2, came[3][0:8, :], came[1][0:8, :])
             value = pick(held, lane_from)
             line = jnp.where(lane == lane_to, jnp.where(which > 0, value, 0.0), line)
         outer.append(line)
@@ -643,27 +650,21 @@
         scratch_shapes=[pltpu.SMEM((nx * ny,), jnp.int32), scalars, scalars, pltpu.SemaphoreType.DMA((12,))],
         compiler_params=PARAMS, name="load",
     )(tables[0], halves, *tables[1:], *inputs)
-    came_x = exchanged(pays[:2], X_ORDER, nx, ny)
-    almost, plan = pl.pallas_call(
+    came_u = exchanged(pays[:2], U_ORDER, nx, ny)
+    almost, plan, flag = pl.pallas_call(
         lambda *refs: inner_kernel((nx, ny), *refs),
-        out_shape=[wide, sds(16, LANES, dtype=jnp.int32)], in_specs=[HBM] * 3 + [VMEM] * 3, out_specs=[VMEM] * 2,
+        out_shape=[wide, sds(16, LANES, dtype=jnp.int32), sds(1, dtype=jnp.int32)],
+        in_specs=[HBM] * 3 + [VMEM] * 5, out_specs=[VMEM, VMEM, SMEM],
         scratch_shapes=[pltpu.VMEM((8, WIDE), jnp.float32), pltpu.SMEM((nx * ny,), jnp.int32), scalars, scalars,
                         pltpu.SemaphoreType.DMA((3,))],
         compiler_params=PARAMS, name="inner",
         cost_estimate=pl.CostEstimate(flops=2000000, bytes_accessed=800000, transcendentals=0),
-    )(*tables, raw, wet_raw, route)
+    )(*tables, raw, wet_raw, route, halves, table)
     sent = pl.pallas_call(
         relay_kernel, out_shape=[pair, pair], in_specs=[VMEM] * 4 + [ANY], out_specs=[VMEM] * 2,
         compiler_params=PARAMS, name="relay",
-    )(*pays[2:], *came_x, almost)
-    came_u = exchanged(sent, U_ORDER, nx, ny)
-    flag = pl.pallas_call(
-        lambda *refs: check_kernel((nx, ny), *refs),
-        out_shape=sds(1, dtype=jnp.int32), in_specs=[VMEM] * 2 + [ANY], out_specs=SMEM,
-        compiler_params=PARAMS, name="check",
-        cost_estimate=pl.CostEstimate(flops=2000000, bytes_accessed=800000, transcendentals=0),
-    )(halves, table, sent[0])
-
+    )(*pays[2:], *came_u, almost)
+    came_x = exchanged(sent, X_ORDER, nx, ny)
     result = pltpu.HBM((6, 1, CELLS), jnp.float32)
     writing = [pltpu.VMEM((8, CELLS), jnp.float32), pltpu.SemaphoreType.DMA((12,))]
 
@@ -671,10 +672,10 @@
         return pl.pallas_call(
             final_kernel, out_shape=result, in_specs=[VMEM] * 9, out_specs=HBM,
             scratch_shapes=writing, compiler_params=PARAMS, name="final",
-        )(route, plan, lines, inner, almost, *came_x, *came_u)
+        )(route, plan, lines, inner, almost, *came_u, *came_x)
 
     def general():
-        came = came_x + came_u
+        came = came_u + came_x
         state, base, base_lines = pl.pallas_call(
             base_kernel, out_shape=[wide, wide, four], in_specs=[VMEM] * 2, out_specs=[VMEM] * 3,
             compiler_params=PARAMS, name="base",
@@ -696,7 +697,7 @@
             scratch_shapes=writing, compiler_params=PARAMS, name="last",
         )(route, lines, own_two, nearly, *came_two)
 
-    out = lax.cond(flag[0] == 0, grid_like, general)
+    out = lax.switch(flag[0], [grid_like, general])
     return out.reshape(1, 6, CELLS)
 
 

time: 17.9 us -> 16.9 us (0.944)
  the two profiles are of different devices: /device:TPU:30 before, /device:TPU:1 now
where the time goes in v5:
time: 16.9 us; the launch traced here: 16.8 us
  starting transfers between devices  10.5 us (62%)
  Pallas kernels  4.35 us (26%)
  waiting for transfers between devices  1.18 us (7%)
  between operations  0.68 us (4%)
    ppermute x4, starting transfers between devices, exchanged(): lax.ppermute(pay, AXES, pairs_of(LINKS[link], nx, ny))  10.5 us
    pallas_call x1, Pallas kernels, on_device(): pl.pallas_call(lambda *refs: inner_kernel((nx, ny), *refs), out_shape=[wi...  1.94 us
    pallas_call x1, Pallas kernels, on_device(): pl.pallas_call(lambda *refs: load_kernel((nx, ny), *refs), out_shape=[sds...  1.25 us
    ppermute x4, waiting for transfers between devices, exchanged(): lax.ppermute(pay, AXES, pairs_of(LINKS[link], nx, ny))  1.18 us
    pallas_call x1, Pallas kernels, grid_like(): pl.pallas_call(final_kernel, out_shape=result, in_specs=[VMEM] * 9, out_s...  1.1 us
  transfers between devices with their start and end apart: 4, of which 2 were waited for; matrix products, arithmetic and copies ran while one was open for 0% of the time, Pallas kernels for 12%

profile of v5, /device:TPU:1, one launch (start us, length us, event | category | flops | bytes accessed | tf_op | source)
XLA Modules:
  0.0 16.8 jit_solution(9247321498816331888)
XLA Ops:
  0.0 1.2 %load.1 = (f32[8,8100]{1,0:T(8,128)S(1)}, s32[8,8100]{1,0:T(8,128)S(1)}, f32[32,128]{1,0:T(8,128)S(1)}, f32[32,128]{1,0:T(8,128)S(1)}, f32[16,128]{1,0:T(8,128)S...) custom-call(s32[256]{0:T(256)} %refs_0_.3, ...), custom_call_target="tpu_custom_call" | custom-call | tf_op jit(solution)/shard_map/load/pallas_call | solution.py:643
  1.3 7.8 %collective-permute-start.4 = (f32[16,128]{1,0:T(8,128)S(1)}, f32[16,128]{1,0:T(8,128)S(1)}, u32[]{:S(2)}, u32[]{:S(2)}) collective-permute-start(f32[16,128]{1,0:T(8,128)S(1)} %get-tuple-element.95), channel_id=1, source_target_pairs={{0,1},{1,0},{2,3},{3,2},{4,5},{5,4},{6,7},{7,6},{8,9},{9,8},{10,11... | collective-permute-start | bytes 24584 | tf_op jit(solution)/shard_map/ppermute | solution.py:78
  9.1 0.0 collective-permute-start.5
  9.1 1.9 %inner.1 = (f32[8,8192]{1,0:T(8,128)S(1)}, s32[16,128]{1,0:T(8,128)S(1)}, s32[1]{0:T(128)}) custom-call(s32[256]{0:T(256)} %refs_0_.3, s32[4,256]{1,0:T(4,128)} %bitcast.11, s32[4,256]{1,0:T(4,128)} %bitcast.13, f32[8,8100]{1,0:T(8,128)S(1)} %get-tuple-element.85.refs_3_, s32[8,8100]{1,0:T(8,128)S(1)} %get-tuple-element.86.refs_4_, ...), custom_call_target="tpu_custom_call" | custom-call | flops 2000000 | bytes 800000 | tf_op jit(solution)/shard_map/inner/pallas_call | solution.py:654
  11.0 0.0 collective-permute-done.4.came0
  11.0 0.8 %collective-permute-done.5.came1 = f32[16,128]{1,0:T(8,128)S(1)} collective-permute-done((f32[16,128]{1,0:T(8,128)S(1)}, f32[16,128]{1,0:T(8,128)S(1)}, u32[]{:S(2)}, u32[]{:S(2)}) %collective-permute-start.5) | collective-permute-done | bytes 8224 | tf_op jit(solution)/shard_map/ppermute | solution.py:78
  11.9 0.1 relay.1
  11.9 2.4 %collective-permute-start.6 = (f32[16,128]{1,0:T(8,128)S(1)}, f32[16,128]{1,0:T(8,128)S(1)}, u32[]{:S(2)}, u32[]{:S(2)}) collective-permute-start(f32[16,128]{1,0:T(8,128)S(1)} %get-tuple-element.99), channel_id=1, source_target_pairs={{0,240},{1,241},{2,242},{3,243},{4,244},{5,245},{6,246},{7,247},{8... | collective-permute-start | bytes 24584 | tf_op jit(solution)/shard_map/ppermute | solution.py:78
  14.3 0.3 %collective-permute-start.7 = (f32[16,128]{1,0:T(8,128)S(1)}, f32[16,128]{1,0:T(8,128)S(1)}, u32[]{:S(2)}, u32[]{:S(2)}) collective-permute-start(f32[16,128]{1,0:T(8,128)S(1)} %get-tuple-element.100), channel_id=1, source_target_pairs={{0,16},{1,17},{2,18},{3,19},{4,20},{5,21},{6,22},{7,23},{8,24},{9,... | collective-permute-start | bytes 24584 | tf_op jit(solution)/shard_map/ppermute | solution.py:78
  15.3 0.3 %collective-permute-done.6 = f32[16,128]{1,0:T(8,128)S(1)} collective-permute-done((f32[16,128]{1,0:T(8,128)S(1)}, f32[16,128]{1,0:T(8,128)S(1)}, u32[]{:S(2)}, u32[]{:S(2)}) %collective-permute-start.6) | collective-permute-done | bytes 8224 | tf_op jit(solution)/shard_map/ppermute | solution.py:78
  15.6 0.0 collective-permute-done.7
  15.6 1.1 %conditional.1 = (f32[1,6,8100]{2,0,1:T(1,128)}) conditional(s32[]{:T(128)} %bitcast.6, (s32[48,128]{1,0:T(8,128)S(1)}, s32[16,128]{1,0:T(8,128)S(1)}, f32[32,128]{1,0:T(8,128)S(1)}, f32[32,128]{1,0:T(8,128)S(1)}, f32[8,8192]{1,0:T(8,128)S(1)}, /*index=5*/f32[16,128]{1,0:T(8,128)S(1)}, f32[16,128]{1,0:T(8,128)S(1)}, f32[16,128]{1,0:T(8,128)S(1)}, ...), branch_computations={%region_0.0_spmd, %region_1.0_spmd} | conditional | flops 4000000 | bytes 1665704 | solution.py:700
  15.6 1.1 %final.1 = f32[6,1,8100]{2,1,0:T(1,128)} custom-call(s32[48,128]{1,0:T(8,128)S(1)} %get-tuple-element.43.route_ref, s32[16,128]{1,0:T(8,128)S(1)} %get-tuple-element.44.plan_ref, f32[32,128]{1,0:T(8,128)S(1)} %get-tuple-element.45.lines_ref, f32[32,128]{1,0:T(8,128)S(1)} %get-tuple-element.46.inner_ref, f32[8,8192]{1,0:T(8,128)S(1)} %get-tuple-element.47.almost_ref, ...), custom_call_target="tpu_custom_call" | custom-call | tf_op jit(solution)/shard_map/cond/branch_0_fun/final/pallas_call | solution.py:672
Async XLA Ops:
  1.3 9.8 %collective-permute-start.4 = (f32[16,128]{1,0:T(8,128)S(1)}, f32[16,128]{1,0:T(8,128)S(1)}, u32[]{:S(2)}, u32[]{:S(2)}) collective-permute-start(f32[16,128]{1,0:T(8,128)S(1)} %get-tuple-element.95), channel_id=1, source_target_pairs={{0,1},{1,0},{2,3},{3,2},{4,5},{5,4},{6,7},{7,6},{8,9},{9,8},{10,11... | collective-permute-start | bytes 24584 | tf_op jit(solution)/shard_map/ppermute | solution.py:78
  9.1 2.8 %collective-permute-start.5 = (f32[16,128]{1,0:T(8,128)S(1)}, f32[16,128]{1,0:T(8,128)S(1)}, u32[]{:S(2)}, u32[]{:S(2)}) collective-permute-start(f32[16,128]{1,0:T(8,128)S(1)} %get-tuple-element.96), channel_id=1, source_target_pairs={{0,128},{1,2},{2,1},{3,4},{4,3},{5,6},{6,5},{7,8},{8,7},{9,10},{10... | collective-permute-start | bytes 24584 | tf_op jit(solution)/shard_map/ppermute | solution.py:78
  11.9 3.7 %collective-permute-start.6 = (f32[16,128]{1,0:T(8,128)S(1)}, f32[16,128]{1,0:T(8,128)S(1)}, u32[]{:S(2)}, u32[]{:S(2)}) collective-permute-start(f32[16,128]{1,0:T(8,128)S(1)} %get-tuple-element.99), channel_id=1, source_target_pairs={{0,240},{1,241},{2,242},{3,243},{4,244},{5,245},{6,246},{7,247},{8... | collective-permute-start | bytes 24584 | tf_op jit(solution)/shard_map/ppermute | solution.py:78
  14.3 1.3 %collective-permute-start.7 = (f32[16,128]{1,0:T(8,128)S(1)}, f32[16,128]{1,0:T(8,128)S(1)}, u32[]{:S(2)}, u32[]{:S(2)}) collective-permute-start(f32[16,128]{1,0:T(8,128)S(1)} %get-tuple-element.100), channel_id=1, source_target_pairs={{0,16},{1,17},{2,18},{3,19},{4,20},{5,21},{6,22},{7,23},{8,24},{9,... | collective-permute-start | bytes 24584 | tf_op jit(solution)/shard_map/ppermute | solution.py:78

commit v6 on v5

--- a/solution.py
+++ b/solution.py
@@ -306,17 +306,15 @@
     return out
 
 
-def load_kernel(shape, tiles_hbm, halves_hbm, near_hbm, turn_hbm, fields_ref, wet_ref,
-                raw, wet_raw, lines_ref, inner_ref, pay0, pay1, pay2, pay3, route_ref, halves_ref, table_ref,
+def load_kernel(shape, tiles_hbm, near_hbm, turn_hbm, fields_ref, wet_ref,
+                raw, wet_raw, lines_ref, inner_ref, pay0, pay1, pay2, pay3, route_ref,
                 tiles_ref, near_ref, turn_ref, sems):
     nx, ny = shape
     tables = [pltpu.make_async_copy(tiles_hbm, tiles_ref, sems.at[7]),
               pltpu.make_async_copy(near_hbm, near_ref, sems.at[8]),
               pltpu.make_async_copy(turn_hbm, turn_ref, sems.at[9])]
-    copies = [pltpu.make_async_copy(fields_ref.at[c, 0], raw.at[c], sems.at[c]) for c in range(6)]
+    copies = [pltpu.make_async_copy(fields_ref.at[:, 0], raw.at[0:6], sems.at[0])]
     copies.append(pltpu.make_async_copy(wet_ref.at[0], wet_raw.at[0], sems.at[6]))
-    copies.append(pltpu.make_async_copy(halves_hbm, halves_ref, sems.at[10]))
-    copies.append(pltpu.make_async_copy(near_hbm, table_ref.at[0:4], sems.at[11]))
     for copy in tables + copies:
         copy.start()
     for copy in tables:
@@ -414,19 +412,21 @@
         base_lines_ref[8 * side:8 * side + 8, :] = lines[side]
 
 
-def inner_kernel(shape, tiles_hbm, near_hbm, turn_hbm, raw, wet_raw, route_ref, halves_ref, table_ref,
-                 almost_ref, plan_ref, flag, state_ref, tiles_ref, near_ref, turn_ref, sems):
+def inner_kernel(shape, tiles_hbm, near_hbm, turn_hbm, halves_hbm, raw, wet_raw, route_ref,
+                 almost_ref, plan_ref, flag, state_ref, tiles_ref, near_ref, turn_ref, halves_ref, table_ref, sems):
     copies = [pltpu.make_async_copy(tiles_hbm, tiles_ref, sems.at[0]),
               pltpu.make_async_copy(near_hbm, near_ref, sems.at[1]),
-              pltpu.make_async_copy(turn_hbm, turn_ref, sems.at[2])]
+              pltpu.make_async_copy(turn_hbm, turn_ref, sems.at[2]),
+              pltpu.make_async_copy(halves_hbm, halves_ref, sems.at[3]),
+              pltpu.make_async_copy(near_hbm, table_ref.at[0:4], sems.at[4])]
     for copy in copies:
         copy.start()
-    flag[0] = off_grid(shape, halves_ref, table_ref)
     state = masked_state(raw, wet_raw, state_ref)
     base, _ = without_rims(state)
     almost_ref[...] = base
     for copy in copies:
         copy.wait()
+    flag[0] = off_grid(shape, halves_ref, table_ref)
     corner_plan(shape, tiles_ref, near_ref, turn_ref, plan_ref)
     base = almost_ref[...]
     row = lax.broadcasted_iota(jnp.int32, (8, WIDE), 0)
@@ -564,9 +564,8 @@
             width = cut.stop - cut.start
             full[:, cut] = (almost_ref[:, c * LANES:(c + 1) * LANES] + (edges[c] + seconds[c]))[:, :width]
         cells = pl.ds(low * LANES, min(high * LANES, CELLS) - low * LANES)
-        for c in range(6):
-            copies.append(pltpu.make_async_copy(full.at[c, cells], out_ref.at[c, 0, cells], sems.at[len(copies)]))
-            copies[-1].start()
+        copies.append(pltpu.make_async_copy(full.at[0:6, cells], out_ref.at[:, 0, cells], sems.at[len(copies)]))
+        copies[-1].start()
     for copy in copies:
         copy.wait()
 
@@ -640,26 +639,26 @@
     tables = [pltpu.with_memory_space_constraint(v, pltpu.HBM) for v in (tile_of_slot, neighbor.T, rotation.T)]
     inputs = [pltpu.with_memory_space_constraint(v, pltpu.HBM) for v in (fields.reshape(6, 1, CELLS), wet_mask)]
     halves = pltpu.with_memory_space_constraint(tile_of_slot.reshape(2, LANES), pltpu.HBM)
-    raw, wet_raw, lines, inner, *pays, route, halves, table = pl.pallas_call(
+    raw, wet_raw, lines, inner, *pays, route = pl.pallas_call(
         lambda *refs: load_kernel((nx, ny), *refs),
         out_shape=[sds(8, CELLS), sds(8, CELLS, dtype=jnp.int32), four, four, pair, pair, pair, pair,
-                   sds(ROUTE, LANES, dtype=jnp.int32),
-                   sds(2, LANES, dtype=jnp.int32), sds(8, nx * ny, dtype=jnp.int32)],
-        in_specs=[HBM] * 6,
-        out_specs=[VMEM] * 11,
+                   sds(ROUTE, LANES, dtype=jnp.int32)],
+        in_specs=[HBM] * 5,
+        out_specs=[VMEM] * 9,
         scratch_shapes=[pltpu.SMEM((nx * ny,), jnp.int32), scalars, scalars, pltpu.SemaphoreType.DMA((12,))],
         compiler_params=PARAMS, name="load",
-    )(tables[0], halves, *tables[1:], *inputs)
+    )(*tables, *inputs)
     came_u = exchanged(pays[:2], U_ORDER, nx, ny)
     almost, plan, flag = pl.pallas_call(
         lambda *refs: inner_kernel((nx, ny), *refs),
         out_shape=[wide, sds(16, LANES, dtype=jnp.int32), sds(1, dtype=jnp.int32)],
-        in_specs=[HBM] * 3 + [VMEM] * 5, out_specs=[VMEM, VMEM, SMEM],
+        in_specs=[HBM] * 4 + [VMEM] * 3, out_specs=[VMEM, VMEM, SMEM],
         scratch_shapes=[pltpu.VMEM((8, WIDE), jnp.float32), pltpu.SMEM((nx * ny,), jnp.int32), scalars, scalars,
-                        pltpu.SemaphoreType.DMA((3,))],
+                        pltpu.VMEM((2, LANES), jnp.int32), pltpu.VMEM((8, nx * ny), jnp.int32),
+                        pltpu.SemaphoreType.DMA((5,))],
         compiler_params=PARAMS, name="inner",
         cost_estimate=pl.CostEstimate(flops=2000000, bytes_accessed=800000, transcendentals=0),
-    )(*tables, raw, wet_raw, route, halves, table)
+    )(*tables, halves, raw, wet_raw, route)
     sent = pl.pallas_call(
         relay_kernel, out_shape=[pair, pair], in_specs=[VMEM] * 4 + [ANY], out_specs=[VMEM] * 2,
         compiler_params=PARAMS, name="relay",

time: 16.9 us -> 16.7 us (0.988)
    pallas_call x1, Pallas kernels: 1.94 us -> 1.76 us  [on_device(): pl.pallas_call(lambda *refs: inner_kernel((nx, ny), *refs), out_shape=[wi...]
  transfers between devices with their start and end apart: 4 -> 4, of which waited for: 2 -> 2; matrix products, arithmetic and copies ran while one was open for 0% -> 0% of each run, Pallas kernels for 12% -> 11%
where the time goes in v6:
time: 16.7 us; the launch traced here: 16.6 us
  starting transfers between devices  10.5 us (63%)
  Pallas kernels  4.2 us (25%)
  waiting for transfers between devices  1.19 us (7%)
  between operations  0.68 us (4%)
    ppermute x4, starting transfers between devices, exchanged(): lax.ppermute(pay, AXES, pairs_of(LINKS[link], nx, ny))  10.5 us
    pallas_call x1, Pallas kernels, on_device(): pl.pallas_call(lambda *refs: inner_kernel((nx, ny), *refs), out_shape=[wi...  1.76 us
    pallas_call x1, Pallas kernels, on_device(): pl.pallas_call(lambda *refs: load_kernel((nx, ny), *refs), out_shape=[sds...  1.25 us
    ppermute x4, waiting for transfers between devices, exchanged(): lax.ppermute(pay, AXES, pairs_of(LINKS[link], nx, ny))  1.19 us
    pallas_call x1, Pallas kernels, grid_like(): pl.pallas_call(final_kernel, out_shape=result, in_specs=[VMEM] * 9, out_s...  1.11 us
  transfers between devices with their start and end apart: 4, of which 2 were waited for; matrix products, arithmetic and copies ran while one was open for 0% of the time, Pallas kernels for 11%

profile of v6, /device:TPU:1, one launch (start us, length us, event | category | flops | bytes accessed | tf_op | source)
XLA Modules:
  0.0 16.6 jit_solution(7959684590874437931)
XLA Ops:
  0.0 1.2 %load.1 = (f32[8,8100]{1,0:T(8,128)S(1)}, s32[8,8100]{1,0:T(8,128)S(1)}, f32[32,128]{1,0:T(8,128)S(1)}, f32[32,128]{1,0:T(8,128)S(1)}, f32[16,128]{1,0:T(8,128)S...) custom-call(s32[256]{0:T(256)} %refs_0_.3, ...), custom_call_target="tpu_custom_call" | custom-call | tf_op jit(solution)/shard_map/load/pallas_call | solution.py:642
  1.3 7.8 %collective-permute-start.4 = (f32[16,128]{1,0:T(8,128)S(1)}, f32[16,128]{1,0:T(8,128)S(1)}, u32[]{:S(2)}, u32[]{:S(2)}) collective-permute-start(f32[16,128]{1,0:T(8,128)S(1)} %get-tuple-element.91), channel_id=1, source_target_pairs={{0,1},{1,0},{2,3},{3,2},{4,5},{5,4},{6,7},{7,6},{8,9},{9,8},{10,11... | collective-permute-start | bytes 24584 | tf_op jit(solution)/shard_map/ppermute | solution.py:78
  9.1 0.0 collective-permute-start.5
  9.1 1.8 %inner.1 = (f32[8,8192]{1,0:T(8,128)S(1)}, s32[16,128]{1,0:T(8,128)S(1)}, s32[1]{0:T(128)}) custom-call(s32[256]{0:T(256)} %refs_0_.3, s32[4,256]{1,0:T(4,128)} %bitcast.11, s32[4,256]{1,0:T(4,128)} %bitcast.13, s32[2,128]{1,0:T(2,128)} %bitcast.14, f32[8,8100]{1,0:T(8,128)S(1)} %get-tuple-element.83.refs_4_, s32[8,8100]{1,0:T(8,128)S(1)} %get-tuple-element.84.refs_5_, ...), custom_call_target="tpu_custom_call" | custom-call | flops 2000000 | bytes 800000 | tf_op jit(solution)/shard_map/inner/pallas_call | solution.py:652
  10.9 0.0 collective-permute-done.4.came0
  10.9 1.0 %collective-permute-done.5.came1 = f32[16,128]{1,0:T(8,128)S(1)} collective-permute-done((f32[16,128]{1,0:T(8,128)S(1)}, f32[16,128]{1,0:T(8,128)S(1)}, u32[]{:S(2)}, u32[]{:S(2)}) %collective-permute-start.5) | collective-permute-done | bytes 8224 | tf_op jit(solution)/shard_map/ppermute | solution.py:78
  11.9 0.1 relay.1
  12.0 2.2 %collective-permute-start.6 = (f32[16,128]{1,0:T(8,128)S(1)}, f32[16,128]{1,0:T(8,128)S(1)}, u32[]{:S(2)}, u32[]{:S(2)}) collective-permute-start(f32[16,128]{1,0:T(8,128)S(1)} %get-tuple-element.95), channel_id=1, source_target_pairs={{0,240},{1,241},{2,242},{3,243},{4,244},{5,245},{6,246},{7,247},{8... | collective-permute-start | bytes 24584 | tf_op jit(solution)/shard_map/ppermute | solution.py:78
  14.1 0.5 %collective-permute-start.7 = (f32[16,128]{1,0:T(8,128)S(1)}, f32[16,128]{1,0:T(8,128)S(1)}, u32[]{:S(2)}, u32[]{:S(2)}) collective-permute-start(f32[16,128]{1,0:T(8,128)S(1)} %get-tuple-element.96), channel_id=1, source_target_pairs={{0,16},{1,17},{2,18},{3,19},{4,20},{5,21},{6,22},{7,23},{8,24},{9,... | collective-permute-start | bytes 24584 | tf_op jit(solution)/shard_map/ppermute | solution.py:78
  15.3 0.2 collective-permute-done.6
  15.5 0.0 collective-permute-done.7
  15.5 1.1 %conditional.1 = (f32[1,6,8100]{2,0,1:T(1,128)}) conditional(s32[]{:T(128)} %bitcast.6, (s32[48,128]{1,0:T(8,128)S(1)}, s32[16,128]{1,0:T(8,128)S(1)}, f32[32,128]{1,0:T(8,128)S(1)}, f32[32,128]{1,0:T(8,128)S(1)}, f32[8,8192]{1,0:T(8,128)S(1)}, /*index=5*/f32[16,128]{1,0:T(8,128)S(1)}, f32[16,128]{1,0:T(8,128)S(1)}, f32[16,128]{1,0:T(8,128)S(1)}, ...), branch_computations={%region_0.0_spmd, %region_1.0_spmd} | conditional | flops 4000000 | bytes 1665704 | solution.py:699
  15.5 1.1 %final.1 = f32[6,1,8100]{2,1,0:T(1,128)} custom-call(s32[48,128]{1,0:T(8,128)S(1)} %get-tuple-element.43.route_ref, s32[16,128]{1,0:T(8,128)S(1)} %get-tuple-element.44.plan_ref, f32[32,128]{1,0:T(8,128)S(1)} %get-tuple-element.45.lines_ref, f32[32,128]{1,0:T(8,128)S(1)} %get-tuple-element.46.inner_ref, f32[8,8192]{1,0:T(8,128)S(1)} %get-tuple-element.47.almost_ref, ...), custom_call_target="tpu_custom_call" | custom-call | tf_op jit(solution)/shard_map/cond/branch_0_fun/final/pallas_call | solution.py:671
Async XLA Ops:
  1.3 9.6 %collective-permute-start.4 = (f32[16,128]{1,0:T(8,128)S(1)}, f32[16,128]{1,0:T(8,128)S(1)}, u32[]{:S(2)}, u32[]{:S(2)}) collective-permute-start(f32[16,128]{1,0:T(8,128)S(1)} %get-tuple-element.91), channel_id=1, source_target_pairs={{0,1},{1,0},{2,3},{3,2},{4,5},{5,4},{6,7},{7,6},{8,9},{9,8},{10,11... | collective-permute-start | bytes 24584 | tf_op jit(solution)/shard_map/ppermute | solution.py:78
  9.1 2.8 %collective-permute-start.5 = (f32[16,128]{1,0:T(8,128)S(1)}, f32[16,128]{1,0:T(8,128)S(1)}, u32[]{:S(2)}, u32[]{:S(2)}) collective-permute-start(f32[16,128]{1,0:T(8,128)S(1)} %get-tuple-element.92), channel_id=1, source_target_pairs={{0,128},{1,2},{2,1},{3,4},{4,3},{5,6},{6,5},{7,8},{8,7},{9,10},{10... | collective-permute-start | bytes 24584 | tf_op jit(solution)/shard_map/ppermute | solution.py:78
  12.0 3.5 %collective-permute-start.6 = (f32[16,128]{1,0:T(8,128)S(1)}, f32[16,128]{1,0:T(8,128)S(1)}, u32[]{:S(2)}, u32[]{:S(2)}) collective-permute-start(f32[16,128]{1,0:T(8,128)S(1)} %get-tuple-element.95), channel_id=1, source_target_pairs={{0,240},{1,241},{2,242},{3,243},{4,244},{5,245},{6,246},{7,247},{8... | collective-permute-start | bytes 24584 | tf_op jit(solution)/shard_map/ppermute | solution.py:78
  14.1 1.3 %collective-permute-start.7 = (f32[16,128]{1,0:T(8,128)S(1)}, f32[16,128]{1,0:T(8,128)S(1)}, u32[]{:S(2)}, u32[]{:S(2)}) collective-permute-start(f32[16,128]{1,0:T(8,128)S(1)} %get-tuple-element.96), channel_id=1, source_target_pairs={{0,16},{1,17},{2,18},{3,19},{4,20},{5,21},{6,22},{7,23},{8,24},{9,... | collective-permute-start | bytes 24584 | tf_op jit(solution)/shard_map/ppermute | solution.py:78

commit v7 on v6

--- a/solution.py
+++ b/solution.py
@@ -517,19 +517,24 @@
     ]
 
 
+def pressure_at(tracer, shift, row):
+    return GRAVITY * (pltpu.roll(tracer, shift, 0)
+                      + jnp.where(row == (5 + shift) % 8, pltpu.roll(tracer, shift + 1, 0), 0.0))
+
+
 def final_kernel(route_ref, plan_ref, lines_ref, inner_ref, almost_ref, first, second, third, fourth, out_ref, full, sems):
     lane, row = lanes(), rows()
     route, plan = Rows(route_ref), Rows(plan_ref)
     came = by_link((first, second, third, fourth), BOTH)
-    outer = []
-    for link in range(4):
-        line = came[link][0:8, :]
-        for end, lane_to in ((0, LANES - 1), (1, TILE)):
+    outer = [came[link][0:8, :] for link in range(4)]
+    ends = []
+    for end in range(2):
+        values = []
+        for link in range(4):
             which, lane_from = plan[2 * (2 * link + end)], plan[2 * (2 * link + end) + 1]
-            held = jnp.where(which == 2, came[3][0:8, :], came[1][0:8, :])
-            value = pick(held, lane_from)
-            line = jnp.where(lane == lane_to, jnp.where(which > 0, value, 0.0), line)
-        outer.append(line)
+            held = jnp.where(which == 2, outer[3], outer[1])
+            values.append(jnp.where(which > 0, pick(held, lane_from), 0.0))
+        ends.append(rims_of(route, None, values))
     rims = rims_of(route, None, outer)
     beyond = rims_of(route, None, [came[link][8:16, :] for link in range(4)])
     lines, inner = four_of(lines_ref), four_of(inner_ref)
@@ -539,23 +544,24 @@
     for side in range(4):
         sign = 1.0 if side in (1, 2) else -1.0
         line, wet, wet_in = rims[side], wet_rows(lines[side]), wet_rows(inner[side])
-        after, before = pltpu.roll(line, LANES - 1, 1), pltpu.roll(line, 1, 1)
-        first, second = pltpu.roll(line, 4, 0), pltpu.roll(line, 2, 0)
-        normal, tangent = (first, second) if side % 2 == 1 else (second, first)
+        after = jnp.where(lane == TILE - 1, ends[1][side], pltpu.roll(line, LANES - 1, 1))
+        before = jnp.where(lane == 0, ends[0][side], pltpu.roll(line, 1, 1))
+        upper, lower = pltpu.roll(line, 4, 0), pltpu.roll(line, 2, 0)
+        normal, tangent = (upper, lower) if side % 2 == 1 else (lower, upper)
         along = normal * (sign * (beyond[side] - lines[side])) + tangent * (after - before)
         round_sum = after + before + beyond[side] + lines[side] - 4.0 * line
         tracer = wet_rows(line) * (line - (0.5 * ADVECT) * along + DIFFUSE * round_sum)
-        far = pressure_of(tracer, row)
-        mine = jnp.where(lane < TILE, pressure_of(whole[side], row), 0.0)
-        drop = pltpu.roll(mine, LANES - 1, 1) - pltpu.roll(mine, 1, 1)
+        mine = jnp.where(lane < TILE, whole[side], 0.0)
         to_normal, to_tangent = (4, 6) if side % 2 == 1 else (6, 4)
         own_row = row < 2 if side % 2 == 1 else (row >= 2) & (row < 4)
         cross_row = (row >= 2) & (row < 4) if side % 2 == 1 else row < 2
-        push = jnp.where(own_row, sign * pltpu.roll(far, to_normal, 0), 0.0)
-        push = jnp.where(cross_row, pltpu.roll(drop, to_tangent, 0), push)
+        cross = pressure_at(mine, to_tangent, row)
+        drop = pltpu.roll(cross, LANES - 1, 1) - pltpu.roll(cross, 1, 1)
+        push = jnp.where(own_row, sign * pressure_at(tracer, to_normal, row), 0.0)
+        push = jnp.where(cross_row, drop, push)
         on_edge.append(patch[side] - (0.5 * STEP_SIZE) * wet * push)
         kept = own_row & (lane > 0) & (lane < TILE - 1)
-        inside.append(jnp.where(kept, (-sign * 0.5 * STEP_SIZE) * wet_in * pltpu.roll(mine, to_normal, 0), 0.0))
+        inside.append(jnp.where(kept, (-sign * 0.5 * STEP_SIZE) * wet_in * pressure_at(mine, to_normal, row), 0.0))
     edges, seconds = spread_chunks(on_edge, 0), spread_chunks(inside, 1)
     copies = []
     for low, high in ((0, 24), (24, CHUNKS)):

time: 16.7 us -> 16.7 us (level)
  no operation moved by 1% of the time
where the time goes in v7:
time: 16.7 us; the launch traced here: 16.5 us
  starting transfers between devices  10.5 us (63%)
  Pallas kernels  4.11 us (25%)
  waiting for transfers between devices  1.19 us (7%)
  between operations  0.68 us (4%)
    ppermute x4, starting transfers between devices, exchanged(): lax.ppermute(pay, AXES, pairs_of(LINKS[link], nx, ny))  10.5 us
    pallas_call x1, Pallas kernels, on_device(): pl.pallas_call(lambda *refs: inner_kernel((nx, ny), *refs), out_shape=[wi...  1.76 us
    pallas_call x1, Pallas kernels, on_device(): pl.pallas_call(lambda *refs: load_kernel((nx, ny), *refs), out_shape=[sds...  1.25 us
    ppermute x4, waiting for transfers between devices, exchanged(): lax.ppermute(pay, AXES, pairs_of(LINKS[link], nx, ny))  1.19 us
    pallas_call x1, Pallas kernels, grid_like(): pl.pallas_call(final_kernel, out_shape=result, in_specs=[VMEM] * 9, out_s...  1.03 us
  transfers between devices with their start and end apart: 4, of which 2 were waited for; matrix products, arithmetic and copies ran while one was open for 0% of the time, Pallas kernels for 11%

profile of v7, /device:TPU:1, one launch (start us, length us, event | category | flops | bytes accessed | tf_op | source)
XLA Modules:
  0.0 16.5 jit_solution(1386299589346769381)
XLA Ops:
  0.0 1.2 %load.1 = (f32[8,8100]{1,0:T(8,128)S(1)}, s32[8,8100]{1,0:T(8,128)S(1)}, f32[32,128]{1,0:T(8,128)S(1)}, f32[32,128]{1,0:T(8,128)S(1)}, f32[16,128]{1,0:T(8,128)S...) custom-call(s32[256]{0:T(256)} %refs_0_.3, ...), custom_call_target="tpu_custom_call" | custom-call | tf_op jit(solution)/shard_map/load/pallas_call | solution.py:648
  1.3 7.8 %collective-permute-start.4 = (f32[16,128]{1,0:T(8,128)S(1)}, f32[16,128]{1,0:T(8,128)S(1)}, u32[]{:S(2)}, u32[]{:S(2)}) collective-permute-start(f32[16,128]{1,0:T(8,128)S(1)} %get-tuple-element.91), channel_id=1, source_target_pairs={{0,1},{1,0},{2,3},{3,2},{4,5},{5,4},{6,7},{7,6},{8,9},{9,8},{10,11... | collective-permute-start | bytes 24584 | tf_op jit(solution)/shard_map/ppermute | solution.py:78
  9.1 0.0 collective-permute-start.5
  9.1 1.8 %inner.1 = (f32[8,8192]{1,0:T(8,128)S(1)}, s32[16,128]{1,0:T(8,128)S(1)}, s32[1]{0:T(128)}) custom-call(s32[256]{0:T(256)} %refs_0_.3, s32[4,256]{1,0:T(4,128)} %bitcast.11, s32[4,256]{1,0:T(4,128)} %bitcast.13, s32[2,128]{1,0:T(2,128)} %bitcast.14, f32[8,8100]{1,0:T(8,128)S(1)} %get-tuple-element.83.refs_4_, s32[8,8100]{1,0:T(8,128)S(1)} %get-tuple-element.84.refs_5_, ...), custom_call_target="tpu_custom_call" | custom-call | flops 2000000 | bytes 800000 | tf_op jit(solution)/shard_map/inner/pallas_call | solution.py:658
  10.9 0.0 collective-permute-done.4.came0
  10.9 1.0 %collective-permute-done.5.came1 = f32[16,128]{1,0:T(8,128)S(1)} collective-permute-done((f32[16,128]{1,0:T(8,128)S(1)}, f32[16,128]{1,0:T(8,128)S(1)}, u32[]{:S(2)}, u32[]{:S(2)}) %collective-permute-start.5) | collective-permute-done | bytes 8224 | tf_op jit(solution)/shard_map/ppermute | solution.py:78
  11.9 0.1 relay.1
  12.0 2.2 %collective-permute-start.6 = (f32[16,128]{1,0:T(8,128)S(1)}, f32[16,128]{1,0:T(8,128)S(1)}, u32[]{:S(2)}, u32[]{:S(2)}) collective-permute-start(f32[16,128]{1,0:T(8,128)S(1)} %get-tuple-element.95), channel_id=1, source_target_pairs={{0,240},{1,241},{2,242},{3,243},{4,244},{5,245},{6,246},{7,247},{8... | collective-permute-start | bytes 24584 | tf_op jit(solution)/shard_map/ppermute | solution.py:78
  14.1 0.5 %collective-permute-start.7 = (f32[16,128]{1,0:T(8,128)S(1)}, f32[16,128]{1,0:T(8,128)S(1)}, u32[]{:S(2)}, u32[]{:S(2)}) collective-permute-start(f32[16,128]{1,0:T(8,128)S(1)} %get-tuple-element.96), channel_id=1, source_target_pairs={{0,16},{1,17},{2,18},{3,19},{4,20},{5,21},{6,22},{7,23},{8,24},{9,... | collective-permute-start | bytes 24584 | tf_op jit(solution)/shard_map/ppermute | solution.py:78
  15.3 0.2 collective-permute-done.6
  15.5 0.0 collective-permute-done.7
  15.5 1.0 %conditional.1 = (f32[1,6,8100]{2,0,1:T(1,128)}) conditional(s32[]{:T(128)} %bitcast.6, (s32[48,128]{1,0:T(8,128)S(1)}, s32[16,128]{1,0:T(8,128)S(1)}, f32[32,128]{1,0:T(8,128)S(1)}, f32[32,128]{1,0:T(8,128)S(1)}, f32[8,8192]{1,0:T(8,128)S(1)}, /*index=5*/f32[16,128]{1,0:T(8,128)S(1)}, f32[16,128]{1,0:T(8,128)S(1)}, f32[16,128]{1,0:T(8,128)S(1)}, ...), branch_computations={%region_0.0_spmd, %region_1.0_spmd} | conditional | flops 4000000 | bytes 1665704 | solution.py:705
  15.5 1.0 %final.1 = f32[6,1,8100]{2,1,0:T(1,128)} custom-call(s32[48,128]{1,0:T(8,128)S(1)} %get-tuple-element.43.route_ref, s32[16,128]{1,0:T(8,128)S(1)} %get-tuple-element.44.plan_ref, f32[32,128]{1,0:T(8,128)S(1)} %get-tuple-element.45.lines_ref, f32[32,128]{1,0:T(8,128)S(1)} %get-tuple-element.46.inner_ref, f32[8,8192]{1,0:T(8,128)S(1)} %get-tuple-element.47.almost_ref, ...), custom_call_target="tpu_custom_call" | custom-call | tf_op jit(solution)/shard_map/cond/branch_0_fun/final/pallas_call | solution.py:677
Async XLA Ops:
  1.3 9.6 %collective-permute-start.4 = (f32[16,128]{1,0:T(8,128)S(1)}, f32[16,128]{1,0:T(8,128)S(1)}, u32[]{:S(2)}, u32[]{:S(2)}) collective-permute-start(f32[16,128]{1,0:T(8,128)S(1)} %get-tuple-element.91), channel_id=1, source_target_pairs={{0,1},{1,0},{2,3},{3,2},{4,5},{5,4},{6,7},{7,6},{8,9},{9,8},{10,11... | collective-permute-start | bytes 24584 | tf_op jit(solution)/shard_map/ppermute | solution.py:78
  9.1 2.8 %collective-permute-start.5 = (f32[16,128]{1,0:T(8,128)S(1)}, f32[16,128]{1,0:T(8,128)S(1)}, u32[]{:S(2)}, u32[]{:S(2)}) collective-permute-start(f32[16,128]{1,0:T(8,128)S(1)} %get-tuple-element.92), channel_id=1, source_target_pairs={{0,128},{1,2},{2,1},{3,4},{4,3},{5,6},{6,5},{7,8},{8,7},{9,10},{10... | collective-permute-start | bytes 24584 | tf_op jit(solution)/shard_map/ppermute | solution.py:78
  12.0 3.5 %collective-permute-start.6 = (f32[16,128]{1,0:T(8,128)S(1)}, f32[16,128]{1,0:T(8,128)S(1)}, u32[]{:S(2)}, u32[]{:S(2)}) collective-permute-start(f32[16,128]{1,0:T(8,128)S(1)} %get-tuple-element.95), channel_id=1, source_target_pairs={{0,240},{1,241},{2,242},{3,243},{4,244},{5,245},{6,246},{7,247},{8... | collective-permute-start | bytes 24584 | tf_op jit(solution)/shard_map/ppermute | solution.py:78
  14.1 1.3 %collective-permute-start.7 = (f32[16,128]{1,0:T(8,128)S(1)}, f32[16,128]{1,0:T(8,128)S(1)}, u32[]{:S(2)}, u32[]{:S(2)}) collective-permute-start(f32[16,128]{1,0:T(8,128)S(1)} %get-tuple-element.96), channel_id=1, source_target_pairs={{0,16},{1,17},{2,18},{3,19},{4,20},{5,21},{6,22},{7,23},{8,24},{9,... | collective-permute-start | bytes 24584 | tf_op jit(solution)/shard_map/ppermute | solution.py:78

commit v8 on v7

--- a/solution.py
+++ b/solution.py
@@ -26,6 +26,14 @@
 HBM = pl.BlockSpec(memory_space=pltpu.HBM)
 
 
+def over(value, count):
+    return value >> (count.bit_length() - 1) if count & (count - 1) == 0 else value // count
+
+
+def rest(value, count):
+    return value & (count - 1) if count & (count - 1) == 0 else value % count
+
+
 def link_x_even(x, y, nx, ny):
     return x ^ 1, y
 
@@ -45,7 +53,8 @@
 
 
 def swapped(x, nx):
-    return (x % (nx // 2) == 0) | (x % (nx // 2) == 2)
+    column = rest(x, nx // 2)
+    return (column == 0) | (column == 2)
 
 
 def link_u_first(x, y, nx, ny):
@@ -83,14 +92,14 @@
 
 
 def partner(me, which, nx, ny):
-    x, y = me // ny, me % ny
+    x, y = over(me, ny), rest(me, ny)
     if which == 1:
-        return me + jnp.where(x % 2 == 0, ny, -ny)
+        return me + jnp.where(rest(x, 2) == 0, ny, -ny)
     if which == 3:
-        return (x + jnp.where(x % 2 == 1, 1, nx - 1)) % nx * ny + y
-    even = me + jnp.where(y % 2 == 0, 1, -1)
+        return rest(me + jnp.where(rest(x, 2) == 1, ny, (nx - 1) * ny), nx * ny)
+    even = me + jnp.where(rest(y, 2) == 0, 1, -1)
     pole = (y == 0) | (y == ny - 1)
-    odd = jnp.where(pole, (x + nx // 2) % nx * ny + y, me + jnp.where(y % 2 == 1, 1, -1))
+    odd = jnp.where(pole, rest(me + nx // 2 * ny, nx * ny), me + jnp.where(rest(y, 2) == 1, 1, -1))
     return jnp.where(swapped(x, nx), even, odd) if which == 0 else jnp.where(swapped(x, nx), odd, even)
 
 
@@ -331,11 +340,11 @@
         for side in range(4):
             route[4 * link + side] = jnp.where((near[side] >= 0) & (near[side] == other), 1, 0)
     for side in range(4):
-        target = (side + 2 + turn[side]) % 4
+        target = (side + 2 + turn[side]) & 3
         for k in range(4):
             route[16 + 4 * side + k] = jnp.where((near[side] >= 0) & (near[side] == tile) & (target == k), 1, 0)
         route[32 + side] = jnp.where((target < 2) != (side >= 2), 1, 0)
-        route[36 + side] = (4 - turn[side]) % 4
+        route[36 + side] = (4 - turn[side]) & 3
     route[40] = jnp.where(live, 1, 0)
     for i in range(41):
         route_ref[i:i + 1, :] = jnp.full((1, LANES), route[i], jnp.int32)
@@ -469,14 +478,14 @@
         side = jnp.int32(-1)
         for k in range(4):
             side = jnp.where((tile >= 0) & (other >= 0) & (near_ref[k, held] == other), k, side)
-        facing = (side + 2 + turn_ref[jnp.maximum(side, 0), held]) % 4
+        facing = (side + 2 + turn_ref[jnp.maximum(side, 0), held]) & 3
         there = jnp.maximum(other, 0)
         for end in range(2):
             later = (side < 2) == (end == 0)
-            lateral = jnp.where(later, facing + 1, facing + 3) % 4
+            lateral = jnp.where(later, facing + 1, facing + 3) & 3
             beyond = jnp.where(side >= 0, near_ref[lateral, there], -1)
-            back = (lateral + 2 + turn_ref[lateral, there]) % 4
-            corner = jnp.where(later, back + 1, back) % 4
+            back = (lateral + 2 + turn_ref[lateral, there]) & 3
+            corner = jnp.where(later, back + 1, back) & 3
             buffer, lane = jnp.int32(0), jnp.int32(0)
             for which, base, name in relayed:
                 here = (beyond >= 0) & (beyond == name)

time: 16.7 us -> 16.7 us (level)
  transfers between devices with their start and end apart: 4 -> 4, of which waited for: 2 -> 3; matrix products, arithmetic and copies ran while one was open for 0% -> 0% of each run, Pallas kernels for 11% -> 10%
where the time goes in v8:
time: 16.7 us; the launch traced here: 16.5 us
  starting transfers between devices  10.5 us (63%)
  Pallas kernels  4.07 us (24%)
  waiting for transfers between devices  1.23 us (7%)
  between operations  0.68 us (4%)
    ppermute x4, starting transfers between devices, exchanged(): lax.ppermute(pay, AXES, pairs_of(LINKS[link], nx, ny))  10.5 us
    pallas_call x1, Pallas kernels, on_device(): pl.pallas_call(lambda *refs: inner_kernel((nx, ny), *refs), out_shape=[wi...  1.72 us
    pallas_call x1, Pallas kernels, on_device(): pl.pallas_call(lambda *refs: load_kernel((nx, ny), *refs), out_shape=[sds...  1.25 us
    ppermute x4, waiting for transfers between devices, exchanged(): lax.ppermute(pay, AXES, pairs_of(LINKS[link], nx, ny))  1.23 us
    pallas_call x1, Pallas kernels, grid_like(): pl.pallas_call(final_kernel, out_shape=result, in_specs=[VMEM] * 9, out_s...  1.03 us
  transfers between devices with their start and end apart: 4, of which 3 were waited for; matrix products, arithmetic and copies ran while one was open for 0% of the time, Pallas kernels for 10%

profile of v8, /device:TPU:1, one launch (start us, length us, event | category | flops | bytes accessed | tf_op | source)
XLA Modules:
  0.0 16.5 jit_solution(17652329469502337352)
XLA Ops:
  0.0 1.2 %load.1 = (f32[8,8100]{1,0:T(8,128)S(1)}, s32[8,8100]{1,0:T(8,128)S(1)}, f32[32,128]{1,0:T(8,128)S(1)}, f32[32,128]{1,0:T(8,128)S(1)}, f32[16,128]{1,0:T(8,128)S...) custom-call(s32[256]{0:T(256)} %refs_0_.3, ...), custom_call_target="tpu_custom_call" | custom-call | tf_op jit(solution)/shard_map/load/pallas_call | solution.py:657
  1.3 7.8 %collective-permute-start.4 = (f32[16,128]{1,0:T(8,128)S(1)}, f32[16,128]{1,0:T(8,128)S(1)}, u32[]{:S(2)}, u32[]{:S(2)}) collective-permute-start(f32[16,128]{1,0:T(8,128)S(1)} %get-tuple-element.91), channel_id=1, source_target_pairs={{0,1},{1,0},{2,3},{3,2},{4,5},{5,4},{6,7},{7,6},{8,9},{9,8},{10,11... | collective-permute-start | bytes 24584 | tf_op jit(solution)/shard_map/ppermute | solution.py:87
  9.1 0.0 collective-permute-start.5
  9.1 1.7 %inner.1 = (f32[8,8192]{1,0:T(8,128)S(1)}, s32[16,128]{1,0:T(8,128)S(1)}, s32[1]{0:T(128)}) custom-call(s32[256]{0:T(256)} %refs_0_.3, s32[4,256]{1,0:T(4,128)} %bitcast.11, s32[4,256]{1,0:T(4,128)} %bitcast.13, s32[2,128]{1,0:T(2,128)} %bitcast.14, f32[8,8100]{1,0:T(8,128)S(1)} %get-tuple-element.83.refs_4_, s32[8,8100]{1,0:T(8,128)S(1)} %get-tuple-element.84.refs_5_, ...), custom_call_target="tpu_custom_call" | custom-call | flops 2000000 | bytes 800000 | tf_op jit(solution)/shard_map/inner/pallas_call | solution.py:667
  10.8 0.0 collective-permute-done.4.came0
  10.8 1.1 %collective-permute-done.5.came1 = f32[16,128]{1,0:T(8,128)S(1)} collective-permute-done((f32[16,128]{1,0:T(8,128)S(1)}, f32[16,128]{1,0:T(8,128)S(1)}, u32[]{:S(2)}, u32[]{:S(2)}) %collective-permute-start.5) | collective-permute-done | bytes 8224 | tf_op jit(solution)/shard_map/ppermute | solution.py:87
  11.9 0.1 relay.1
  12.0 2.1 %collective-permute-start.6 = (f32[16,128]{1,0:T(8,128)S(1)}, f32[16,128]{1,0:T(8,128)S(1)}, u32[]{:S(2)}, u32[]{:S(2)}) collective-permute-start(f32[16,128]{1,0:T(8,128)S(1)} %get-tuple-element.95), channel_id=1, source_target_pairs={{0,240},{1,241},{2,242},{3,243},{4,244},{5,245},{6,246},{7,247},{8... | collective-permute-start | bytes 24584 | tf_op jit(solution)/shard_map/ppermute | solution.py:87
  14.1 0.6 %collective-permute-start.7 = (f32[16,128]{1,0:T(8,128)S(1)}, f32[16,128]{1,0:T(8,128)S(1)}, u32[]{:S(2)}, u32[]{:S(2)}) collective-permute-start(f32[16,128]{1,0:T(8,128)S(1)} %get-tuple-element.96), channel_id=1, source_target_pairs={{0,16},{1,17},{2,18},{3,19},{4,20},{5,21},{6,22},{7,23},{8,24},{9,... | collective-permute-start | bytes 24584 | tf_op jit(solution)/shard_map/ppermute | solution.py:87
  15.3 0.1 collective-permute-done.6
  15.4 0.1 collective-permute-done.7
  15.5 1.0 %conditional.1 = (f32[1,6,8100]{2,0,1:T(1,128)}) conditional(s32[]{:T(128)} %bitcast.6, (s32[48,128]{1,0:T(8,128)S(1)}, s32[16,128]{1,0:T(8,128)S(1)}, f32[32,128]{1,0:T(8,128)S(1)}, f32[32,128]{1,0:T(8,128)S(1)}, f32[8,8192]{1,0:T(8,128)S(1)}, /*index=5*/f32[16,128]{1,0:T(8,128)S(1)}, f32[16,128]{1,0:T(8,128)S(1)}, f32[16,128]{1,0:T(8,128)S(1)}, ...), branch_computations={%region_0.0_spmd, %region_1.0_spmd} | conditional | flops 4000000 | bytes 1665704 | solution.py:714
  15.5 1.0 %final.1 = f32[6,1,8100]{2,1,0:T(1,128)} custom-call(s32[48,128]{1,0:T(8,128)S(1)} %get-tuple-element.43.route_ref, s32[16,128]{1,0:T(8,128)S(1)} %get-tuple-element.44.plan_ref, f32[32,128]{1,0:T(8,128)S(1)} %get-tuple-element.45.lines_ref, f32[32,128]{1,0:T(8,128)S(1)} %get-tuple-element.46.inner_ref, f32[8,8192]{1,0:T(8,128)S(1)} %get-tuple-element.47.almost_ref, ...), custom_call_target="tpu_custom_call" | custom-call | tf_op jit(solution)/shard_map/cond/branch_0_fun/final/pallas_call | solution.py:686
Async XLA Ops:
  1.3 9.6 %collective-permute-start.4 = (f32[16,128]{1,0:T(8,128)S(1)}, f32[16,128]{1,0:T(8,128)S(1)}, u32[]{:S(2)}, u32[]{:S(2)}) collective-permute-start(f32[16,128]{1,0:T(8,128)S(1)} %get-tuple-element.91), channel_id=1, source_target_pairs={{0,1},{1,0},{2,3},{3,2},{4,5},{5,4},{6,7},{7,6},{8,9},{9,8},{10,11... | collective-permute-start | bytes 24584 | tf_op jit(solution)/shard_map/ppermute | solution.py:87
  9.1 2.8 %collective-permute-start.5 = (f32[16,128]{1,0:T(8,128)S(1)}, f32[16,128]{1,0:T(8,128)S(1)}, u32[]{:S(2)}, u32[]{:S(2)}) collective-permute-start(f32[16,128]{1,0:T(8,128)S(1)} %get-tuple-element.92), channel_id=1, source_target_pairs={{0,128},{1,2},{2,1},{3,4},{4,3},{5,6},{6,5},{7,8},{8,7},{9,10},{10... | collective-permute-start | bytes 24584 | tf_op jit(solution)/shard_map/ppermute | solution.py:87
  12.0 3.5 %collective-permute-start.6 = (f32[16,128]{1,0:T(8,128)S(1)}, f32[16,128]{1,0:T(8,128)S(1)}, u32[]{:S(2)}, u32[]{:S(2)}) collective-permute-start(f32[16,128]{1,0:T(8,128)S(1)} %get-tuple-element.95), channel_id=1, source_target_pairs={{0,240},{1,241},{2,242},{3,243},{4,244},{5,245},{6,246},{7,247},{8... | collective-permute-start | bytes 24584 | tf_op jit(solution)/shard_map/ppermute | solution.py:87
  14.1 1.4 %collective-permute-start.7 = (f32[16,128]{1,0:T(8,128)S(1)}, f32[16,128]{1,0:T(8,128)S(1)}, u32[]{:S(2)}, u32[]{:S(2)}) collective-permute-start(f32[16,128]{1,0:T(8,128)S(1)} %get-tuple-element.96), channel_id=1, source_target_pairs={{0,16},{1,17},{2,18},{3,19},{4,20},{5,21},{6,22},{7,23},{8,24},{9,... | collective-permute-start | bytes 24584 | tf_op jit(solution)/shard_map/ppermute | solution.py:87

commit v9 on v8

--- a/solution.py
+++ b/solution.py
@@ -548,7 +548,9 @@
     beyond = rims_of(route, None, [came[link][8:16, :] for link in range(4)])
     lines, inner = four_of(lines_ref), four_of(inner_ref)
     patch = edge_patches(lines, rims)
-    whole = with_ends(patch)
+    kept = [jnp.where(lane < TILE, one, 0.0) for one in patch]
+    across = [pressure_at(kept[side], 4 if side % 2 == 1 else 6, row) for side in range(4)]
+    crossing = ((3, 1, 0), (0, 2, TILE - 1), (3, 1, TILE - 1), (0, 2, 0))
     on_edge, inside = [], []
     for side in range(4):
         sign = 1.0 if side in (1, 2) else -1.0
@@ -560,17 +562,18 @@
         along = normal * (sign * (beyond[side] - lines[side])) + tangent * (after - before)
         round_sum = after + before + beyond[side] + lines[side] - 4.0 * line
         tracer = wet_rows(line) * (line - (0.5 * ADVECT) * along + DIFFUSE * round_sum)
-        mine = jnp.where(lane < TILE, whole[side], 0.0)
         to_normal, to_tangent = (4, 6) if side % 2 == 1 else (6, 4)
         own_row = row < 2 if side % 2 == 1 else (row >= 2) & (row < 4)
         cross_row = (row >= 2) & (row < 4) if side % 2 == 1 else row < 2
-        cross = pressure_at(mine, to_tangent, row)
+        cross = pressure_at(kept[side], to_tangent, row)
+        start, stop, lane_there = crossing[side]
         drop = pltpu.roll(cross, LANES - 1, 1) - pltpu.roll(cross, 1, 1)
+        drop = drop + at_ends(across[stop], lane_there, TILE - 2) - at_ends(across[start], lane_there, 1)
         push = jnp.where(own_row, sign * pressure_at(tracer, to_normal, row), 0.0)
         push = jnp.where(cross_row, drop, push)
         on_edge.append(patch[side] - (0.5 * STEP_SIZE) * wet * push)
-        kept = own_row & (lane > 0) & (lane < TILE - 1)
-        inside.append(jnp.where(kept, (-sign * 0.5 * STEP_SIZE) * wet_in * pressure_at(mine, to_normal, row), 0.0))
+        between = own_row & (lane > 0) & (lane < TILE - 1)
+        inside.append(jnp.where(between, (-sign * 0.5 * STEP_SIZE) * wet_in * across[side], 0.0))
     edges, seconds = spread_chunks(on_edge, 0), spread_chunks(inside, 1)
     copies = []
     for low, high in ((0, 24), (24, CHUNKS)):

time: 16.7 us -> 16.6 us (level)
  no operation moved by 1% of the time
where the time goes in v9:
time: 16.6 us; the launch traced here: 16.5 us
  starting transfers between devices  10.5 us (63%)
  Pallas kernels  4.02 us (24%)
  waiting for transfers between devices  1.23 us (7%)
  between operations  0.68 us (4%)
    ppermute x4, starting transfers between devices, exchanged(): lax.ppermute(pay, AXES, pairs_of(LINKS[link], nx, ny))  10.5 us
    pallas_call x1, Pallas kernels, on_device(): pl.pallas_call(lambda *refs: inner_kernel((nx, ny), *refs), out_shape=[wi...  1.72 us
    pallas_call x1, Pallas kernels, on_device(): pl.pallas_call(lambda *refs: load_kernel((nx, ny), *refs), out_shape=[sds...  1.25 us
    ppermute x4, waiting for transfers between devices, exchanged(): lax.ppermute(pay, AXES, pairs_of(LINKS[link], nx, ny))  1.23 us
    pallas_call x1, Pallas kernels, grid_like(): pl.pallas_call(final_kernel, out_shape=result, in_specs=[VMEM] * 9, out_s...  0.98 us
  transfers between devices with their start and end apart: 4, of which 3 were waited for; matrix products, arithmetic and copies ran while one was open for 0% of the time, Pallas kernels for 10%

profile of v9, /device:TPU:1, one launch (start us, length us, event | category | flops | bytes accessed | tf_op | source)
XLA Modules:
  0.0 16.5 jit_solution(2505357052725001722)
XLA Ops:
  0.0 1.2 %load.1 = (f32[8,8100]{1,0:T(8,128)S(1)}, s32[8,8100]{1,0:T(8,128)S(1)}, f32[32,128]{1,0:T(8,128)S(1)}, f32[32,128]{1,0:T(8,128)S(1)}, f32[16,128]{1,0:T(8,128)S...) custom-call(s32[256]{0:T(256)} %refs_0_.3, ...), custom_call_target="tpu_custom_call" | custom-call | tf_op jit(solution)/shard_map/load/pallas_call | solution.py:660
  1.3 7.8 %collective-permute-start.4 = (f32[16,128]{1,0:T(8,128)S(1)}, f32[16,128]{1,0:T(8,128)S(1)}, u32[]{:S(2)}, u32[]{:S(2)}) collective-permute-start(f32[16,128]{1,0:T(8,128)S(1)} %get-tuple-element.91), channel_id=1, source_target_pairs={{0,1},{1,0},{2,3},{3,2},{4,5},{5,4},{6,7},{7,6},{8,9},{9,8},{10,11... | collective-permute-start | bytes 24584 | tf_op jit(solution)/shard_map/ppermute | solution.py:87
  9.1 0.0 collective-permute-start.5
  9.1 1.7 %inner.1 = (f32[8,8192]{1,0:T(8,128)S(1)}, s32[16,128]{1,0:T(8,128)S(1)}, s32[1]{0:T(128)}) custom-call(s32[256]{0:T(256)} %refs_0_.3, s32[4,256]{1,0:T(4,128)} %bitcast.11, s32[4,256]{1,0:T(4,128)} %bitcast.13, s32[2,128]{1,0:T(2,128)} %bitcast.14, f32[8,8100]{1,0:T(8,128)S(1)} %get-tuple-element.83.refs_4_, s32[8,8100]{1,0:T(8,128)S(1)} %get-tuple-element.84.refs_5_, ...), custom_call_target="tpu_custom_call" | custom-call | flops 2000000 | bytes 800000 | tf_op jit(solution)/shard_map/inner/pallas_call | solution.py:670
  10.8 0.0 collective-permute-done.4.came0
  10.8 1.1 %collective-permute-done.5.came1 = f32[16,128]{1,0:T(8,128)S(1)} collective-permute-done((f32[16,128]{1,0:T(8,128)S(1)}, f32[16,128]{1,0:T(8,128)S(1)}, u32[]{:S(2)}, u32[]{:S(2)}) %collective-permute-start.5) | collective-permute-done | bytes 8224 | tf_op jit(solution)/shard_map/ppermute | solution.py:87
  11.9 0.1 relay.1
  12.0 2.1 %collective-permute-start.6 = (f32[16,128]{1,0:T(8,128)S(1)}, f32[16,128]{1,0:T(8,128)S(1)}, u32[]{:S(2)}, u32[]{:S(2)}) collective-permute-start(f32[16,128]{1,0:T(8,128)S(1)} %get-tuple-element.95), channel_id=1, source_target_pairs={{0,240},{1,241},{2,242},{3,243},{4,244},{5,245},{6,246},{7,247},{8... | collective-permute-start | bytes 24584 | tf_op jit(solution)/shard_map/ppermute | solution.py:87
  14.1 0.6 %collective-permute-start.7 = (f32[16,128]{1,0:T(8,128)S(1)}, f32[16,128]{1,0:T(8,128)S(1)}, u32[]{:S(2)}, u32[]{:S(2)}) collective-permute-start(f32[16,128]{1,0:T(8,128)S(1)} %get-tuple-element.96), channel_id=1, source_target_pairs={{0,16},{1,17},{2,18},{3,19},{4,20},{5,21},{6,22},{7,23},{8,24},{9,... | collective-permute-start | bytes 24584 | tf_op jit(solution)/shard_map/ppermute | solution.py:87
  15.3 0.1 collective-permute-done.6
  15.4 0.1 collective-permute-done.7
  15.5 1.0 %conditional.1 = (f32[1,6,8100]{2,0,1:T(1,128)}) conditional(s32[]{:T(128)} %bitcast.6, (s32[48,128]{1,0:T(8,128)S(1)}, s32[16,128]{1,0:T(8,128)S(1)}, f32[32,128]{1,0:T(8,128)S(1)}, f32[32,128]{1,0:T(8,128)S(1)}, f32[8,8192]{1,0:T(8,128)S(1)}, /*index=5*/f32[16,128]{1,0:T(8,128)S(1)}, f32[16,128]{1,0:T(8,128)S(1)}, f32[16,128]{1,0:T(8,128)S(1)}, ...), branch_computations={%region_0.0_spmd, %region_1.0_spmd} | conditional | flops 4000000 | bytes 1665704 | solution.py:717
  15.5 1.0 %final.1 = f32[6,1,8100]{2,1,0:T(1,128)} custom-call(s32[48,128]{1,0:T(8,128)S(1)} %get-tuple-element.43.route_ref, s32[16,128]{1,0:T(8,128)S(1)} %get-tuple-element.44.plan_ref, f32[32,128]{1,0:T(8,128)S(1)} %get-tuple-element.45.lines_ref, f32[32,128]{1,0:T(8,128)S(1)} %get-tuple-element.46.inner_ref, f32[8,8192]{1,0:T(8,128)S(1)} %get-tuple-element.47.almost_ref, ...), custom_call_target="tpu_custom_call" | custom-call | tf_op jit(solution)/shard_map/cond/branch_0_fun/final/pallas_call | solution.py:689
Async XLA Ops:
  1.3 9.6 %collective-permute-start.4 = (f32[16,128]{1,0:T(8,128)S(1)}, f32[16,128]{1,0:T(8,128)S(1)}, u32[]{:S(2)}, u32[]{:S(2)}) collective-permute-start(f32[16,128]{1,0:T(8,128)S(1)} %get-tuple-element.91), channel_id=1, source_target_pairs={{0,1},{1,0},{2,3},{3,2},{4,5},{5,4},{6,7},{7,6},{8,9},{9,8},{10,11... | collective-permute-start | bytes 24584 | tf_op jit(solution)/shard_map/ppermute | solution.py:87
  9.1 2.8 %collective-permute-start.5 = (f32[16,128]{1,0:T(8,128)S(1)}, f32[16,128]{1,0:T(8,128)S(1)}, u32[]{:S(2)}, u32[]{:S(2)}) collective-permute-start(f32[16,128]{1,0:T(8,128)S(1)} %get-tuple-element.92), channel_id=1, source_target_pairs={{0,128},{1,2},{2,1},{3,4},{4,3},{5,6},{6,5},{7,8},{8,7},{9,10},{10... | collective-permute-start | bytes 24584 | tf_op jit(solution)/shard_map/ppermute | solution.py:87
  12.0 3.5 %collective-permute-start.6 = (f32[16,128]{1,0:T(8,128)S(1)}, f32[16,128]{1,0:T(8,128)S(1)}, u32[]{:S(2)}, u32[]{:S(2)}) collective-permute-start(f32[16,128]{1,0:T(8,128)S(1)} %get-tuple-element.95), channel_id=1, source_target_pairs={{0,240},{1,241},{2,242},{3,243},{4,244},{5,245},{6,246},{7,247},{8... | collective-permute-start | bytes 24584 | tf_op jit(solution)/shard_map/ppermute | solution.py:87
  14.1 1.4 %collective-permute-start.7 = (f32[16,128]{1,0:T(8,128)S(1)}, f32[16,128]{1,0:T(8,128)S(1)}, u32[]{:S(2)}, u32[]{:S(2)}) collective-permute-start(f32[16,128]{1,0:T(8,128)S(1)} %get-tuple-element.96), channel_id=1, source_target_pairs={{0,16},{1,17},{2,18},{3,19},{4,20},{5,21},{6,22},{7,23},{8,24},{9,... | collective-permute-start | bytes 24584 | tf_op jit(solution)/shard_map/ppermute | solution.py:87

commit v10 on v9

--- a/solution.py
+++ b/solution.py
@@ -576,7 +576,7 @@
         inside.append(jnp.where(between, (-sign * 0.5 * STEP_SIZE) * wet_in * across[side], 0.0))
     edges, seconds = spread_chunks(on_edge, 0), spread_chunks(inside, 1)
     copies = []
-    for low, high in ((0, 24), (24, CHUNKS)):
+    for low, high in ((0, 48), (48, CHUNKS)):
         for c in range(low, high):
             cut = slice(c * LANES, min((c + 1) * LANES, CELLS))
             width = cut.stop - cut.start

time: 16.6 us -> 16.6 us (level)
  no operation moved by 1% of the time
where the time goes in v10:
time: 16.6 us; the launch traced here: 16.5 us
  starting transfers between devices  10.5 us (63%)
  Pallas kernels  4.04 us (24%)
  waiting for transfers between devices  1.23 us (7%)
  between operations  0.68 us (4%)
    ppermute x4, starting transfers between devices, exchanged(): lax.ppermute(pay, AXES, pairs_of(LINKS[link], nx, ny))  10.5 us
    pallas_call x1, Pallas kernels, on_device(): pl.pallas_call(lambda *refs: inner_kernel((nx, ny), *refs), out_shape=[wi...  1.72 us
    pallas_call x1, Pallas kernels, on_device(): pl.pallas_call(lambda *refs: load_kernel((nx, ny), *refs), out_shape=[sds...  1.25 us
    ppermute x4, waiting for transfers between devices, exchanged(): lax.ppermute(pay, AXES, pairs_of(LINKS[link], nx, ny))  1.23 us
    pallas_call x1, Pallas kernels, grid_like(): pl.pallas_call(final_kernel, out_shape=result, in_specs=[VMEM] * 9, out_s...  1 us
  transfers between devices with their start and end apart: 4, of which 3 were waited for; matrix products, arithmetic and copies ran while one was open for 0% of the time, Pallas kernels for 10%

profile of v10, /device:TPU:1, one launch (start us, length us, event | category | flops | bytes accessed | tf_op | source)
XLA Modules:
  0.0 16.5 jit_solution(16242499888015855739)
XLA Ops:
  0.0 1.2 %load.1 = (f32[8,8100]{1,0:T(8,128)S(1)}, s32[8,8100]{1,0:T(8,128)S(1)}, f32[32,128]{1,0:T(8,128)S(1)}, f32[32,128]{1,0:T(8,128)S(1)}, f32[16,128]{1,0:T(8,128)S...) custom-call(s32[256]{0:T(256)} %refs_0_.3, ...), custom_call_target="tpu_custom_call" | custom-call | tf_op jit(solution)/shard_map/load/pallas_call | solution.py:660
  1.3 7.8 %collective-permute-start.4 = (f32[16,128]{1,0:T(8,128)S(1)}, f32[16,128]{1,0:T(8,128)S(1)}, u32[]{:S(2)}, u32[]{:S(2)}) collective-permute-start(f32[16,128]{1,0:T(8,128)S(1)} %get-tuple-element.91), channel_id=1, source_target_pairs={{0,1},{1,0},{2,3},{3,2},{4,5},{5,4},{6,7},{7,6},{8,9},{9,8},{10,11... | collective-permute-start | bytes 24584 | tf_op jit(solution)/shard_map/ppermute | solution.py:87
  9.1 0.0 collective-permute-start.5
  9.1 1.7 %inner.1 = (f32[8,8192]{1,0:T(8,128)S(1)}, s32[16,128]{1,0:T(8,128)S(1)}, s32[1]{0:T(128)}) custom-call(s32[256]{0:T(256)} %refs_0_.3, s32[4,256]{1,0:T(4,128)} %bitcast.11, s32[4,256]{1,0:T(4,128)} %bitcast.13, s32[2,128]{1,0:T(2,128)} %bitcast.14, f32[8,8100]{1,0:T(8,128)S(1)} %get-tuple-element.83.refs_4_, s32[8,8100]{1,0:T(8,128)S(1)} %get-tuple-element.84.refs_5_, ...), custom_call_target="tpu_custom_call" | custom-call | flops 2000000 | bytes 800000 | tf_op jit(solution)/shard_map/inner/pallas_call | solution.py:670
  10.8 0.0 collective-permute-done.4.came0
  10.8 1.1 %collective-permute-done.5.came1 = f32[16,128]{1,0:T(8,128)S(1)} collective-permute-done((f32[16,128]{1,0:T(8,128)S(1)}, f32[16,128]{1,0:T(8,128)S(1)}, u32[]{:S(2)}, u32[]{:S(2)}) %collective-permute-start.5) | collective-permute-done | bytes 8224 | tf_op jit(solution)/shard_map/ppermute | solution.py:87
  11.9 0.1 relay.1
  12.0 2.1 %collective-permute-start.6 = (f32[16,128]{1,0:T(8,128)S(1)}, f32[16,128]{1,0:T(8,128)S(1)}, u32[]{:S(2)}, u32[]{:S(2)}) collective-permute-start(f32[16,128]{1,0:T(8,128)S(1)} %get-tuple-element.95), channel_id=1, source_target_pairs={{0,240},{1,241},{2,242},{3,243},{4,244},{5,245},{6,246},{7,247},{8... | collective-permute-start | bytes 24584 | tf_op jit(solution)/shard_map/ppermute | solution.py:87
  14.1 0.6 %collective-permute-start.7 = (f32[16,128]{1,0:T(8,128)S(1)}, f32[16,128]{1,0:T(8,128)S(1)}, u32[]{:S(2)}, u32[]{:S(2)}) collective-permute-start(f32[16,128]{1,0:T(8,128)S(1)} %get-tuple-element.96), channel_id=1, source_target_pairs={{0,16},{1,17},{2,18},{3,19},{4,20},{5,21},{6,22},{7,23},{8,24},{9,... | collective-permute-start | bytes 24584 | tf_op jit(solution)/shard_map/ppermute | solution.py:87
  15.3 0.1 collective-permute-done.6
  15.4 0.1 collective-permute-done.7
  15.5 1.0 %conditional.1 = (f32[1,6,8100]{2,0,1:T(1,128)}) conditional(s32[]{:T(128)} %bitcast.6, (s32[48,128]{1,0:T(8,128)S(1)}, s32[16,128]{1,0:T(8,128)S(1)}, f32[32,128]{1,0:T(8,128)S(1)}, f32[32,128]{1,0:T(8,128)S(1)}, f32[8,8192]{1,0:T(8,128)S(1)}, /*index=5*/f32[16,128]{1,0:T(8,128)S(1)}, f32[16,128]{1,0:T(8,128)S(1)}, f32[16,128]{1,0:T(8,128)S(1)}, ...), branch_computations={%region_0.0_spmd, %region_1.0_spmd} | conditional | flops 4000000 | bytes 1665704 | solution.py:717
  15.5 1.0 %final.1 = f32[6,1,8100]{2,1,0:T(1,128)} custom-call(s32[48,128]{1,0:T(8,128)S(1)} %get-tuple-element.43.route_ref, s32[16,128]{1,0:T(8,128)S(1)} %get-tuple-element.44.plan_ref, f32[32,128]{1,0:T(8,128)S(1)} %get-tuple-element.45.lines_ref, f32[32,128]{1,0:T(8,128)S(1)} %get-tuple-element.46.inner_ref, f32[8,8192]{1,0:T(8,128)S(1)} %get-tuple-element.47.almost_ref, ...), custom_call_target="tpu_custom_call" | custom-call | tf_op jit(solution)/shard_map/cond/branch_0_fun/final/pallas_call | solution.py:689
Async XLA Ops:
  1.3 9.6 %collective-permute-start.4 = (f32[16,128]{1,0:T(8,128)S(1)}, f32[16,128]{1,0:T(8,128)S(1)}, u32[]{:S(2)}, u32[]{:S(2)}) collective-permute-start(f32[16,128]{1,0:T(8,128)S(1)} %get-tuple-element.91), channel_id=1, source_target_pairs={{0,1},{1,0},{2,3},{3,2},{4,5},{5,4},{6,7},{7,6},{8,9},{9,8},{10,11... | collective-permute-start | bytes 24584 | tf_op jit(solution)/shard_map/ppermute | solution.py:87
  9.1 2.8 %collective-permute-start.5 = (f32[16,128]{1,0:T(8,128)S(1)}, f32[16,128]{1,0:T(8,128)S(1)}, u32[]{:S(2)}, u32[]{:S(2)}) collective-permute-start(f32[16,128]{1,0:T(8,128)S(1)} %get-tuple-element.92), channel_id=1, source_target_pairs={{0,128},{1,2},{2,1},{3,4},{4,3},{5,6},{6,5},{7,8},{8,7},{9,10},{10... | collective-permute-start | bytes 24584 | tf_op jit(solution)/shard_map/ppermute | solution.py:87
  12.0 3.5 %collective-permute-start.6 = (f32[16,128]{1,0:T(8,128)S(1)}, f32[16,128]{1,0:T(8,128)S(1)}, u32[]{:S(2)}, u32[]{:S(2)}) collective-permute-start(f32[16,128]{1,0:T(8,128)S(1)} %get-tuple-element.95), channel_id=1, source_target_pairs={{0,240},{1,241},{2,242},{3,243},{4,244},{5,245},{6,246},{7,247},{8... | collective-permute-start | bytes 24584 | tf_op jit(solution)/shard_map/ppermute | solution.py:87
  14.1 1.4 %collective-permute-start.7 = (f32[16,128]{1,0:T(8,128)S(1)}, f32[16,128]{1,0:T(8,128)S(1)}, u32[]{:S(2)}, u32[]{:S(2)}) collective-permute-start(f32[16,128]{1,0:T(8,128)S(1)} %get-tuple-element.96), channel_id=1, source_target_pairs={{0,16},{1,17},{2,18},{3,19},{4,20},{5,21},{6,22},{7,23},{8,24},{9,... | collective-permute-start | bytes 24584 | tf_op jit(solution)/shard_map/ppermute | solution.py:87
